TPU v7x, 32 devices: a whole 2x2x4 slice. The times are simulated.
32 devices in a mesh: clips: 2 (over y), frame: 4 (over z), head: 2 (over x), seq: 2 (over core).
Axes of the slice: x: 2, y: 2, z: 4, core: 2. Of those that a mesh axis runs over, the one named last changes fastest.
Arguments:
- queries: bfloat16 [32, 1024, 1536], P(('clips', 'frame'), 'seq', 'head'), parts along dimension 0, may hold values from -150 to 150, as said below
- key_rows: bfloat16 [32, 1024, 1536], P(('clips', 'frame'), 'seq', 'head'), parts along dimension 0, may hold values from -5 to 5, as said below
- value_rows: bfloat16 [32, 1024, 1536], P(('clips', 'frame'), 'seq', 'head'), parts along dimension 0, may hold values from -6 to 6
- list_one: int32 [32, 2, 4], P('clips'), parts along dimension 0, may hold values from 0 to 7, as said below
- list_two: int32 [32, 2, 2], P('clips'), parts along dimension 0, may hold values from 0 to 7, as said below
- list_four: int32 [32, 2, 1], P('clips'), parts along dimension 0, may hold values from 0 to 7, as said below
- tile_counts: int32 [32, 2, 3], P('clips'), parts along dimension 0, may hold values from 0 to 4, as said below
Outputs:
- attended: bfloat16 [32, 1024, 1536], P(('clips', 'frame'), 'seq', 'head'), parts along dimension 0
There are 2 independent parts, one for each index of `clips`. A program takes and returns all parts, laid end to end along the dimension named above; each array names one. Nothing has to cross between parts.
Inputs may be any that keep to these rules, and one draw needn't show every extreme that they name: Real-valued queries; a few query rows of a frame may be far larger in magnitude than the others. `key_rows`: Real-valued keys of order one. The entries of list_one[f, e, :] are distinct tile numbers of the frame f - 1 (e = 0) or f + 1 (e = 1). The entries of list_two[f, e, :] are distinct tile numbers of the frame f - 2 (e = 0) or f + 2 (e = 1). The entries of list_four[f, e, :] are distinct tile numbers of the frame f - 4 (e = 0) or f + 4 (e = 1). tile_counts[f, e, j] counts the live leading entries of the list of distance 1, 2, 4 (j = 0, 1, 2) for frame f and direction e; it is 0 exactly where the source frame lies outside the clip, else at least 1 and at most that list's length; frame 0's lists toward later frames are full.
All inputs are finite; a program needn't handle non-finite values.
Results may differ from a plain program's by a relative error of at most 0.0032.
Values may be sent and summed in bfloat16 or wider, within the bound.
No kernel may reach another device: no remote copies, remote signals or barrier semaphores. Data moves between devices by JAX's collectives and lax.ppermute only.
A program may use at most 128 MiB of HBM per device.

v0:
```python
import jax
import jax.numpy as jnp
from jax import lax
from jax.sharding import PartitionSpec as P

HEAD_DIM = 128
TILE_TOKENS = 128


def passed_along(block, axis, distance):
    devices = range(lax.axis_size(axis))
    route = [(i - distance, i) for i in devices if i - distance in devices]
    return lax.ppermute(block, axis, route)


def select_tiles(tile_array, sources, chosen):
    return tile_array[sources[:, None], chosen]


def to_tiles(rows):
    return rows.reshape(rows.shape[0], rows.shape[1] // TILE_TOKENS, TILE_TOKENS, rows.shape[2])


def pack_lists(tile_array, own_frames, local_index, reaches, frame_total):
    packed = {}
    for direction in (0, 1):
        step_sign = 2 * direction - 1
        for distance, tile_list in reaches:
            targets = jnp.clip(own_frames - step_sign * distance, 0, frame_total - 1)
            chosen = jnp.take(tile_list, targets, axis=0)[:, direction, :]
            packed[direction, distance] = select_tiles(tile_array, local_index, chosen)
    return packed


def join_lists(packed, from_later, from_earlier, frames_here):
    selected = {}
    for rank, distance in enumerate((1, 2, 4)):
        selected[1, distance] = jnp.concatenate(
            [packed[1, distance][distance:], from_later[rank]], axis=0
        )
        selected[0, distance] = jnp.concatenate(
            [from_earlier[rank], packed[0, distance][: frames_here - distance]], axis=0
        )
    return selected


def attend_frame(frame_item):
    query_block, pair_block, live_block = frame_item
    width = query_block.shape[1]
    score_scale = HEAD_DIM ** (-0.5)
    pieces = []
    for head_index in range(width // HEAD_DIM):
        column_start = head_index * HEAD_DIM
        query_head = query_block[:, column_start : column_start + HEAD_DIM]
        key_head = pair_block[:, column_start : column_start + HEAD_DIM]
        value_head = pair_block[:, width + column_start : width + column_start + HEAD_DIM]
        scores = (
            lax.dot_general(
                query_head, key_head, (((1,), (1,)), ((), ())), preferred_element_type=jnp.float32
            )
            * score_scale
        )
        scores = jnp.where(live_block[None, :] > 0, scores, -jnp.inf)
        row_max = jnp.max(scores, axis=1, keepdims=True)
        exponent = jnp.exp(scores - row_max)
        row_total = jnp.sum(exponent, axis=1, keepdims=True)
        rounded = exponent.astype(jnp.bfloat16)
        mixed_head = jnp.dot(rounded, value_head, preferred_element_type=jnp.float32) / row_total
        pieces.append(mixed_head)
    return jnp.concatenate(pieces, axis=1).astype(jnp.bfloat16)


def per_device(queries, key_rows, value_rows, list_one, list_two, list_four, tile_counts):
    frames_here = queries.shape[0]
    paired = jnp.concatenate([key_rows, value_rows], axis=2)
    channels = paired.shape[2]
    first_frame = lax.axis_index("frame") * frames_here
    local_index = jnp.arange(frames_here, dtype=jnp.int32)
    frame_total = list_one.shape[0]
    own_frames = first_frame + local_index
    own_counts = jnp.take(tile_counts, own_frames, axis=0)
    reaches = ((1, list_one), (2, list_two), (4, list_four))
    whole_frames = lax.all_gather(paired, "seq", axis=1, tiled=True)
    packed = pack_lists(to_tiles(whole_frames), own_frames, local_index, reaches, frame_total)
    from_later = passed_along((packed[1, 1][:1], packed[1, 2][:2], packed[1, 4]), "frame", -1)
    from_earlier = passed_along(
        (packed[0, 1][frames_here - 1 :], packed[0, 2][frames_here - 2 :], packed[0, 4]), "frame", 1
    )
    selected = join_lists(packed, from_later, from_earlier, frames_here)
    frame_length = whole_frames.shape[1]
    key_parts = [whole_frames]
    live_parts = [jnp.ones((frames_here, frame_length), jnp.int32)]
    for direction in (0, 1):
        for slot_index, (distance, tile_list) in enumerate(reaches):
            tile_group = selected[direction, distance]
            length = tile_group.shape[1]
            key_parts.append(tile_group.reshape(frames_here, length * TILE_TOKENS, channels))
            slot_rank = jnp.arange(length * TILE_TOKENS, dtype=jnp.int32) // TILE_TOKENS
            live_parts.append(
                (slot_rank[None, :] < own_counts[:, direction, slot_index][:, None]).astype(
                    jnp.int32
                )
            )
    key_set = jnp.concatenate(key_parts, axis=1)
    live_slots = jnp.concatenate(live_parts, axis=1)
    return lax.map(attend_frame, (queries, key_set, live_slots))


def solution(mesh):
    placed = (
        P(("clips", "frame"), "seq", "head"),
        P(("clips", "frame"), "seq", "head"),
        P(("clips", "frame"), "seq", "head"),
        P("clips", None, None),
        P("clips", None, None),
        P("clips", None, None),
        P("clips", None, None),
    )
    return jax.shard_map(
        per_device,
        mesh=mesh,
        in_specs=placed,
        out_specs=P(("clips", "frame"), "seq", "head"),
        check_vma=False,
    )
```

profile of v0, /device:TPU:19, one launch (start us, length us, event | category | flops | bytes accessed | tf_op | source)
XLA Modules:
  0.0 470.2 jit_solution(3644444854377102763)
XLA Ops:
  6.5 6.0 %pad_maximum_fusion = bf16[4,512,1536]{2,1,0:T(8,128)(2,1)} fusion(bf16[4,512,768]{2,1,0:T(8,128)(2,1)} %param.17, bf16[4,512,768]{2,1,0:T(8,128)(2,1)} %param.16), kind=kLoop, calls=%fused_computation.119 | loop fusion | flops 12582912 | bytes 12582912 | tf_op jit(solution)/shard_map/concatenate | solution.py:75
  20.2 18.7 %all-gather.2.cloned.1.call-done = bf16[4,1024,1536]{2,1,0:T(8,128)(2,1)} async-done(((bf16[4,512,1536]{2,1,0:T(8,128)(2,1)}), bf16[4,1024,1536]{2,1,0:T(8,128)(2,1)}) %all-gather.2.cloned.1.call-update) | async-done | bytes 12582928 | tf_op jit(solution)/shard_map/all_gather | solution.py:83
  38.9 8.2 %gather_fusion.1 = bf16[16,128,1536]{2,1,0:T(8,128)(2,1)} fusion(bf16[4,8,128,1536]{3,2,1,0:T(8,128)(2,1)} %bitcast.97, s32[16]{0:T(128)S(1)} %reshape.429), kind=kCustom, calls=%fused_computation.7 | custom fusion | bytes 12583040 | tf_op jit(solution)/shard_map/gather | solution.py:17
  54.5 8.1 %gather_fusion.4 = bf16[16,128,1536]{2,1,0:T(8,128)(2,1)} fusion(bf16[4,8,128,1536]{3,2,1,0:T(8,128)(2,1)} %bitcast.98, s32[16]{0:T(128)S(1)} %reshape.449), kind=kCustom, calls=%fused_computation.10 | custom fusion | bytes 12583040 | tf_op jit(solution)/shard_map/gather | solution.py:17
  69.8 5.3 %gather_fusion.2 = bf16[8,128,1536]{2,1,0:T(8,128)(2,1)S(1)} fusion(bf16[4,8,128,1536]{3,2,1,0:T(8,128)(2,1)} %bitcast.99, s32[8]{0:T(128)S(1)} %reshape.435), kind=kCustom, calls=%fused_computation.8 | custom fusion | bytes 6291520 | tf_op jit(solution)/shard_map/gather | solution.py:17
  79.0 6.4 %gather_fusion.3 = bf16[4,128,1536]{2,1,0:T(8,128)(2,1)} fusion(bf16[4,8,128,1536]{3,2,1,0:T(8,128)(2,1)} %bitcast.100, s32[4]{0:T(128)S(1)} %or_bitcast_fusion.1), kind=kCustom, calls=%fused_computation.9 | custom fusion | bytes 3145760 | tf_op jit(solution)/shard_map/gather | solution.py:17
  90.7 5.3 %gather_fusion.5 = bf16[8,128,1536]{2,1,0:T(8,128)(2,1)S(1)} fusion(bf16[4,8,128,1536]{3,2,1,0:T(8,128)(2,1)} %bitcast.101, s32[8]{0:T(128)S(1)} %reshape.455), kind=kCustom, calls=%fused_computation.11 | custom fusion | bytes 6291520 | tf_op jit(solution)/shard_map/gather | solution.py:17
  102.6 10.5 %constant_dynamic-update-slice_fusion.12 = bf16[4,2816,1536]{2,1,0:T(8,128)(2,1)} fusion(bf16[4,1024,1536]{2,1,0:T(8,128)(2,1)} %all-gather.2.cloned.1.call-done), kind=kLoop, calls=%fused_computation.139 | loop fusion | bytes 25165824
  113.1 5.2 %gather_fusion.6 = bf16[4,128,1536]{2,1,0:T(8,128)(2,1)S(1)} fusion(bf16[4,8,128,1536]{3,2,1,0:T(8,128)(2,1)} %bitcast.102, s32[4]{0:T(128)S(1)} %or_bitcast_fusion), kind=kCustom, calls=%fused_computation.12 | custom fusion | bytes 3145760 | tf_op jit(solution)/shard_map/gather | solution.py:17
  123.8 14.5 %collective-permute-done.1 = bf16[2,2,128,1536]{3,2,1,0:T(8,128)(2,1)} collective-permute-done((bf16[2,2,128,1536]{3,2,1,0:T(8,128)(2,1)}, bf16[2,2,128,1536]{3,2,1,0:T(8,128)(2,1)}, u32[]{:S(2)}, u32[]{:S(2)}) %collective-permute-start.1) | collective-permute-done | bytes 1572896 | tf_op jit(solution)/shard_map/ppermute | solution.py:13
  148.6 10.1 %collective-permute-done.4 = bf16[2,2,128,1536]{3,2,1,0:T(8,128)(2,1)S(1)} collective-permute-done((bf16[2,2,128,1536]{3,2,1,0:T(8,128)(2,1)}, bf16[2,2,128,1536]{3,2,1,0:T(8,128)(2,1)S(1)}, u32[]{:S(2)}, u32[]{:S(2)}) %collective-permute-start.4) | collective-permute-done | bytes 1572896 | tf_op jit(solution)/shard_map/ppermute | solution.py:13
  158.9 13.0 %collective-permute-done.2 = bf16[4,1,128,1536]{3,2,0,1:T(8,128)(2,1)} collective-permute-done((bf16[4,1,128,1536]{3,2,0,1:T(8,128)(2,1)}, bf16[4,1,128,1536]{3,2,0,1:T(8,128)(2,1)}, u32[]{:S(2)}, u32[]{:S(2)}) %collective-permute-start.2) | collective-permute-done | bytes 1572896 | tf_op jit(solution)/shard_map/ppermute | solution.py:13
  179.6 12.7 %collective-permute-done.5 = bf16[4,1,128,1536]{3,2,0,1:T(8,128)(2,1)S(1)} collective-permute-done((bf16[4,1,128,1536]{3,2,0,1:T(8,128)(2,1)S(1)}, bf16[4,1,128,1536]{3,2,0,1:T(8,128)(2,1)S(1)}, u32[]{:S(2)}, u32[]{:S(2)}) %collective-permute-start.5) | collective-permute-done | bytes 1572896 | tf_op jit(solution)/shard_map/ppermute | solution.py:13
  193.5 269.8 %while.10 = (s32[]{:T(128)}, bf16[4,512,768]{2,1,0:T(8,128)(2,1)}, s32[4,2816]{1,0:T(4,128)S(1)}, bf16[4,512,768]{2,1,0:T(8,128)(2,1)}, bf16[4,2816,1536]{2,1,0:T(8,128)(2,1)}, /*index=5*/s32[]{:T(128)}) while((s32[]{:T(128)}, bf16[4,512,768]{2,1,0:T(8,128)(2,1)}, s32[4,2816]{1,0:T(4,128)S(1)}, bf16[4,512,768]{2,1,0:T(8,128)(2,1)}, ...), condition=%wide.region_13.17_spmd, body=%wide.region_0.16_spmd.sunk | while | flops 4525126656 | bytes 196972000 | solution.py:106
  193.5 7.4 %dynamic-slice_bitcast_fusion.4 = bf16[2816,1536]{1,0:T(8,128)(2,1)} fusion(bf16[4,2816,1536]{2,1,0:T(8,128)(2,1)} %get-tuple-element.159, s32[]{:T(128)} %get-tuple-element.149), kind=kLoop, calls=%fused_computation.13.clone.1 | loop fusion | bytes 17301508 | tf_op jit(solution)/shard_map/while/body/jit(dynamic_index_in_dim)/squeeze | solution.py:106
  204.5 5.3 %fusion.216 = (f32[512]{0:T(512)S(1)}, f32[512]{0:T(512)S(1)}, f32[512,2816]{1,0:T(8,128)}) fusion(pred[2816]{0:T(1024)(128)(4,1)S(1)} %compare_reduce_fusion.2, f32[512,2816]{1,0:T(8,128)S(1)} %fusion.215, bf16[2816,1536]{1,0:T(8,128)(2,1)} %dynamic-slice_bitcast_fusion.4, bf16[512,768]{1,0:T(8,128)(2,1)S(1)} %dynamic-slice_bitcast_fusion.5), kind=kOutput, calls=%fused_computation.31.clone.1 | convolution fusion | flops 377748480 | bytes 12393472 | tf_op jit(solution)/shard_map/while/body/eval_jaxpr/dot_general | solution.py:58
  218.4 10.9 %fusion.220 = (f32[512]{0:T(512)S(1)}, f32[512]{0:T(512)S(1)}, f32[512]{0:T(512)S(1)}, f32[512]{0:T(512)S(1)}, f32[512]{0:T(512)S(1)}, /*index=5*/f32[512]{0:T(512)S(1)}, f32[512,2816]{1,0:T(8,128)}) fusion(f32[512,2816]{1,0:T(8,128)} %get-tuple-element.130, f32[512]{0:T(512)S(1)} %get-tuple-element.131, ...), kind=kOutput, calls=%fused_computation.42.clone.1 | convolution fusion | flops 397931520 | bytes 35474176 | tf_op jit(solution)/shard_map/while/body/eval_jaxpr/dot_general | solution.py:58
  229.3 8.0 %fusion.222 = (f32[512]{0:T(512)S(1)}, f32[512]{0:T(512)S(1)}, f32[512]{0:T(512)S(1)}, f32[512]{0:T(512)S(1)}) fusion(f32[512,2816]{1,0:T(8,128)S(1)} %fusion.219, f32[512]{0:T(512)S(1)} %get-tuple-element.135, pred[2816]{0:T(1024)(128)(4,1)S(1)} %compare_reduce_fusion.2, f32[512]{0:T(512)S(1)} %get-tuple-element.134, ...), kind=kLoop, calls=%fused_computation.40.clone.1 | loop fusion | flops 23066624 | bytes 23087872 | tf_op jit(solution)/shard_map/while/body/eval_jaxpr/reduce_sum | solution.py:66
  243.8 4.9 %fusion.224 = bf16[1,512,768]{1,2,0:T(8,128)(2,1)} fusion(bf16[1,512,768]{1,2,0:T(8,128)(2,1)} %fusion.223, f32[512,2816]{1,0:T(8,128)} %fusion.217, f32[512]{0:T(512)S(1)} %get-tuple-element.136, pred[2816]{0:T(1024)(128)(4,1)S(1)} %compare_reduce_fusion.2, bf16[2816,1536]{1,0:T(8,128)(2,1)} %dynamic-slice_bitcast_fusion.4, ...), kind=kOutput, calls=%fused_computation.67.clone.1 | convolution fusion | flops 374996992 | bytes 6626048 | tf_op jit(solution)/shard_map/while/body/eval_jaxpr/dot_general | solution.py:68
  261.0 7.4 %dynamic-slice_bitcast_fusion.4 = bf16[2816,1536]{1,0:T(8,128)(2,1)} fusion(bf16[4,2816,1536]{2,1,0:T(8,128)(2,1)} %get-tuple-element.159, s32[]{:T(128)} %get-tuple-element.149), kind=kLoop, calls=%fused_computation.13.clone.1 | loop fusion | bytes 17301508 | tf_op jit(solution)/shard_map/while/body/jit(dynamic_index_in_dim)/squeeze | solution.py:106
  272.0 5.3 %fusion.216 = (f32[512]{0:T(512)S(1)}, f32[512]{0:T(512)S(1)}, f32[512,2816]{1,0:T(8,128)}) fusion(pred[2816]{0:T(1024)(128)(4,1)S(1)} %compare_reduce_fusion.2, f32[512,2816]{1,0:T(8,128)S(1)} %fusion.215, bf16[2816,1536]{1,0:T(8,128)(2,1)} %dynamic-slice_bitcast_fusion.4, bf16[512,768]{1,0:T(8,128)(2,1)S(1)} %dynamic-slice_bitcast_fusion.5), kind=kOutput, calls=%fused_computation.31.clone.1 | convolution fusion | flops 377748480 | bytes 12393472 | tf_op jit(solution)/shard_map/while/body/eval_jaxpr/dot_general | solution.py:58
  285.8 10.9 %fusion.220 = (f32[512]{0:T(512)S(1)}, f32[512]{0:T(512)S(1)}, f32[512]{0:T(512)S(1)}, f32[512]{0:T(512)S(1)}, f32[512]{0:T(512)S(1)}, /*index=5*/f32[512]{0:T(512)S(1)}, f32[512,2816]{1,0:T(8,128)}) fusion(f32[512,2816]{1,0:T(8,128)} %get-tuple-element.130, f32[512]{0:T(512)S(1)} %get-tuple-element.131, ...), kind=kOutput, calls=%fused_computation.42.clone.1 | convolution fusion | flops 397931520 | bytes 35474176 | tf_op jit(solution)/shard_map/while/body/eval_jaxpr/dot_general | solution.py:58
  296.7 8.0 %fusion.222 = (f32[512]{0:T(512)S(1)}, f32[512]{0:T(512)S(1)}, f32[512]{0:T(512)S(1)}, f32[512]{0:T(512)S(1)}) fusion(f32[512,2816]{1,0:T(8,128)S(1)} %fusion.219, f32[512]{0:T(512)S(1)} %get-tuple-element.135, pred[2816]{0:T(1024)(128)(4,1)S(1)} %compare_reduce_fusion.2, f32[512]{0:T(512)S(1)} %get-tuple-element.134, ...), kind=kLoop, calls=%fused_computation.40.clone.1 | loop fusion | flops 23066624 | bytes 23087872 | tf_op jit(solution)/shard_map/while/body/eval_jaxpr/reduce_sum | solution.py:66
  311.2 4.9 %fusion.224 = bf16[1,512,768]{1,2,0:T(8,128)(2,1)} fusion(bf16[1,512,768]{1,2,0:T(8,128)(2,1)} %fusion.223, f32[512,2816]{1,0:T(8,128)} %fusion.217, f32[512]{0:T(512)S(1)} %get-tuple-element.136, pred[2816]{0:T(1024)(128)(4,1)S(1)} %compare_reduce_fusion.2, bf16[2816,1536]{1,0:T(8,128)(2,1)} %dynamic-slice_bitcast_fusion.4, ...), kind=kOutput, calls=%fused_computation.67.clone.1 | convolution fusion | flops 374996992 | bytes 6626048 | tf_op jit(solution)/shard_map/while/body/eval_jaxpr/dot_general | solution.py:68
  328.5 7.4 %dynamic-slice_bitcast_fusion.4 = bf16[2816,1536]{1,0:T(8,128)(2,1)} fusion(bf16[4,2816,1536]{2,1,0:T(8,128)(2,1)} %get-tuple-element.159, s32[]{:T(128)} %get-tuple-element.149), kind=kLoop, calls=%fused_computation.13.clone.1 | loop fusion | bytes 17301508 | tf_op jit(solution)/shard_map/while/body/jit(dynamic_index_in_dim)/squeeze | solution.py:106
  339.4 5.3 %fusion.216 = (f32[512]{0:T(512)S(1)}, f32[512]{0:T(512)S(1)}, f32[512,2816]{1,0:T(8,128)}) fusion(pred[2816]{0:T(1024)(128)(4,1)S(1)} %compare_reduce_fusion.2, f32[512,2816]{1,0:T(8,128)S(1)} %fusion.215, bf16[2816,1536]{1,0:T(8,128)(2,1)} %dynamic-slice_bitcast_fusion.4, bf16[512,768]{1,0:T(8,128)(2,1)S(1)} %dynamic-slice_bitcast_fusion.5), kind=kOutput, calls=%fused_computation.31.clone.1 | convolution fusion | flops 377748480 | bytes 12393472 | tf_op jit(solution)/shard_map/while/body/eval_jaxpr/dot_general | solution.py:58
  353.3 10.9 %fusion.220 = (f32[512]{0:T(512)S(1)}, f32[512]{0:T(512)S(1)}, f32[512]{0:T(512)S(1)}, f32[512]{0:T(512)S(1)}, f32[512]{0:T(512)S(1)}, /*index=5*/f32[512]{0:T(512)S(1)}, f32[512,2816]{1,0:T(8,128)}) fusion(f32[512,2816]{1,0:T(8,128)} %get-tuple-element.130, f32[512]{0:T(512)S(1)} %get-tuple-element.131, ...), kind=kOutput, calls=%fused_computation.42.clone.1 | convolution fusion | flops 397931520 | bytes 35474176 | tf_op jit(solution)/shard_map/while/body/eval_jaxpr/dot_general | solution.py:58
  364.2 8.0 %fusion.222 = (f32[512]{0:T(512)S(1)}, f32[512]{0:T(512)S(1)}, f32[512]{0:T(512)S(1)}, f32[512]{0:T(512)S(1)}) fusion(f32[512,2816]{1,0:T(8,128)S(1)} %fusion.219, f32[512]{0:T(512)S(1)} %get-tuple-element.135, pred[2816]{0:T(1024)(128)(4,1)S(1)} %compare_reduce_fusion.2, f32[512]{0:T(512)S(1)} %get-tuple-element.134, ...), kind=kLoop, calls=%fused_computation.40.clone.1 | loop fusion | flops 23066624 | bytes 23087872 | tf_op jit(solution)/shard_map/while/body/eval_jaxpr/reduce_sum | solution.py:66
  395.9 7.4 %dynamic-slice_bitcast_fusion.4 = bf16[2816,1536]{1,0:T(8,128)(2,1)} fusion(bf16[4,2816,1536]{2,1,0:T(8,128)(2,1)} %get-tuple-element.159, s32[]{:T(128)} %get-tuple-element.149), kind=kLoop, calls=%fused_computation.13.clone.1 | loop fusion | bytes 17301508 | tf_op jit(solution)/shard_map/while/body/jit(dynamic_index_in_dim)/squeeze | solution.py:106
  406.9 5.3 %fusion.216 = (f32[512]{0:T(512)S(1)}, f32[512]{0:T(512)S(1)}, f32[512,2816]{1,0:T(8,128)}) fusion(pred[2816]{0:T(1024)(128)(4,1)S(1)} %compare_reduce_fusion.2, f32[512,2816]{1,0:T(8,128)S(1)} %fusion.215, bf16[2816,1536]{1,0:T(8,128)(2,1)} %dynamic-slice_bitcast_fusion.4, bf16[512,768]{1,0:T(8,128)(2,1)S(1)} %dynamic-slice_bitcast_fusion.5), kind=kOutput, calls=%fused_computation.31.clone.1 | convolution fusion | flops 377748480 | bytes 12393472 | tf_op jit(solution)/shard_map/while/body/eval_jaxpr/dot_general | solution.py:58
  420.7 10.9 %fusion.220 = (f32[512]{0:T(512)S(1)}, f32[512]{0:T(512)S(1)}, f32[512]{0:T(512)S(1)}, f32[512]{0:T(512)S(1)}, f32[512]{0:T(512)S(1)}, /*index=5*/f32[512]{0:T(512)S(1)}, f32[512,2816]{1,0:T(8,128)}) fusion(f32[512,2816]{1,0:T(8,128)} %get-tuple-element.130, f32[512]{0:T(512)S(1)} %get-tuple-element.131, ...), kind=kOutput, calls=%fused_computation.42.clone.1 | convolution fusion | flops 397931520 | bytes 35474176 | tf_op jit(solution)/shard_map/while/body/eval_jaxpr/dot_general | solution.py:58
  431.6 8.0 %fusion.222 = (f32[512]{0:T(512)S(1)}, f32[512]{0:T(512)S(1)}, f32[512]{0:T(512)S(1)}, f32[512]{0:T(512)S(1)}) fusion(f32[512,2816]{1,0:T(8,128)S(1)} %fusion.219, f32[512]{0:T(512)S(1)} %get-tuple-element.135, pred[2816]{0:T(1024)(128)(4,1)S(1)} %compare_reduce_fusion.2, f32[512]{0:T(512)S(1)} %get-tuple-element.134, ...), kind=kLoop, calls=%fused_computation.40.clone.1 | loop fusion | flops 23066624 | bytes 23087872 | tf_op jit(solution)/shard_map/while/body/eval_jaxpr/reduce_sum | solution.py:66
  (208 shorter events, 196.2 us)
Async XLA Ops:
  6.5 32.4 %all-gather.2.cloned.1.call-start = ((), (), s32[]{:S(2)}) async-start(), calls=%async_computation | async-start | bytes 18874368 | tf_op jit(solution)/shard_map/all_gather | solution.py:83
  12.5 5.8 %copy-start.5 = (s32[16,2,3]{0,1,2:T(2,128)S(1)}, s32[16,2,3]{0,1,2:T(2,128)}, u32[]{:S(2)}) copy-start(s32[16,2,3]{0,1,2:T(2,128)} %param.21) | copy-start | bytes 1156
  62.6 2.8 copy-start.1
  66.6 51.7 %collective-permute-start = (bf16[1,4,128,1536]{3,2,1,0:T(8,128)(2,1)}, bf16[1,4,128,1536]{3,2,1,0:T(8,128)(2,1)}, u32[]{:S(2)}, u32[]{:S(2)}) collective-permute-start(bf16[1,4,128,1536]{3,2,1,0:T(8,128)(2,1)} %slice_bitcast_fusion.1), channel_id=1, source_target_pairs={{0,4},{4,8},{8,12},{1,5},{5,9},{9,13},{2,6},{6,10},{10,14},{3,7},{... | collective-permute-start | bytes 4718600 | tf_op jit(solution)/shard_map/ppermute | solution.py:13
  77.1 61.2 %collective-permute-start.1 = (bf16[2,2,128,1536]{3,2,1,0:T(8,128)(2,1)}, bf16[2,2,128,1536]{3,2,1,0:T(8,128)(2,1)}, u32[]{:S(2)}, u32[]{:S(2)}) collective-permute-start(bf16[2,2,128,1536]{3,2,1,0:T(8,128)(2,1)} %bitcast.15), channel_id=1, source_target_pairs={{0,4},{4,8},{8,12},{1,5},{5,9},{9,13},{2,6},{6,10},{10,14},{3,7},{... | collective-permute-start | bytes 4718600 | tf_op jit(solution)/shard_map/ppermute | solution.py:13
  85.5 86.5 %collective-permute-start.2 = (bf16[4,1,128,1536]{3,2,0,1:T(8,128)(2,1)}, bf16[4,1,128,1536]{3,2,0,1:T(8,128)(2,1)}, u32[]{:S(2)}, u32[]{:S(2)}) collective-permute-start(bf16[4,1,128,1536]{3,2,0,1:T(8,128)(2,1)} %bitcast.22), channel_id=1, source_target_pairs={{0,4},{4,8},{8,12},{1,5},{5,9},{9,13},{2,6},{6,10},{10,14},{3,7},{... | collective-permute-start | bytes 4718600 | tf_op jit(solution)/shard_map/ppermute | solution.py:13
  87.4 57.5 %collective-permute-start.3 = (bf16[1,4,128,1536]{3,2,1,0:T(8,128)(2,1)}, bf16[1,4,128,1536]{3,2,1,0:T(8,128)(2,1)}, u32[]{:S(2)}, u32[]{:S(2)}) collective-permute-start(bf16[1,4,128,1536]{3,2,1,0:T(8,128)(2,1)} %slice_bitcast_fusion), channel_id=1, source_target_pairs={{4,0},{8,4},{12,8},{5,1},{9,5},{13,9},{6,2},{10,6},{14,10},{7,3},{... | collective-permute-start | bytes 4718600 | tf_op jit(solution)/shard_map/ppermute | solution.py:13
  98.1 60.6 %collective-permute-start.4 = (bf16[2,2,128,1536]{3,2,1,0:T(8,128)(2,1)}, bf16[2,2,128,1536]{3,2,1,0:T(8,128)(2,1)S(1)}, u32[]{:S(2)}, u32[]{:S(2)}) collective-permute-start(bf16[2,2,128,1536]{3,2,1,0:T(8,128)(2,1)} %bitcast.30), channel_id=1, source_target_pairs={{4,0},{8,4},{12,8},{5,1},{9,5},{13,9},{6,2},{10,6},{14,10},{7,3},{... | collective-permute-start | bytes 4718600 | tf_op jit(solution)/shard_map/ppermute | solution.py:13
  118.4 73.9 %collective-permute-start.5 = (bf16[4,1,128,1536]{3,2,0,1:T(8,128)(2,1)S(1)}, bf16[4,1,128,1536]{3,2,0,1:T(8,128)(2,1)S(1)}, u32[]{:S(2)}, u32[]{:S(2)}) collective-permute-start(bf16[4,1,128,1536]{3,2,0,1:T(8,128)(2,1)S(1)} %bitcast.111), channel_id=1, source_target_pairs={{4,0},{8,4},{12,8},{5,1},{9,5},{13,9},{6,2},{10,6},{14,10},{7,3},{... | collective-permute-start | bytes 4718600 | tf_op jit(solution)/shard_map/ppermute | solution.py:13
  120.3 18.0 %copy-start.3 = (bf16[4,128,1536]{2,1,0:T(8,128)(2,1)S(1)}, bf16[4,128,1536]{2,1,0:T(8,128)(2,1)}, u32[]{:S(2)}) copy-start(bf16[4,128,1536]{2,1,0:T(8,128)(2,1)} %get-tuple-element.69) | copy-start | bytes 4718596
  143.1 3.5 slice-start.4
  146.5 12.1 %copy-start.2 = (bf16[4,128,1536]{2,1,0:T(8,128)(2,1)S(1)}, bf16[4,128,1536]{2,1,0:T(8,128)(2,1)}, u32[]{:S(2)}) copy-start(bf16[4,128,1536]{2,1,0:T(8,128)(2,1)} %get-tuple-element.66) | copy-start | bytes 4718596
  202.1 14.2 %copy-start = (bf16[512,768]{1,0:T(8,128)(2,1)}, bf16[512,768]{1,0:T(8,128)(2,1)S(1)}, u32[]{:S(2)}) copy-start(bf16[512,768]{1,0:T(8,128)(2,1)S(1)} %dynamic-slice_bitcast_fusion.5) | copy-start | bytes 2359300 | tf_op jit(solution)/shard_map/while
  229.3 11.3 %slice-start.2 = ((s8[5767168]{0:T(1024)(128)(4,1)}), s8[4194304]{0:T(1024)(128)(4,1)S(1)}, s32[]{:S(2)}) async-start(s8[5767168]{0:T(1024)(128)(4,1)} %bitcast.95), calls=%async_computation.3 | async-start | bytes 8388608 | tf_op jit(solution)/shard_map/while
  229.3 11.3 %slice-start.3 = ((s8[5767168]{0:T(1024)(128)(4,1)}), s8[1572864]{0:T(1024)(128)(4,1)S(1)}, s32[]{:S(2)}) async-start(s8[5767168]{0:T(1024)(128)(4,1)} %bitcast.95), calls=%async_computation.4 | async-start | bytes 3145728 | tf_op jit(solution)/shard_map/while
  248.7 6.7 %slice-start = ((s8[5767168]{0:T(1024)(128)(4,1)}), s8[4194304]{0:T(1024)(128)(4,1)S(1)}, s32[]{:S(2)}) async-start(s8[5767168]{0:T(1024)(128)(4,1)} %bitcast.93), calls=%async_computation.1 | async-start | bytes 8388608 | tf_op jit(solution)/shard_map/while
  252.1 3.4 slice-start.1
  269.6 14.2 %copy-start = (bf16[512,768]{1,0:T(8,128)(2,1)}, bf16[512,768]{1,0:T(8,128)(2,1)S(1)}, u32[]{:S(2)}) copy-start(bf16[512,768]{1,0:T(8,128)(2,1)S(1)} %dynamic-slice_bitcast_fusion.5) | copy-start | bytes 2359300 | tf_op jit(solution)/shard_map/while
  296.7 11.3 %slice-start.2 = ((s8[5767168]{0:T(1024)(128)(4,1)}), s8[4194304]{0:T(1024)(128)(4,1)S(1)}, s32[]{:S(2)}) async-start(s8[5767168]{0:T(1024)(128)(4,1)} %bitcast.95), calls=%async_computation.3 | async-start | bytes 8388608 | tf_op jit(solution)/shard_map/while
  296.7 11.3 %slice-start.3 = ((s8[5767168]{0:T(1024)(128)(4,1)}), s8[1572864]{0:T(1024)(128)(4,1)S(1)}, s32[]{:S(2)}) async-start(s8[5767168]{0:T(1024)(128)(4,1)} %bitcast.95), calls=%async_computation.4 | async-start | bytes 3145728 | tf_op jit(solution)/shard_map/while
  316.1 6.7 %slice-start = ((s8[5767168]{0:T(1024)(128)(4,1)}), s8[4194304]{0:T(1024)(128)(4,1)S(1)}, s32[]{:S(2)}) async-start(s8[5767168]{0:T(1024)(128)(4,1)} %bitcast.93), calls=%async_computation.1 | async-start | bytes 8388608 | tf_op jit(solution)/shard_map/while
  319.5 3.4 slice-start.1
  337.0 14.2 %copy-start = (bf16[512,768]{1,0:T(8,128)(2,1)}, bf16[512,768]{1,0:T(8,128)(2,1)S(1)}, u32[]{:S(2)}) copy-start(bf16[512,768]{1,0:T(8,128)(2,1)S(1)} %dynamic-slice_bitcast_fusion.5) | copy-start | bytes 2359300 | tf_op jit(solution)/shard_map/while
  364.2 11.3 %slice-start.2 = ((s8[5767168]{0:T(1024)(128)(4,1)}), s8[4194304]{0:T(1024)(128)(4,1)S(1)}, s32[]{:S(2)}) async-start(s8[5767168]{0:T(1024)(128)(4,1)} %bitcast.95), calls=%async_computation.3 | async-start | bytes 8388608 | tf_op jit(solution)/shard_map/while
  364.2 11.3 %slice-start.3 = ((s8[5767168]{0:T(1024)(128)(4,1)}), s8[1572864]{0:T(1024)(128)(4,1)S(1)}, s32[]{:S(2)}) async-start(s8[5767168]{0:T(1024)(128)(4,1)} %bitcast.95), calls=%async_computation.4 | async-start | bytes 3145728 | tf_op jit(solution)/shard_map/while
  383.6 6.7 %slice-start = ((s8[5767168]{0:T(1024)(128)(4,1)}), s8[4194304]{0:T(1024)(128)(4,1)S(1)}, s32[]{:S(2)}) async-start(s8[5767168]{0:T(1024)(128)(4,1)} %bitcast.93), calls=%async_computation.1 | async-start | bytes 8388608 | tf_op jit(solution)/shard_map/while
  387.0 3.4 slice-start.1
  404.5 14.2 %copy-start = (bf16[512,768]{1,0:T(8,128)(2,1)}, bf16[512,768]{1,0:T(8,128)(2,1)S(1)}, u32[]{:S(2)}) copy-start(bf16[512,768]{1,0:T(8,128)(2,1)S(1)} %dynamic-slice_bitcast_fusion.5) | copy-start | bytes 2359300 | tf_op jit(solution)/shard_map/while
  431.6 11.3 %slice-start.2 = ((s8[5767168]{0:T(1024)(128)(4,1)}), s8[4194304]{0:T(1024)(128)(4,1)S(1)}, s32[]{:S(2)}) async-start(s8[5767168]{0:T(1024)(128)(4,1)} %bitcast.95), calls=%async_computation.3 | async-start | bytes 8388608 | tf_op jit(solution)/shard_map/while
  431.6 11.3 %slice-start.3 = ((s8[5767168]{0:T(1024)(128)(4,1)}), s8[1572864]{0:T(1024)(128)(4,1)S(1)}, s32[]{:S(2)}) async-start(s8[5767168]{0:T(1024)(128)(4,1)} %bitcast.95), calls=%async_computation.4 | async-start | bytes 3145728 | tf_op jit(solution)/shard_map/while
  451.0 6.7 %slice-start = ((s8[5767168]{0:T(1024)(128)(4,1)}), s8[4194304]{0:T(1024)(128)(4,1)S(1)}, s32[]{:S(2)}) async-start(s8[5767168]{0:T(1024)(128)(4,1)} %bitcast.93), calls=%async_computation.1 | async-start | bytes 8388608 | tf_op jit(solution)/shard_map/while
  454.4 3.4 slice-start.1
  (3 other events, 4.8 us)
Sparse Core Ops, SparseCore 0:
  12.7 26.1 all-gather.1
where the time goes:
time: 479 us; the launch traced here: 470 us
  matrix products  193 us (40%)
  local copies, waits for them, and re-layouts  130 us (27%)
  waiting for transfers between devices  68.9 us (14%)
  other arithmetic  46.9 us (10%)
  starting transfers between devices  16.8 us (4%)
  between operations  13.7 us (3%)
    dot_general x24, matrix products, attend_frame(): lax.dot_general(query_head, key_head, (((1,), (1,)), ((), ())), preferred...  108 us
    dot_general x24, matrix products, attend_frame(): jnp.dot(rounded, value_head, preferred_element_type=jnp.float32) / row_total  85.3 us
    ppermute x6, waiting for transfers between devices, passed_along(): return lax.ppermute(block, axis, route)  50.3 us
    gather x6, local copies, waits for them, and re-layouts, select_tiles(): return tile_array[sources[:, None], chosen]  38.6 us
    squeeze x8, local copies, waits for them, and re-layouts, per_device(): return lax.map(attend_frame, (queries, key_set, live_slots))  34.3 us
    reduce_sum x4, other arithmetic, attend_frame(): row_total = jnp.sum(exponent, axis=1, keepdims=True)  32.2 us
    unnamed x24, local copies, waits for them, and re-layouts  26.8 us
    all_gather x1, waiting for transfers between devices, per_device(): whole_frames = lax.all_gather(paired, 'seq', axis=1, tiled=True)  18.7 us
  transfers between devices with their start and end apart: 7, of which 5 were waited for; matrix products, arithmetic and copies ran while one was open for 14% of the time, Pallas kernels for 0%

commit v1 on v0

v1 whole, which is shorter than its diff:
```python
import functools
import math

import jax
import jax.numpy as jnp
from jax import lax
from jax.experimental import pallas as pl
from jax.experimental.pallas import tpu as pltpu
from jax.sharding import PartitionSpec as P

HEAD_DIM = 128
TILE = 128
HALF = TILE // 2
DISTANCES = (1, 2, 4)
POSITIONS = sum(d * n for d, n in ((1, 4), (2, 2), (4, 1)))
EARLY = 8
STRIDE = 16
SCALE = math.log2(math.e) / math.sqrt(HEAD_DIM)
LARGE = 2.0**100
NT = (((1,), (1,)), ((), ()))
BF = jnp.bfloat16
F32 = jnp.float32
ANY = pl.BlockSpec(memory_space=pltpu.HBM)
VMEM_LIMIT = 56 * 2**20


class Layout:
    def __init__(self, frames_here, frame_tiles, frames, lengths):
        self.frames_here = frames_here
        self.frame_tiles = frame_tiles
        self.frames = frames
        self.lengths = lengths
        self.row = 2 * (sum(lengths) + 3)
        self.local = 2 * POSITIONS
        self.early = self.local + frames_here * STRIDE
        self.late = self.early + frames_here * STRIDE
        self.need = self.late + frames_here * STRIDE
        self.size = self.need + 1

    def entry(self, frame, direction, column, slot):
        start = 2 * sum(self.lengths[:column])
        return frame * self.row + start + direction * self.lengths[column] + slot

    def count(self, frame, direction, column):
        return frame * self.row + 2 * sum(self.lengths) + direction * 3 + column

    def remote(self, direction):
        found = []
        for away in reversed(range(self.frames_here)):
            for column in reversed(range(3)):
                distance = DISTANCES[column]
                if away < distance:
                    frame = away if direction == 0 else self.frames_here - 1 - away
                    source = frame - distance if direction == 0 else frame + distance
                    found.append((frame, column, source % self.frames_here))
        return found


def table_kernel(lay, place_ref, lists_ref, table_ref, seen_ref):
    first = place_ref[0]
    here = lay.frames_here

    def distinct(target, direction, on_slot, on_new):
        def clear(i, _):
            seen_ref[i] = -1
            return 0

        lax.fori_loop(0, here * lay.frame_tiles, clear, 0)
        used = jnp.int32(0)
        for frame, column, source in lay.remote(direction):
            live = lists_ref[lay.count(target + frame, direction, column)]
            for slot in range(lay.lengths[column]):
                name = lists_ref[lay.entry(target + frame, direction, column, slot)]
                name = name + source * lay.frame_tiles
                alive = slot < live
                known = seen_ref[name]
                fresh = jnp.logical_and(alive, known < 0)
                place = jnp.where(fresh, used, known)
                seen_ref[name] = place
                on_new(used, name)
                on_slot(frame, place, alive)
                used = used + fresh.astype(jnp.int32)
        return used

    def clear_table(i, _):
        table_ref[i] = 0
        return 0

    lax.fori_loop(0, lay.size, clear_table, 0)
    for direction in (0, 1):
        target = first + (here if direction == 0 else -here)
        target = jnp.clip(target, 0, lay.frames - here)

        def note(used, name, direction=direction):
            table_ref[direction * POSITIONS + jnp.minimum(used, POSITIONS - 1)] = name

        last = distinct(target, direction, lambda *_: None, note)
        del last

    def append(base, frame, item, alive):
        at = base + frame * STRIDE
        filled = table_ref[at]
        table_ref[at + 1 + filled] = item
        table_ref[at] = filled + alive.astype(jnp.int32)

    for direction in (0, 1):

        def on_slot(frame, place, alive, direction=direction):
            early = place < EARLY
            append(lay.early, frame, direction * EARLY + place, jnp.logical_and(alive, early))
            late = direction * (POSITIONS - EARLY) + place - EARLY
            append(lay.late, frame, late, jnp.logical_and(alive, jnp.logical_not(early)))

        distinct(first, direction, on_slot, lambda *_: None)
        for frame in range(here):
            for column, distance in enumerate(DISTANCES):
                source = frame + (2 * direction - 1) * distance
                if 0 <= source < here:
                    live = lists_ref[lay.count(first + frame, direction, column)]
                    for slot in range(lay.lengths[column]):
                        name = lists_ref[lay.entry(first + frame, direction, column, slot)]
                        append(lay.local, frame, source * lay.frame_tiles + name, slot < live)


def make_table(lay, place, lists):
    smem = pl.BlockSpec(memory_space=pltpu.SMEM)
    return pl.pallas_call(
        functools.partial(table_kernel, lay),
        in_specs=[smem, smem],
        out_specs=smem,
        out_shape=jax.ShapeDtypeStruct((lay.size,), jnp.int32),
        scratch_shapes=[pltpu.SMEM((lay.frames_here * lay.frame_tiles,), jnp.int32)],
        name="tile_tables",
    )(place, lists)


def pack_kernel(lay, jobs, place_ref, table_ref, *refs):
    sources, outs, sems = refs[:-1 - len(jobs)], refs[-1 - len(jobs) : -1], refs[-1]
    core = place_ref[1]
    tiles_here = lay.frame_tiles // 2
    number = 0
    waits = []
    for (pair, direction, begin, length, lead), out in zip(jobs, outs):
        for item in range(length):
            name = table_ref[direction * POSITIONS + begin + item]
            frame = name // lay.frame_tiles
            tile = name % lay.frame_tiles
            mine = tile // tiles_here == core
            row = pl.multiple_of((tile % tiles_here) * TILE + core * HALF, HALF)
            target = out.at[item] if lead is None else out.at[lead, item]
            own = sources[2 * pair].at[frame, pl.ds(row, HALF), :]
            other = sources[2 * pair + 1].at[frame, pl.ds(row, HALF), :]
            sem = sems.at[number]
            number += 1

            @pl.when(mine)
            def _(own=own, target=target, sem=sem):
                pltpu.make_async_copy(own, target, sem).start()

            @pl.when(jnp.logical_not(mine))
            def _(other=other, target=target, sem=sem):
                pltpu.make_async_copy(other, target, sem).start()

            waits.append((own, target, sem))
    for own, target, sem in waits:
        pltpu.make_async_copy(own, target, sem).wait()


def attend_tiles(q_ref, kbuf, vbuf, ids, m_s, l_s, add, heads):
    for head in range(heads):
        cols = slice(head * HEAD_DIM, (head + 1) * HEAD_DIM)
        keys = jnp.concatenate([kbuf[i, :, cols] for i in ids], axis=0)
        values = jnp.concatenate([vbuf[i, :, cols] for i in ids], axis=0)
        scores = lax.dot_general(q_ref[0, :, cols], keys, NT, preferred_element_type=F32)
        shift = jnp.concatenate([m_s[head]] * len(ids), axis=1)
        weights = jnp.exp2((scores - shift) * SCALE).astype(BF)
        mixed = jnp.dot(
            weights,
            jnp.concatenate([values, jnp.ones_like(values)], axis=1),
            preferred_element_type=F32,
        )
        add(cols, mixed[:, :HEAD_DIM])
        l_s[head] += mixed[:, HEAD_DIM:]


def attend_list(q_ref, kbuf, vbuf, table_ref, base, m_s, l_s, add, heads):
    count = table_ref[base]

    def ids(start, n):
        return [table_ref[base + 1 + start + j] for j in range(n)]

    def four(i, _):
        attend_tiles(q_ref, kbuf, vbuf, ids(4 * i, 4), m_s, l_s, add, heads)
        return 0

    lax.fori_loop(0, count // 4, four, 0)

    @pl.when(count % 4 >= 2)
    def _():
        attend_tiles(q_ref, kbuf, vbuf, ids(count // 4 * 4, 2), m_s, l_s, add, heads)

    @pl.when(count % 2 == 1)
    def _():
        attend_tiles(q_ref, kbuf, vbuf, ids(count - 1, 1), m_s, l_s, add, heads)


def save_stats(stat_ref, m_s, l_s, heads):
    rows = stat_ref.shape[1]
    lane = lax.broadcasted_iota(jnp.int32, (rows, 128), 1)
    stat = jnp.zeros((rows, 128), F32)
    for head in range(heads):
        stat = jnp.where(lane == head, l_s[head], stat)
        stat = jnp.where(lane == 64 + head, m_s[head], stat)
    stat_ref[0] = stat


def load_stats(stat_ref, m_s, l_s, heads):
    rows = stat_ref.shape[1]
    for head in range(heads):
        l_s[head] = jnp.broadcast_to(stat_ref[0, :, head : head + 1], (rows, 128))
        m_s[head] = jnp.broadcast_to(stat_ref[0, :, 64 + head : 65 + head], (rows, 128))


def local_kernel(lay, heads, place_ref, table_ref, q_ref, k_own, k_other, v_own, v_other, acc_ref, stat_ref, kbuf, vbuf, m_s, l_s, sems):
    frame = pl.program_id(0)
    core = place_ref[1]
    here, tiles = lay.frames_here, lay.frame_tiles
    half = tiles // 2

    def copies(index):
        found = []
        for piece, (source, buf, side) in enumerate(
            ((k_own, kbuf, core), (k_other, kbuf, 1 - core), (v_own, vbuf, core), (v_other, vbuf, 1 - core))
        ):
            for tile in range(half):
                found.append(
                    pltpu.make_async_copy(
                        source.at[index, pl.ds(tile * TILE, TILE), :],
                        buf.at[index * tiles + side * half + tile],
                        sems.at[index, piece * half + tile],
                    )
                )
        return found

    @pl.when(frame == 0)
    def _():
        for index in range(here):
            for copy in copies(index):
                copy.start()
        for copy in copies(0):
            copy.wait()

    for head in range(heads):
        cols = slice(head * HEAD_DIM, (head + 1) * HEAD_DIM)
        own = pl.ds(frame * tiles, tiles)
        keys = kbuf[own, :, cols].reshape(tiles * TILE, HEAD_DIM)
        values = vbuf[own, :, cols].reshape(tiles * TILE, HEAD_DIM)
        scores = lax.dot_general(q_ref[0, :, cols], keys, NT, preferred_element_type=F32)
        top = jnp.max(scores, axis=1, keepdims=True)
        weights = jnp.exp2((scores - top) * SCALE).astype(BF)
        mixed = jnp.dot(
            weights,
            jnp.concatenate([values, jnp.ones_like(values)], axis=1),
            preferred_element_type=F32,
        )
        acc_ref[0, :, cols] = mixed[:, :HEAD_DIM]
        l_s[head] = mixed[:, HEAD_DIM:]
        m_s[head] = jnp.broadcast_to(top, m_s.shape[1:])

    @pl.when(frame == 0)
    def _():
        for index in range(1, here):
            for copy in copies(index):
                copy.wait()

    def add(cols, more):
        acc_ref[0, :, cols] += more

    attend_list(q_ref, kbuf, vbuf, table_ref, lay.local + frame * STRIDE, m_s, l_s, add, heads)
    save_stats(stat_ref, m_s, l_s, heads)


def local_call(lay, heads, place, table, queries, k_own, k_other, v_own, v_other):
    here, rows, width = queries.shape
    tiles = lay.frame_tiles
    block = pl.BlockSpec((1, rows, width), lambda f, *_: (f, 0, 0))
    stat = pl.BlockSpec((1, rows, 128), lambda f, *_: (f, 0, 0))
    return pl.pallas_call(
        functools.partial(local_kernel, lay, heads),
        grid_spec=pltpu.PrefetchScalarGridSpec(
            num_scalar_prefetch=2,
            grid=(here,),
            in_specs=[block, ANY, ANY, ANY, ANY],
            out_specs=[block, stat],
            scratch_shapes=[
                pltpu.VMEM((here * tiles, TILE, width), BF),
                pltpu.VMEM((here * tiles, TILE, width), BF),
                pltpu.VMEM((heads, rows, 128), F32),
                pltpu.VMEM((heads, rows, 128), F32),
                pltpu.SemaphoreType.DMA((here, 2 * tiles)),
            ],
        ),
        out_shape=[
            jax.ShapeDtypeStruct((here, rows, width), F32),
            jax.ShapeDtypeStruct((here, rows, 128), F32),
        ],
        compiler_params=pltpu.CompilerParams(vmem_limit_bytes=VMEM_LIMIT),
        cost_estimate=cost(here * rows * heads * 16 * TILE),
        name="attend_local",
    )(place, table, queries, k_own, k_other, v_own, v_other)


def cost(scores):
    return pl.CostEstimate(flops=scores * 4 * HEAD_DIM, bytes_accessed=scores // 8, transcendentals=scores)


def exact_frame(lay, heads, frame, core, table_ref, q_ref, local, received, acc_s, m_s, l_s, tk, tv, sems):
    tiles = lay.frame_tiles
    half = tiles // 2
    m_s[...] = jnp.full(m_s.shape, -jnp.inf, F32)
    l_s[...] = jnp.zeros(l_s.shape, F32)
    acc_s[...] = jnp.zeros(acc_s.shape, F32)

    def fetch(pairs):
        found = [pltpu.make_async_copy(a, b, sems.at[i]) for i, (a, b) in enumerate(pairs)]
        for copy in found:
            copy.start()
        for copy in found:
            copy.wait()

    def tile_step():
        for head in range(heads):
            cols = slice(head * HEAD_DIM, (head + 1) * HEAD_DIM)
            scores = lax.dot_general(q_ref[0, :, cols], tk[:, cols], NT, preferred_element_type=F32)
            before = m_s[head]
            top = jnp.maximum(before, jnp.max(scores, axis=1, keepdims=True))
            fade = jnp.exp2((before - top) * SCALE)
            weights = jnp.exp2((scores - top) * SCALE).astype(BF)
            values = tv[:, cols]
            mixed = jnp.dot(
                weights,
                jnp.concatenate([values, jnp.ones_like(values)], axis=1),
                preferred_element_type=F32,
            )
            acc_s[:, cols] = acc_s[:, cols] * fade + mixed[:, :HEAD_DIM]
            l_s[head] = l_s[head] * fade + mixed[:, HEAD_DIM:]
            m_s[head] = top

    def local_tile(name):
        source, tile = name // tiles, name % tiles
        rows = pl.ds(pl.multiple_of(tile % half * TILE, TILE), TILE)
        mine = tile // half == core

        @pl.when(mine)
        def _():
            fetch(((local[0].at[source, rows, :], tk), (local[2].at[source, rows, :], tv)))

        @pl.when(jnp.logical_not(mine))
        def _():
            fetch(((local[1].at[source, rows, :], tk), (local[3].at[source, rows, :], tv)))

        tile_step()

    def own_step(i, _):
        local_tile(frame * tiles + i)
        return 0

    def list_step(i, _):
        local_tile(table_ref[lay.local + frame * STRIDE + 1 + i])
        return 0

    lax.fori_loop(0, tiles, own_step, 0)
    lax.fori_loop(0, table_ref[lay.local + frame * STRIDE], list_step, 0)
    mine = pl.ds(pl.multiple_of(core * HALF, HALF), HALF)
    others = pl.ds(pl.multiple_of((1 - core) * HALF, HALF), HALF)
    for base, length, pieces in received:

        def far_step(i, _, base=base, length=length, pieces=pieces):
            item = table_ref[base + frame * STRIDE + 1 + i]
            for direction in (0, 1):

                @pl.when(item // length == direction)
                def _():
                    at = item % length
                    fetch(
                        tuple(
                            (pieces(direction, kv, side, at), buf.at[rows, :])
                            for kv, buf in enumerate((tk, tv))
                            for side, rows in enumerate((mine, others))
                        )
                    )

            tile_step()
            return 0

        lax.fori_loop(0, table_ref[base + frame * STRIDE], far_step, 0)


def finish(out_ref, acc_s, l_s, heads):
    for head in range(heads):
        cols = slice(head * HEAD_DIM, (head + 1) * HEAD_DIM)
        out_ref[0, :, cols] = (acc_s[:, cols] / l_s[head]).astype(out_ref.dtype)


def early_piece(refs, direction, kv, side, at):
    return refs[4 * kv + 2 * side + direction].at[at]


def late_piece(refs, direction, kv, side, at):
    return refs[2 * side + direction].at[kv, at]


def far_kernel(lay, heads, final, place_ref, table_ref, q_ref, acc_ref, stat_ref, *refs):
    here = lay.frames_here
    core = place_ref[1]
    local = refs[:4]
    early_refs = refs[4:12]
    refs = refs[12:]
    received = [(lay.early, EARLY, functools.partial(early_piece, early_refs))]
    length = EARLY
    base = lay.early
    if final:
        late_refs = refs[:4]
        refs = refs[5:]
        length = POSITIONS - EARLY
        base = lay.late
        received.append((lay.late, length, functools.partial(late_piece, late_refs)))
        out_ref, kbuf, vbuf, acc_s, m_s, l_s, tk, tv, sems = refs
    else:
        out_ref, acc_out, stat_out, kbuf, vbuf, acc_s, m_s, l_s, tk, tv, sems = refs
    piece = received[-1][2]
    step = pl.program_id(0)
    frame = step * (here - 1) if final else step
    rows_of = [pl.ds(pl.multiple_of(s * HALF, HALF), HALF) for s in (core, 1 - core)]

    def copies():
        found = []
        for kv, buf in enumerate((kbuf, vbuf)):
            for side in (0, 1):
                for direction in (0, 1):
                    for at in range(length):
                        found.append(
                            pltpu.make_async_copy(
                                piece(direction, kv, side, at),
                                buf.at[direction * length + at, rows_of[side], :],
                                sems.at[len(found)],
                            )
                        )
        return found

    @pl.when(step == 0)
    def _():
        for copy in copies():
            copy.start()

    load_stats(stat_ref, m_s, l_s, heads)
    acc_s[...] = acc_ref[0]

    @pl.when(step == 0)
    def _():
        for copy in copies():
            copy.wait()

    def add(cols, more):
        acc_s[:, cols] += more

    attend_list(q_ref, kbuf, vbuf, table_ref, base + frame * STRIDE, m_s, l_s, add, heads)

    def end():
        @pl.when(jnp.max(l_s[...]) > LARGE)
        def _():
            exact_frame(lay, heads, frame, core, table_ref, q_ref, local, received, acc_s, m_s, l_s, tk, tv, sems)

        finish(out_ref, acc_s, l_s, heads)

    if final:
        end()
    else:
        edge = jnp.logical_or(frame == 0, frame == here - 1)

        @pl.when(jnp.logical_not(edge))
        def _():
            end()

        @pl.when(edge)
        def _():
            acc_out[0] = acc_s[...]
            save_stats(stat_out, m_s, l_s, heads)


def far_call(lay, heads, final, place, table, queries, acc, stats, local, early, late=(), partial_out=None):
    here, rows, width = queries.shape
    steps = 2 if final else here
    index = (lambda s, *_: (s * (here - 1), 0, 0)) if final else (lambda s, *_: (s, 0, 0))
    block = pl.BlockSpec((1, rows, width), index)
    stat = pl.BlockSpec((1, rows, 128), index)
    length = POSITIONS - EARLY if final else EARLY
    anys = [*local, *early, *late] + ([partial_out] if final else [])
    out_shape = [jax.ShapeDtypeStruct((here, rows, width), BF)]
    out_specs = [block]
    aliases = {}
    if final:
        aliases = {5 + len(anys) - 1: 0}
    else:
        out_shape += [jax.ShapeDtypeStruct(acc.shape, F32), jax.ShapeDtypeStruct(stats.shape, F32)]
        out_specs += [block, stat]
        aliases = {3: 1, 4: 2}
    return pl.pallas_call(
        functools.partial(far_kernel, lay, heads, final),
        grid_spec=pltpu.PrefetchScalarGridSpec(
            num_scalar_prefetch=2,
            grid=(steps,),
            in_specs=[block, block, stat] + [ANY] * len(anys),
            out_specs=out_specs,
            scratch_shapes=[
                pltpu.VMEM((2 * length, TILE, width), BF),
                pltpu.VMEM((2 * length, TILE, width), BF),
                pltpu.VMEM((rows, width), F32),
                pltpu.VMEM((heads, rows, 128), F32),
                pltpu.VMEM((heads, rows, 128), F32),
                pltpu.VMEM((TILE, width), BF),
                pltpu.VMEM((TILE, width), BF),
                pltpu.SemaphoreType.DMA((8 * length,)),
            ],
        ),
        out_shape=out_shape,
        input_output_aliases=aliases,
        compiler_params=pltpu.CompilerParams(vmem_limit_bytes=VMEM_LIMIT),
        cost_estimate=cost(steps * rows * heads * 4 * TILE),
        name="attend_late" if final else "attend_early",
    )(place, table, queries, acc, stats, *anys)


def pack_call(lay, jobs, place, table, sources, shapes):
    return pl.pallas_call(
        functools.partial(pack_kernel, lay, jobs),
        in_specs=[pl.BlockSpec(memory_space=pltpu.SMEM)] * 2 + [ANY] * len(sources),
        out_specs=[ANY] * len(shapes),
        out_shape=[jax.ShapeDtypeStruct(s, BF) for s in shapes],
        scratch_shapes=[pltpu.SemaphoreType.DMA((sum(j[3] for j in jobs),))],
        name="pack_tiles",
    )(place, table, *sources)


def shifted(block, axis, step):
    devices = range(lax.axis_size(axis))
    return lax.ppermute(block, axis, [(i, i + step) for i in devices if i + step in devices])


def swapped(block):
    return lax.ppermute(block, "seq", [(0, 1), (1, 0)])


def per_device(queries, key_rows, value_rows, list_one, list_two, list_four, tile_counts):
    here, rows, width = queries.shape
    heads = width // HEAD_DIM
    frames = list_one.shape[0]
    lay = Layout(here, 2 * rows // TILE, frames, (list_one.shape[2], list_two.shape[2], list_four.shape[2]))
    place = jnp.stack([lax.axis_index("frame") * here, lax.axis_index("seq")]).astype(jnp.int32)
    lists = jnp.concatenate(
        [a.reshape(frames, -1) for a in (list_one, list_two, list_four, tile_counts)], axis=1
    ).reshape(-1)

    k_other = swapped(key_rows)
    v_other = swapped(value_rows)
    table = make_table(lay, place, lists)
    late = POSITIONS - EARLY
    one = (EARLY, HALF, width)
    k_up, k_down = pack_call(
        lay, [(0, 0, 0, EARLY, None), (0, 1, 0, EARLY, None)], place, table, (key_rows, k_other), (one, one)
    )
    far_k = (shifted(k_up, "frame", 1), shifted(k_down, "frame", -1))
    v_up, v_down = pack_call(
        lay, [(0, 0, 0, EARLY, None), (0, 1, 0, EARLY, None)], place, table, (value_rows, v_other), (one, one)
    )
    far_v = (shifted(v_up, "frame", 1), shifted(v_down, "frame", -1))
    two = (2, late, HALF, width)
    late_up, late_down = late_pack(lay, place, table, (key_rows, k_other, value_rows, v_other), two)
    far_late = (shifted(late_up, "frame", 1), shifted(late_down, "frame", -1))

    local = (key_rows, k_other, value_rows, v_other)
    acc, stats = local_call(lay, heads, place, table, queries, *local)
    early = (*far_k, *map(swapped, far_k), *far_v, *map(swapped, far_v))
    out, acc, stats = far_call(lay, heads, False, place, table, queries, acc, stats, local, early)
    late_all = (*far_late, *map(swapped, far_late))
    (out,) = far_call(lay, heads, True, place, table, queries, acc, stats, local, early, late_all, out)
    return out


def late_pack_kernel(lay, late, place_ref, table_ref, k_own, k_other, v_own, v_other, up, down, sems):
    jobs = []
    refs = []
    for direction, out in ((0, up), (1, down)):
        for kv in (0, 1):
            jobs.append((kv, direction, EARLY, late, kv))
            refs.append(out)
    pack_kernel(lay, jobs, place_ref, table_ref, k_own, k_other, v_own, v_other, *refs, sems)


def late_pack(lay, place, table, sources, shape):
    late = shape[1]
    return pl.pallas_call(
        functools.partial(late_pack_kernel, lay, late),
        in_specs=[pl.BlockSpec(memory_space=pltpu.SMEM)] * 2 + [ANY] * 4,
        out_specs=[ANY] * 2,
        out_shape=[jax.ShapeDtypeStruct(shape, BF)] * 2,
        scratch_shapes=[pltpu.SemaphoreType.DMA((4 * late,))],
        name="pack_late",
    )(place, table, *sources)


def solution(mesh):
    placed = (
        P(("clips", "frame"), "seq", "head"),
        P(("clips", "frame"), "seq", "head"),
        P(("clips", "frame"), "seq", "head"),
        P("clips", None, None),
        P("clips", None, None),
        P("clips", None, None),
        P("clips", None, None),
    )
    return jax.shard_map(
        per_device,
        mesh=mesh,
        in_specs=placed,
        out_specs=P(("clips", "frame"), "seq", "head"),
        check_vma=False,
    )
```

time: 479 us -> 269 us (0.56); the launches traced: 470 us -> 266 us
  Pallas kernels: 0 us -> 220 us
  matrix products: 193 us -> 0 us
  local copies, waits for them, and re-layouts: 130 us -> 4.54 us
  waiting for transfers between devices: 68.9 us -> 15.2 us
  other arithmetic: 46.9 us -> 1.37 us
  between operations: 13.7 us -> 0.45 us
  starting transfers between devices: 16.8 us -> 24.3 us
    pallas_call x0 -> x7, Pallas kernels: none -> 220 us  [the longest x2 99.2 us: pack_call(): pl.pallas_call(functools.partial(pack_kernel, lay, jobs), in_specs=[pl.Bl...]
    dot_general x48 -> x0, matrix products: 193 us -> none  [the longest x24 108 us: attend_frame(): lax.dot_general(query_head, key_head, (((1,), (1,)), ((), ())), preferred...]
    gather x15 -> x0, local copies, waits for them, and re-layouts: 42.7 us -> none  [the longest x6 38.6 us: select_tiles(): return tile_array[sources[:, None], chosen]]
    ppermute x6 -> x14, waiting for transfers between devices: 50.3 us -> 15.2 us  [the longest x6 12.3 us: shifted(): lax.ppermute(block, axis, [(i, i + step) for i in devices if i + step in...]
    squeeze x8 -> x0, local copies, waits for them, and re-layouts: 34.3 us -> none  [per_device(): return lax.map(attend_frame, (queries, key_set, live_slots))]
    reduce_sum x4 -> x0, other arithmetic: 32.2 us -> none  [attend_frame(): row_total = jnp.sum(exponent, axis=1, keepdims=True)]
    unnamed x24 -> x23, local copies, waits for them, and re-layouts: 26.8 us -> 3.78 us
    all_gather x1 -> x0, waiting for transfers between devices: 18.7 us -> none  [per_device(): whole_frames = lax.all_gather(paired, 'seq', axis=1, tiled=True)]
  transfers between devices with their start and end apart: 7 -> 14, of which waited for: 5 -> 3; matrix products, arithmetic and copies ran while one was open for 14% -> 1% of each run, Pallas kernels for 0% -> 80%
where the time goes in v1:
time: 269 us; the launch traced here: 266 us
  Pallas kernels  220 us (82%)
  starting transfers between devices  24.3 us (9%)
  waiting for transfers between devices  15.2 us (6%)
  local copies, waits for them, and re-layouts  4.54 us (2%)
    pallas_call x2, Pallas kernels, pack_call(): pl.pallas_call(functools.partial(pack_kernel, lay, jobs), in_specs=[pl.Bl...  99.2 us
    pallas_call x1, Pallas kernels, late_pack(): pl.pallas_call(functools.partial(late_pack_kernel, lay, late), in_specs=[...  49.6 us
    pallas_call x1, Pallas kernels, local_call(): pl.pallas_call(functools.partial(local_kernel, lay, heads), grid_spec=plt...  35.2 us
    pallas_call x2, Pallas kernels, far_call(): pl.pallas_call(functools.partial(far_kernel, lay, heads, final), grid_spe...  32.2 us
    ppermute x6, starting transfers between devices, shifted(): lax.ppermute(block, axis, [(i, i + step) for i in devices if i + step in...  15.8 us
    ppermute x6, waiting for transfers between devices, shifted(): lax.ppermute(block, axis, [(i, i + step) for i in devices if i + step in...  12.3 us
    ppermute x8, starting transfers between devices, swapped(): return lax.ppermute(block, 'seq', [(0, 1), (1, 0)])  8.5 us
  transfers between devices with their start and end apart: 14, of which 3 were waited for; matrix products, arithmetic and copies ran while one was open for 1% of the time, Pallas kernels for 80%

profile of v1, /device:TPU:19, one launch (start us, length us, event | category | flops | bytes accessed | tf_op | source)
XLA Modules:
  0.0 265.9 jit_solution(11759987628214319494)
XLA Ops:
  0.0 0.7 collective-permute-start
  0.7 0.7 copy.12
  1.4 0.7 pad_add_fusion
  2.1 0.1 copy.13
  2.2 0.7 reshape.19.lists_ref
  2.9 0.6 pad_add_fusion.1.place_ref
  3.5 3.9 %tile_tables.1.table_ref = s32[217]{0:T(256)} custom-call(s32[2]{0:T(128)} %pad_add_fusion.1.place_ref, s32[320]{0:T(512)} %reshape.19.lists_ref), custom_call_target="tpu_custom_call" | custom-call | tf_op jit(solution)/shard_map/tile_tables/pallas_call | solution.py:127
  7.4 2.9 %collective-permute-done.k_other.refs_1_ = bf16[4,512,768]{2,1,0:T(8,128)(2,1)S(1)} collective-permute-done((bf16[4,512,768]{2,1,0:T(8,128)(2,1)}, bf16[4,512,768]{2,1,0:T(8,128)(2,1)S(1)}, u32[]{:S(2)}, u32[]{:S(2)}) %collective-permute-start) | collective-permute-done | bytes 3145760 | tf_op jit(solution)/shard_map/ppermute | solution.py:551
  10.3 1.7 copy-done
  12.0 49.6 %pack_tiles.2 = (bf16[8,64,768]{2,1,0:T(8,128)(2,1)}, bf16[8,64,768]{2,1,0:T(8,128)(2,1)}) custom-call(s32[2]{0:T(128)} %pad_add_fusion.1.place_ref, s32[217]{0:T(256)} %tile_tables.1.table_ref, bf16[4,512,768]{2,1,0:T(8,128)(2,1)} %refs_0_.7, bf16[4,512,768]{2,1,0:T(8,128)(2,1)} %copy-done), custom_call_target="tpu_custom_call" | custom-call | tf_op jit(solution)/shard_map/pack_tiles/pallas_call | solution.py:535
  61.6 3.2 %collective-permute-start.2 = (bf16[8,64,768]{2,1,0:T(8,128)(2,1)}, bf16[8,64,768]{2,1,0:T(8,128)(2,1)S(1)}, u32[]{:S(2)}, u32[]{:S(2)}) collective-permute-start(bf16[8,64,768]{2,1,0:T(8,128)(2,1)} %get-tuple-element.18), channel_id=1, source_target_pairs={{0,4},{4,8},{8,12},{1,5},{5,9},{9,13},{2,6},{6,10},{10,14},{3,7},{... | collective-permute-start | bytes 2359304 | tf_op jit(solution)/shard_map/ppermute | solution.py:547
  64.8 2.1 collective-permute-start.3
  66.9 49.6 %pack_tiles.3 = (bf16[8,64,768]{2,1,0:T(8,128)(2,1)}, bf16[8,64,768]{2,1,0:T(8,128)(2,1)}) custom-call(s32[2]{0:T(128)} %pad_add_fusion.1.place_ref, s32[217]{0:T(256)} %tile_tables.1.table_ref, bf16[4,512,768]{2,1,0:T(8,128)(2,1)} %refs_2_.3, bf16[4,512,768]{2,1,0:T(8,128)(2,1)} %collective-permute-done.1.v_other.refs_1_.refs_3_), custom_call_target="tpu_custom_call" | custom-call | tf_op jit(solution)/shard_map/pack_tiles/pallas_call | solution.py:535
  116.5 3.2 %collective-permute-start.6 = (bf16[8,64,768]{2,1,0:T(8,128)(2,1)}, bf16[8,64,768]{2,1,0:T(8,128)(2,1)S(1)}, u32[]{:S(2)}, u32[]{:S(2)}) collective-permute-start(bf16[8,64,768]{2,1,0:T(8,128)(2,1)} %get-tuple-element.20), channel_id=1, source_target_pairs={{0,4},{4,8},{8,12},{1,5},{5,9},{9,13},{2,6},{6,10},{10,14},{3,7},{... | collective-permute-start | bytes 2359304 | tf_op jit(solution)/shard_map/ppermute | solution.py:547
  119.8 2.0 collective-permute-start.7
  121.8 49.6 %pack_late.1 = (bf16[2,4,64,768]{3,2,1,0:T(8,128)(2,1)}, bf16[2,4,64,768]{3,2,1,0:T(8,128)(2,1)}) custom-call(s32[2]{0:T(128)} %pad_add_fusion.1.place_ref, s32[217]{0:T(256)} %tile_tables.1.table_ref, bf16[4,512,768]{2,1,0:T(8,128)(2,1)} %refs_0_.7, bf16[4,512,768]{2,1,0:T(8,128)(2,1)} %copy-done, bf16[4,512,768]{2,1,0:T(8,128)(2,1)} %refs_2_.3, ...), custom_call_target="tpu_custom_call" | custom-call | tf_op jit(solution)/shard_map/pack_late/pallas_call | solution.py:602
  171.4 3.3 %collective-permute-start.10 = (bf16[2,4,64,768]{3,2,1,0:T(8,128)(2,1)}, bf16[2,4,64,768]{3,2,1,0:T(8,128)(2,1)S(1)}, u32[]{:S(2)}, u32[]{:S(2)}) collective-permute-start(bf16[2,4,64,768]{3,2,1,0:T(8,128)(2,1)} %get-tuple-element.24), channel_id=1, source_target_pairs={{0,4},{4,8},{8,12},{1,5},{5,9},{9,13},{2,6},{6,10},{10,14},{3,7},{... | collective-permute-start | bytes 2359304 | tf_op jit(solution)/shard_map/ppermute | solution.py:547
  174.7 2.0 collective-permute-start.11
  176.7 2.1 collective-permute-start.4
  178.9 0.1 collective-permute-start.5
  179.0 0.4 collective-permute-start.8
  179.4 11.7 %collective-permute-done.10.refs_12_ = bf16[2,4,64,768]{3,2,1,0:T(8,128)(2,1)S(1)} collective-permute-done((bf16[2,4,64,768]{3,2,1,0:T(8,128)(2,1)}, bf16[2,4,64,768]{3,2,1,0:T(8,128)(2,1)S(1)}, u32[]{:S(2)}, u32[]{:S(2)}) %collective-permute-start.10) | collective-permute-done | bytes 786464 | tf_op jit(solution)/shard_map/ppermute | solution.py:547
  191.1 2.4 collective-permute-start.9
  193.5 0.6 collective-permute-done.11.refs_13_
  194.1 2.7 %collective-permute-start.12 = (bf16[2,4,64,768]{3,2,1,0:T(8,128)(2,1)S(1)}, bf16[2,4,64,768]{3,2,1,0:T(8,128)(2,1)}, u32[]{:S(2)}, u32[]{:S(2)}) collective-permute-start(bf16[2,4,64,768]{3,2,1,0:T(8,128)(2,1)S(1)} %collective-permute-done.10.refs_12_), channel_id=1, source_target_pairs={{0,1},{1,0},{2,3},{3,2},{4,5},{5,4},{6,7},{7,6},{8,9},{9,8},{10,11... | collective-permute-start | bytes 2359304 | tf_op jit(solution)/shard_map/ppermute | solution.py:551
  196.8 0.1 collective-permute-start.13
  196.9 35.2 %attend_local.1 = (f32[4,512,768]{2,1,0:T(8,128)}, f32[4,512,128]{2,1,0:T(8,128)}) custom-call(s32[2]{0:T(128)} %pad_add_fusion.1.place_ref, s32[217]{0:T(256)} %tile_tables.1.table_ref, bf16[4,512,768]{2,1,0:T(8,128)(2,1)} %q_ref.5, bf16[4,512,768]{2,1,0:T(8,128)(2,1)} %refs_0_.7, bf16[4,512,768]{2,1,0:T(8,128)(2,1)} %copy-done, ...), custom_call_target="tpu_custom_call" | custom-call | flops 12884901888 | bytes 3145728 | tf_op jit(solution)/shard_map/attend_local/pallas_call | solution.py:288
  232.2 0.8 copy-done.6
  233.0 0.3 copy-done.7
  233.3 0.3 copy-done.8
  233.6 23.9 %attend_early.1 = (bf16[4,512,768]{2,1,0:T(8,128)(2,1)}, f32[4,512,768]{2,1,0:T(8,128)}, f32[4,512,128]{2,1,0:T(8,128)}) custom-call(s32[2]{0:T(128)} %pad_add_fusion.1.place_ref, s32[217]{0:T(256)} %tile_tables.1.table_ref, bf16[4,512,768]{2,1,0:T(8,128)(2,1)} %q_ref.5, ...), custom_call_target="tpu_custom_call", output_to_operand_aliasing={{1}: (3, {}), {2}: (4, {})} | custom-call | flops 3221225472 | bytes 786432 | tf_op jit(solution)/shard_map/attend_early/pallas_call | solution.py:508
  257.5 8.2 %attend_late.1 = bf16[4,512,768]{2,1,0:T(8,128)(2,1)} custom-call(s32[2]{0:T(128)} %pad_add_fusion.1.place_ref, s32[217]{0:T(256)} %tile_tables.1.table_ref, bf16[4,512,768]{2,1,0:T(8,128)(2,1)} %q_ref.5, f32[4,512,768]{2,1,0:T(8,128)} %get-tuple-element.22.acc_ref, f32[4,512,128]{2,1,0:T(8,128)} %get-tuple-element.23.stat_ref, ...), custom_call_target="tpu_custom_call", output_to_operand_aliasing={{}: (21, {})} | custom-call | flops 1610612736 | bytes 393216 | tf_op jit(solution)/shard_map/attend_late/pallas_call | solution.py:508
  (31 shorter events, 0.1 us)
Async XLA Ops:
  0.0 10.3 %collective-permute-start = (bf16[4,512,768]{2,1,0:T(8,128)(2,1)}, bf16[4,512,768]{2,1,0:T(8,128)(2,1)S(1)}, u32[]{:S(2)}, u32[]{:S(2)}) collective-permute-start(bf16[4,512,768]{2,1,0:T(8,128)(2,1)} %refs_0_.7), channel_id=1, source_target_pairs={{0,1},{1,0},{2,3},{3,2},{4,5},{5,4},{6,7},{7,6},{8,9},{9,8},{10,11... | collective-permute-start | bytes 9437192 | tf_op jit(solution)/shard_map/ppermute | solution.py:551
  0.7 66.2 %collective-permute-start.1 = (bf16[4,512,768]{2,1,0:T(8,128)(2,1)}, bf16[4,512,768]{2,1,0:T(8,128)(2,1)}, u32[]{:S(2)}, u32[]{:S(2)}) collective-permute-start(bf16[4,512,768]{2,1,0:T(8,128)(2,1)} %refs_2_.3), channel_id=1, source_target_pairs={{0,1},{1,0},{2,3},{3,2},{4,5},{5,4},{6,7},{7,6},{8,9},{9,8},{10,11... | collective-permute-start | bytes 9437192 | tf_op jit(solution)/shard_map/ppermute | solution.py:551
  10.3 1.7 copy-start
  61.6 113.1 %collective-permute-start.2 = (bf16[8,64,768]{2,1,0:T(8,128)(2,1)}, bf16[8,64,768]{2,1,0:T(8,128)(2,1)S(1)}, u32[]{:S(2)}, u32[]{:S(2)}) collective-permute-start(bf16[8,64,768]{2,1,0:T(8,128)(2,1)} %get-tuple-element.18), channel_id=1, source_target_pairs={{0,4},{4,8},{8,12},{1,5},{5,9},{9,13},{2,6},{6,10},{10,14},{3,7},{... | collective-permute-start | bytes 2359304 | tf_op jit(solution)/shard_map/ppermute | solution.py:547
  64.8 111.9 %collective-permute-start.3 = (bf16[8,64,768]{2,1,0:T(8,128)(2,1)}, bf16[8,64,768]{2,1,0:T(8,128)(2,1)S(1)}, u32[]{:S(2)}, u32[]{:S(2)}) collective-permute-start(bf16[8,64,768]{2,1,0:T(8,128)(2,1)} %get-tuple-element.19), channel_id=1, source_target_pairs={{4,0},{8,4},{12,8},{5,1},{9,5},{13,9},{6,2},{10,6},{14,10},{7,3},{... | collective-permute-start | bytes 2359304 | tf_op jit(solution)/shard_map/ppermute | solution.py:547
  116.5 62.4 %collective-permute-start.6 = (bf16[8,64,768]{2,1,0:T(8,128)(2,1)}, bf16[8,64,768]{2,1,0:T(8,128)(2,1)S(1)}, u32[]{:S(2)}, u32[]{:S(2)}) collective-permute-start(bf16[8,64,768]{2,1,0:T(8,128)(2,1)} %get-tuple-element.20), channel_id=1, source_target_pairs={{0,4},{4,8},{8,12},{1,5},{5,9},{9,13},{2,6},{6,10},{10,14},{3,7},{... | collective-permute-start | bytes 2359304 | tf_op jit(solution)/shard_map/ppermute | solution.py:547
  119.8 59.2 %collective-permute-start.7 = (bf16[8,64,768]{2,1,0:T(8,128)(2,1)}, bf16[8,64,768]{2,1,0:T(8,128)(2,1)S(1)}, u32[]{:S(2)}, u32[]{:S(2)}) collective-permute-start(bf16[8,64,768]{2,1,0:T(8,128)(2,1)} %get-tuple-element.21), channel_id=1, source_target_pairs={{4,0},{8,4},{12,8},{5,1},{9,5},{13,9},{6,2},{10,6},{14,10},{7,3},{... | collective-permute-start | bytes 2359304 | tf_op jit(solution)/shard_map/ppermute | solution.py:547
  171.4 19.6 %collective-permute-start.10 = (bf16[2,4,64,768]{3,2,1,0:T(8,128)(2,1)}, bf16[2,4,64,768]{3,2,1,0:T(8,128)(2,1)S(1)}, u32[]{:S(2)}, u32[]{:S(2)}) collective-permute-start(bf16[2,4,64,768]{3,2,1,0:T(8,128)(2,1)} %get-tuple-element.24), channel_id=1, source_target_pairs={{0,4},{4,8},{8,12},{1,5},{5,9},{9,13},{2,6},{6,10},{10,14},{3,7},{... | collective-permute-start | bytes 2359304 | tf_op jit(solution)/shard_map/ppermute | solution.py:547
  174.7 57.3 %copy-start.1 = (bf16[8,64,768]{2,1,0:T(8,128)(2,1)}, bf16[8,64,768]{2,1,0:T(8,128)(2,1)S(1)}, u32[]{:S(2)}) copy-start(bf16[8,64,768]{2,1,0:T(8,128)(2,1)S(1)} %collective-permute-done.2.refs_4_) | copy-start | bytes 2359300
  174.7 19.4 %collective-permute-start.11 = (bf16[2,4,64,768]{3,2,1,0:T(8,128)(2,1)}, bf16[2,4,64,768]{3,2,1,0:T(8,128)(2,1)S(1)}, u32[]{:S(2)}, u32[]{:S(2)}) collective-permute-start(bf16[2,4,64,768]{3,2,1,0:T(8,128)(2,1)} %get-tuple-element.25), channel_id=1, source_target_pairs={{4,0},{8,4},{12,8},{5,1},{9,5},{13,9},{6,2},{10,6},{14,10},{7,3},{... | collective-permute-start | bytes 2359304 | tf_op jit(solution)/shard_map/ppermute | solution.py:547
  176.7 55.3 %copy-start.2 = (bf16[8,64,768]{2,1,0:T(8,128)(2,1)}, bf16[8,64,768]{2,1,0:T(8,128)(2,1)S(1)}, u32[]{:S(2)}) copy-start(bf16[8,64,768]{2,1,0:T(8,128)(2,1)S(1)} %collective-permute-done.3.refs_5_) | copy-start | bytes 2359300
  176.7 20.1 %collective-permute-start.4 = (bf16[8,64,768]{2,1,0:T(8,128)(2,1)S(1)}, bf16[8,64,768]{2,1,0:T(8,128)(2,1)S(1)}, u32[]{:S(2)}, u32[]{:S(2)}) collective-permute-start(bf16[8,64,768]{2,1,0:T(8,128)(2,1)S(1)} %collective-permute-done.2.refs_4_), channel_id=1, source_target_pairs={{0,1},{1,0},{2,3},{3,2},{4,5},{5,4},{6,7},{7,6},{8,9},{9,8},{10,11... | collective-permute-start | bytes 2359304 | tf_op jit(solution)/shard_map/ppermute | solution.py:551
  178.9 53.2 %copy-start.3 = (bf16[8,64,768]{2,1,0:T(8,128)(2,1)}, bf16[8,64,768]{2,1,0:T(8,128)(2,1)S(1)}, u32[]{:S(2)}) copy-start(bf16[8,64,768]{2,1,0:T(8,128)(2,1)S(1)} %collective-permute-done.6.refs_8_) | copy-start | bytes 2359300
  178.9 53.2 %collective-permute-start.5 = (bf16[8,64,768]{2,1,0:T(8,128)(2,1)S(1)}, bf16[8,64,768]{2,1,0:T(8,128)(2,1)S(1)}, u32[]{:S(2)}, u32[]{:S(2)}) collective-permute-start(bf16[8,64,768]{2,1,0:T(8,128)(2,1)S(1)} %collective-permute-done.3.refs_5_), channel_id=1, source_target_pairs={{0,1},{1,0},{2,3},{3,2},{4,5},{5,4},{6,7},{7,6},{8,9},{9,8},{10,11... | collective-permute-start | bytes 2359304 | tf_op jit(solution)/shard_map/ppermute | solution.py:551
  179.0 53.1 %copy-start.4 = (bf16[8,64,768]{2,1,0:T(8,128)(2,1)}, bf16[8,64,768]{2,1,0:T(8,128)(2,1)S(1)}, u32[]{:S(2)}) copy-start(bf16[8,64,768]{2,1,0:T(8,128)(2,1)S(1)} %collective-permute-done.7.refs_9_) | copy-start | bytes 2359300
  179.0 53.2 %collective-permute-start.8 = (bf16[8,64,768]{2,1,0:T(8,128)(2,1)S(1)}, bf16[8,64,768]{2,1,0:T(8,128)(2,1)S(1)}, u32[]{:S(2)}, u32[]{:S(2)}) collective-permute-start(bf16[8,64,768]{2,1,0:T(8,128)(2,1)S(1)} %collective-permute-done.6.refs_8_), channel_id=1, source_target_pairs={{0,1},{1,0},{2,3},{3,2},{4,5},{5,4},{6,7},{7,6},{8,9},{9,8},{10,11... | collective-permute-start | bytes 2359304 | tf_op jit(solution)/shard_map/ppermute | solution.py:551
  191.0 41.0 %copy-start.9 = (bf16[2,4,64,768]{3,2,1,0:T(8,128)(2,1)}, bf16[2,4,64,768]{3,2,1,0:T(8,128)(2,1)S(1)}, u32[]{:S(2)}) copy-start(bf16[2,4,64,768]{3,2,1,0:T(8,128)(2,1)S(1)} %collective-permute-done.10.refs_12_) | copy-start | bytes 2359300
  191.1 41.1 %collective-permute-start.9 = (bf16[8,64,768]{2,1,0:T(8,128)(2,1)S(1)}, bf16[8,64,768]{2,1,0:T(8,128)(2,1)S(1)}, u32[]{:S(2)}, u32[]{:S(2)}) collective-permute-start(bf16[8,64,768]{2,1,0:T(8,128)(2,1)S(1)} %collective-permute-done.7.refs_9_), channel_id=1, source_target_pairs={{0,1},{1,0},{2,3},{3,2},{4,5},{5,4},{6,7},{7,6},{8,9},{9,8},{10,11... | collective-permute-start | bytes 2359304 | tf_op jit(solution)/shard_map/ppermute | solution.py:551
  194.1 38.0 %copy-start.10 = (bf16[2,4,64,768]{3,2,1,0:T(8,128)(2,1)}, bf16[2,4,64,768]{3,2,1,0:T(8,128)(2,1)S(1)}, u32[]{:S(2)}) copy-start(bf16[2,4,64,768]{3,2,1,0:T(8,128)(2,1)S(1)} %collective-permute-done.11.refs_13_) | copy-start | bytes 2359300
  194.1 63.4 %collective-permute-start.12 = (bf16[2,4,64,768]{3,2,1,0:T(8,128)(2,1)S(1)}, bf16[2,4,64,768]{3,2,1,0:T(8,128)(2,1)}, u32[]{:S(2)}, u32[]{:S(2)}) collective-permute-start(bf16[2,4,64,768]{3,2,1,0:T(8,128)(2,1)S(1)} %collective-permute-done.10.refs_12_), channel_id=1, source_target_pairs={{0,1},{1,0},{2,3},{3,2},{4,5},{5,4},{6,7},{7,6},{8,9},{9,8},{10,11... | collective-permute-start | bytes 2359304 | tf_op jit(solution)/shard_map/ppermute | solution.py:551
  196.8 35.3 %copy-start.5 = (bf16[8,64,768]{2,1,0:T(8,128)(2,1)}, bf16[8,64,768]{2,1,0:T(8,128)(2,1)S(1)}, u32[]{:S(2)}) copy-start(bf16[8,64,768]{2,1,0:T(8,128)(2,1)S(1)} %collective-permute-done.4.refs_6_) | copy-start | bytes 2359300
  196.8 60.7 %collective-permute-start.13 = (bf16[2,4,64,768]{3,2,1,0:T(8,128)(2,1)S(1)}, bf16[2,4,64,768]{3,2,1,0:T(8,128)(2,1)}, u32[]{:S(2)}, u32[]{:S(2)}) collective-permute-start(bf16[2,4,64,768]{3,2,1,0:T(8,128)(2,1)S(1)} %collective-permute-done.11.refs_13_), channel_id=1, source_target_pairs={{0,1},{1,0},{2,3},{3,2},{4,5},{5,4},{6,7},{7,6},{8,9},{9,8},{10,11... | collective-permute-start | bytes 2359304 | tf_op jit(solution)/shard_map/ppermute | solution.py:551
  232.1 0.9 copy-start.6
  232.1 1.2 copy-start.7
  232.2 1.4 copy-start.8

commit v2 on v0

v2 whole, which is shorter than its diff:
```python
import functools
import math

import jax
import jax.numpy as jnp
from jax import lax
from jax.experimental import pallas as pl
from jax.experimental.pallas import tpu as pltpu
from jax.sharding import PartitionSpec as P

HEAD_DIM = 128
TILE = 128
HALF = TILE // 2
DISTANCES = (1, 2, 4)
STRIDE = 24
SCALE = math.log2(math.e) / math.sqrt(HEAD_DIM)
LARGE = 2.0**100
NT = (((1,), (1,)), ((), ()))
BF = jnp.bfloat16
F32 = jnp.float32
ANY = pl.BlockSpec(memory_space=pl.ANY)
SMEM = pl.BlockSpec(memory_space=pltpu.SMEM)
VMEM_LIMIT = 56 * 2**20


class Layout:
    def __init__(self, frames_here, frame_tiles, frames, lengths):
        self.here = frames_here
        self.tiles = frame_tiles
        self.half = frame_tiles // 2
        self.own = frames_here * frame_tiles
        self.frames = frames
        self.lengths = lengths
        self.early = self.late = 0
        for frame, column, _ in self.remote(0):
            if self.edge(frame):
                self.late += lengths[column]
            else:
                self.early += lengths[column]
        self.places = self.early + self.late
        self.near = 2 * self.places
        self.far = self.near + frames_here * STRIDE
        self.size = self.far + frames_here * STRIDE

    def edge(self, frame):
        return frame in (0, self.here - 1)

    def remote(self, direction):
        found = []
        for away in (*range(1, self.here - 1), self.here - 1, 0):
            for column in reversed(range(3)):
                distance = DISTANCES[column]
                if away < distance:
                    frame = away if direction == 0 else self.here - 1 - away
                    source = frame - distance if direction == 0 else frame + distance
                    found.append((frame, column, source % self.here))
        return found


def table_kernel(lay, place_ref, one_ref, two_ref, four_ref, count_ref, table_ref, seen_ref):
    lists = (one_ref, two_ref, four_ref)
    first = place_ref[0]

    def distinct(target, direction, on_slot, on_new):
        for i in range(lay.own):
            seen_ref[i] = -1
        used = jnp.int32(0)
        for frame, column, source in lay.remote(direction):
            live = count_ref[column, direction, target + frame]
            for slot in range(lay.lengths[column]):
                name = lists[column][direction, slot, target + frame] + source * lay.tiles
                alive = slot < live
                known = seen_ref[name]
                fresh = jnp.logical_and(alive, known < 0)
                place = jnp.where(fresh, used, known)
                seen_ref[name] = place
                on_new(used, name)
                on_slot(frame, place, alive)
                used = used + fresh.astype(jnp.int32)
        return used

    filled = {}

    def append(base, frame, item, alive):
        at = base + frame * STRIDE
        count = filled.get(at, jnp.int32(0))
        table_ref[at + 1 + count] = item
        filled[at] = count + alive.astype(jnp.int32)

    for direction in (0, 1):
        target = first + (lay.here if direction == 0 else -lay.here)
        target = jnp.clip(target, 0, lay.frames - lay.here)
        for place in range(lay.places):
            table_ref[direction * lay.places + place] = 0

        def note(used, name, direction=direction):
            table_ref[direction * lay.places + jnp.minimum(used, lay.places - 1)] = name

        distinct(target, direction, lambda *_: None, note)

    for direction in (0, 1):

        def on_slot(frame, place, alive, direction=direction):
            if lay.edge(frame):
                append(lay.far, frame, direction * lay.places + place, alive)
            else:
                append(lay.near, frame, lay.own + direction * lay.early + place, alive)

        distinct(first, direction, on_slot, lambda *_: None)
        for frame in range(lay.here):
            for column, distance in enumerate(DISTANCES):
                source = frame + (2 * direction - 1) * distance
                if 0 <= source < lay.here:
                    live = count_ref[column, direction, first + frame]
                    for slot in range(lay.lengths[column]):
                        name = lists[column][direction, slot, first + frame]
                        append(lay.near, frame, source * lay.tiles + name, slot < live)
    for frame in range(lay.here):
        for base in (lay.near, lay.far):
            at = base + frame * STRIDE
            table_ref[at] = filled.get(at, jnp.int32(0))


def make_table(lay, place, lists):
    return pl.pallas_call(
        functools.partial(table_kernel, lay),
        in_specs=[SMEM] * 5,
        out_specs=SMEM,
        out_shape=jax.ShapeDtypeStruct((lay.size,), jnp.int32),
        scratch_shapes=[pltpu.SMEM((lay.own,), jnp.int32)],
        compiler_params=pltpu.CompilerParams(vmem_limit_bytes=VMEM_LIMIT),
        name="tile_tables",
    )(place, *lists)


def pack_kernel(lay, begin, length, place_ref, table_ref, k_own, k_sent, v_own, v_sent, up, down, sems):
    core = place_ref[1]
    waits = []
    for direction, out in ((0, up), (1, down)):
        for item in range(length):
            name = table_ref[direction * lay.places + begin + item]
            frame = name // lay.tiles
            tile = name % lay.tiles
            mine = tile // lay.half == core
            tile = tile % lay.half
            for kv, (own, sent) in enumerate(((k_own, k_sent), (v_own, v_sent))):
                target = out.at[kv, item]
                sem = sems.at[len(waits)]
                here = pltpu.make_async_copy(own.at[frame, tile, core], target, sem)
                there = pltpu.make_async_copy(sent.at[frame, tile], target, sem)
                pl.when(mine)(here.start)
                pl.when(jnp.logical_not(mine))(there.start)
                waits.append(here)
    for copy in waits:
        copy.wait()


def pack_call(lay, begin, length, place, table, sources):
    width = sources[0].shape[-1]
    shape = jax.ShapeDtypeStruct((2, length, HALF, width), BF)
    return pl.pallas_call(
        functools.partial(pack_kernel, lay, begin, length),
        in_specs=[SMEM] * 2 + [ANY] * 4,
        out_specs=[pl.BlockSpec(memory_space=pltpu.VMEM)] * 2,
        out_shape=[shape] * 2,
        scratch_shapes=[pltpu.SemaphoreType.DMA((4 * length,))],
        compiler_params=pltpu.CompilerParams(vmem_limit_bytes=VMEM_LIMIT),
        name="pack_tiles",
    )(place, table, *sources)


def rows_of(buf, index, cols):
    tiles = buf[index, :, :, cols]
    return tiles.reshape(tiles.size // HEAD_DIM, HEAD_DIM)


def mix(weights, values):
    return jnp.dot(
        weights.astype(BF),
        jnp.concatenate([values, jnp.ones_like(values)], axis=1),
        preferred_element_type=F32,
    )


def attend_tiles(q_ref, kbuf, vbuf, ids, m_s, l_s, acc_s, heads):
    for head in range(heads):
        cols = slice(head * HEAD_DIM, (head + 1) * HEAD_DIM)
        keys = jnp.concatenate([rows_of(kbuf, i, cols) for i in ids], axis=0)
        values = jnp.concatenate([rows_of(vbuf, i, cols) for i in ids], axis=0)
        scores = lax.dot_general(q_ref[0, :, cols], keys, NT, preferred_element_type=F32)
        shift = jnp.concatenate([m_s[head]] * len(ids), axis=1)
        mixed = mix(jnp.exp2((scores - shift) * SCALE), values)
        acc_s[:, cols] += mixed[:, :HEAD_DIM]
        l_s[head] += mixed[:, HEAD_DIM:]


def attend_list(q_ref, kbuf, vbuf, table_ref, base, m_s, l_s, acc_s, heads):
    count = table_ref[base]

    def add(start, n):
        ids = [table_ref[base + 1 + start + j] for j in range(n)]
        attend_tiles(q_ref, kbuf, vbuf, ids, m_s, l_s, acc_s, heads)

    def four(i, _):
        add(4 * i, 4)
        return 0

    lax.fori_loop(0, count // 4, four, 0)

    @pl.when(count % 4 >= 2)
    def _():
        add(count // 4 * 4, 2)

    @pl.when(count % 2 == 1)
    def _():
        add(count - 1, 1)


def attend_own(lay, q_ref, kbuf, vbuf, frame, m_s, l_s, acc_s, heads):
    for head in range(heads):
        cols = slice(head * HEAD_DIM, (head + 1) * HEAD_DIM)
        own = pl.ds(frame * lay.tiles, lay.tiles)
        scores = lax.dot_general(
            q_ref[0, :, cols], rows_of(kbuf, own, cols), NT, preferred_element_type=F32
        )
        top = jnp.max(scores[:, :TILE], axis=1, keepdims=True)
        mixed = mix(jnp.exp2((scores - top) * SCALE), rows_of(vbuf, own, cols))
        acc_s[:, cols] = mixed[:, :HEAD_DIM]
        l_s[head] = mixed[:, HEAD_DIM:]
        m_s[head] = jnp.broadcast_to(top, m_s.shape[1:])


def save_stats(stat_ref, m_s, l_s, heads):
    rows = stat_ref.shape[1]
    lane = lax.broadcasted_iota(jnp.int32, (rows, 128), 1)
    stat = jnp.zeros((rows, 128), F32)
    for head in range(heads):
        stat = jnp.where(lane == head, l_s[head], stat)
        stat = jnp.where(lane == 64 + head, m_s[head], stat)
    stat_ref[0] = stat


def load_stats(stat_ref, m_s, l_s, heads):
    rows = stat_ref.shape[1]
    for head in range(heads):
        l_s[head] = jnp.broadcast_to(stat_ref[0, :, head : head + 1], (rows, 128))
        m_s[head] = jnp.broadcast_to(stat_ref[0, :, 64 + head : 65 + head], (rows, 128))


def finish(out_ref, acc_s, l_s, heads):
    for head in range(heads):
        cols = slice(head * HEAD_DIM, (head + 1) * HEAD_DIM)
        out_ref[0, :, cols] = (acc_s[:, cols] / l_s[head]).astype(out_ref.dtype)


def local_copies(lay, index, core, local, bufs, sems):
    found = []
    for kv, (buf, (own, sent, kept)) in enumerate(zip(bufs, (local[:3], local[3:]))):
        mine = pl.ds(index * lay.tiles + core * lay.half, lay.half)
        others = pl.ds(index * lay.tiles + (1 - core) * lay.half, lay.half)
        for piece, (source, target) in enumerate(
            ((own, buf.at[mine]), (sent, buf.at[others, core]), (kept, buf.at[others, 1 - core]))
        ):
            found.append(pltpu.make_async_copy(source.at[index], target, sems.at[index, 3 * kv + piece]))
    return found


def far_copies(core, parts, bufs, begins, sems):
    found = []
    for part, begin in zip(parts, begins):
        length = part[0].shape[1]
        for side in (0, 1):
            for direction in (0, 1):
                for kv in (0, 1):
                    target = bufs[kv].at[
                        pl.ds(begin[direction], length), core if side == 0 else 1 - core
                    ]
                    source = part[2 * side + direction].at[kv]
                    found.append(pltpu.make_async_copy(source, target, sems.at[len(found)]))
    return found


def exact_frame(lay, heads, frame, core, table_ref, q_ref, local, parts, acc_s, m_s, l_s, tk, tv, sems):
    m_s[...] = jnp.full(m_s.shape, -jnp.inf, F32)
    l_s[...] = jnp.zeros(l_s.shape, F32)
    acc_s[...] = jnp.zeros(acc_s.shape, F32)

    def fetch(*pairs):
        found = [pltpu.make_async_copy(a, b, sems.at[i]) for i, (a, b) in enumerate(pairs)]
        for copy in found:
            copy.start()
        for copy in found:
            copy.wait()

    def add_tile():
        for head in range(heads):
            cols = slice(head * HEAD_DIM, (head + 1) * HEAD_DIM)
            keys, values = (t[:, :, cols].reshape(TILE, HEAD_DIM) for t in (tk, tv))
            scores = lax.dot_general(q_ref[0, :, cols], keys, NT, preferred_element_type=F32)
            before = m_s[head]
            top = jnp.maximum(before, jnp.max(scores, axis=1, keepdims=True))
            fade = jnp.exp2((before - top) * SCALE)
            mixed = mix(jnp.exp2((scores - top) * SCALE), values)
            acc_s[:, cols] = acc_s[:, cols] * fade + mixed[:, :HEAD_DIM]
            l_s[head] = l_s[head] * fade + mixed[:, HEAD_DIM:]
            m_s[head] = top

    def near_tile(name):
        source, tile = name // lay.tiles, name % lay.tiles
        mine = tile // lay.half == core
        tile = tile % lay.half
        k_own, k_sent, k_kept, v_own, v_sent, v_kept = (ref.at[source, tile] for ref in local)

        @pl.when(mine)
        def _():
            fetch((k_own, tk), (v_own, tv))

        @pl.when(jnp.logical_not(mine))
        def _():
            fetch(
                (k_sent, tk.at[core]),
                (k_kept, tk.at[1 - core]),
                (v_sent, tv.at[core]),
                (v_kept, tv.at[1 - core]),
            )

    def far_tile(direction, part, item):
        up, other = part[direction], part[2 + direction]
        fetch(
            (up.at[0, item], tk.at[core]),
            (other.at[0, item], tk.at[1 - core]),
            (up.at[1, item], tv.at[core]),
            (other.at[1, item], tv.at[1 - core]),
        )

    def far_places(item, length):
        begin = 0
        for part in parts:
            size = part[0].shape[1]
            for direction in (0, 1):
                at = item - direction * length - begin

                @pl.when(jnp.logical_and(at >= 0, at < size))
                def _(direction=direction, part=part, at=at):
                    far_tile(direction, part, at)

            begin += size

    def own_step(i, _):
        near_tile(frame * lay.tiles + i)
        add_tile()
        return 0

    def near_step(i, _):
        name = table_ref[lay.near + frame * STRIDE + 1 + i]

        @pl.when(name < lay.own)
        def _():
            near_tile(name)

        @pl.when(name >= lay.own)
        def _():
            far_places(name - lay.own, lay.early)

        add_tile()
        return 0

    def far_step(i, _):
        far_places(table_ref[lay.far + frame * STRIDE + 1 + i], lay.places)
        add_tile()
        return 0

    lax.fori_loop(0, lay.tiles, own_step, 0)
    lax.fori_loop(0, table_ref[lay.near + frame * STRIDE], near_step, 0)
    lax.fori_loop(0, table_ref[lay.far + frame * STRIDE], far_step, 0)


def near_kernel(lay, heads, whole, place_ref, table_ref, q_ref, *refs):
    local, refs = refs[:6], refs[6:]
    parts = ()
    if whole:
        parts, refs = (refs[:4],), refs[4:]
        out_ref, acc_s, kbuf, vbuf, m_s, l_s, sems, tk, tv, far_sems = refs
    else:
        acc_out, stat_ref, kbuf, vbuf, m_s, l_s, sems = refs
        acc_s = acc_out.at[0]
    core = place_ref[1]
    step = pl.program_id(0)
    frame = step + 1 if whole else step * (lay.here - 1)
    begin = 1 if whole else 0

    def copies(index):
        return local_copies(lay, index, core, local, (kbuf, vbuf), sems)

    def far():
        return far_copies(core, parts, (kbuf, vbuf), [(lay.own, lay.own + lay.early)] * len(parts), far_sems)

    order = [begin] + [i for i in range(lay.here) if i != begin]

    @pl.when(step == 0)
    def _():
        for index in order:
            for copy in copies(index):
                copy.start()
        if whole:
            for copy in far():
                copy.start()
        for copy in copies(begin):
            copy.wait()

    attend_own(lay, q_ref, kbuf, vbuf, frame, m_s, l_s, acc_s, heads)

    @pl.when(step == 0)
    def _():
        for index in order[1:]:
            for copy in copies(index):
                copy.wait()
        if whole:
            for copy in far():
                copy.wait()

    attend_list(q_ref, kbuf, vbuf, table_ref, lay.near + frame * STRIDE, m_s, l_s, acc_s, heads)
    if whole:

        @pl.when(jnp.max(l_s[...]) > LARGE)
        def _():
            exact_frame(lay, heads, frame, core, table_ref, q_ref, local, parts, acc_s, m_s, l_s, tk, tv, far_sems)

        finish(out_ref, acc_s, l_s, heads)
    else:
        save_stats(stat_ref, m_s, l_s, heads)


def cost(scores):
    return pl.CostEstimate(flops=scores * 4 * HEAD_DIM, bytes_accessed=scores // 8, transcendentals=scores)


def near_call(lay, heads, whole, place, table, queries, local, early=()):
    here, rows, width = queries.shape
    steps = here - 2 if whole else 2
    index = (lambda s, *_: (s + 1, 0, 0)) if whole else (lambda s, *_: (s * (here - 1), 0, 0))
    block = pl.BlockSpec((1, rows, width), index)
    count = lay.own + (2 * lay.early if whole else 0)
    bufs = [pltpu.VMEM((count, 2, HALF, width), BF)] * 2
    sums = [pltpu.VMEM((heads, rows, 128), F32)] * 2
    sems = [pltpu.SemaphoreType.DMA((here, 6))]
    if whole:
        out_specs = [block]
        out_shape = [jax.ShapeDtypeStruct((here, rows, width), BF)]
        scratch = [pltpu.VMEM((rows, width), F32), *bufs, *sums, *sems]
        scratch += [pltpu.VMEM((2, HALF, width), BF)] * 2 + [pltpu.SemaphoreType.DMA((8,))]
    else:
        out_specs = [
            pl.BlockSpec((1, rows, width), lambda s, *_: (s, 0, 0)),
            pl.BlockSpec((1, rows, 128), lambda s, *_: (s, 0, 0)),
        ]
        out_shape = [jax.ShapeDtypeStruct((2, rows, n), F32) for n in (width, 128)]
        scratch = [*bufs, *sums, *sems]
    return pl.pallas_call(
        functools.partial(near_kernel, lay, heads, whole),
        grid_spec=pltpu.PrefetchScalarGridSpec(
            num_scalar_prefetch=2,
            grid=(steps,),
            in_specs=[block] + [ANY] * (6 + len(early)),
            out_specs=out_specs,
            scratch_shapes=scratch,
        ),
        out_shape=out_shape,
        compiler_params=pltpu.CompilerParams(vmem_limit_bytes=VMEM_LIMIT),
        cost_estimate=cost(steps * rows * heads * 16 * TILE),
        name="attend_middle" if whole else "attend_edges",
    )(place, table, queries, *local, *early)


def far_kernel(lay, heads, place_ref, table_ref, q_ref, acc_ref, stat_ref, *refs):
    local, parts = refs[:6], (refs[6:10], refs[10:14])
    out_ref, kbuf, vbuf, acc_s, m_s, l_s, tk, tv, sems = refs[15:]
    step = pl.program_id(0)
    frame = step * (lay.here - 1)
    core = place_ref[1]

    def copies():
        begins = [(0, lay.places), (lay.early, lay.places + lay.early)]
        return far_copies(core, parts, (kbuf, vbuf), begins, sems)

    @pl.when(step == 0)
    def _():
        for copy in copies():
            copy.start()

    load_stats(stat_ref, m_s, l_s, heads)
    acc_s[...] = acc_ref[0]

    @pl.when(step == 0)
    def _():
        for copy in copies():
            copy.wait()

    attend_list(q_ref, kbuf, vbuf, table_ref, lay.far + frame * STRIDE, m_s, l_s, acc_s, heads)

    @pl.when(jnp.max(l_s[...]) > LARGE)
    def _():
        exact_frame(lay, heads, frame, core, table_ref, q_ref, local, parts, acc_s, m_s, l_s, tk, tv, sems)

    finish(out_ref, acc_s, l_s, heads)


def far_call(lay, heads, place, table, queries, acc, stats, local, early, late, out):
    here, rows, width = queries.shape
    block = pl.BlockSpec((1, rows, width), lambda s, *_: (s * (here - 1), 0, 0))
    anys = [*local, *early, *late, out]
    return pl.pallas_call(
        functools.partial(far_kernel, lay, heads),
        grid_spec=pltpu.PrefetchScalarGridSpec(
            num_scalar_prefetch=2,
            grid=(2,),
            in_specs=[
                block,
                pl.BlockSpec((1, rows, width), lambda s, *_: (s, 0, 0)),
                pl.BlockSpec((1, rows, 128), lambda s, *_: (s, 0, 0)),
            ]
            + [ANY] * len(anys),
            out_specs=block,
            scratch_shapes=[
                pltpu.VMEM((2 * lay.places, 2, HALF, width), BF),
                pltpu.VMEM((2 * lay.places, 2, HALF, width), BF),
                pltpu.VMEM((rows, width), F32),
                pltpu.VMEM((heads, rows, 128), F32),
                pltpu.VMEM((heads, rows, 128), F32),
                pltpu.VMEM((2, HALF, width), BF),
                pltpu.VMEM((2, HALF, width), BF),
                pltpu.SemaphoreType.DMA((16,)),
            ],
        ),
        out_shape=jax.ShapeDtypeStruct((here, rows, width), BF),
        input_output_aliases={5 + len(anys) - 1: 0},
        compiler_params=pltpu.CompilerParams(vmem_limit_bytes=VMEM_LIMIT),
        cost_estimate=cost(2 * rows * heads * 7 * TILE),
        name="attend_late",
    )(place, table, queries, acc, stats, *anys)


def shifted(block, axis, step):
    devices = range(lax.axis_size(axis))
    return lax.ppermute(block, axis, [(i, i + step) for i in devices if i + step in devices])


def swapped(block):
    return lax.ppermute(block, "seq", [(0, 1), (1, 0)])


def per_device(queries, key_rows, value_rows, list_one, list_two, list_four, tile_counts):
    here, rows, width = queries.shape
    heads = width // HEAD_DIM
    frames = list_one.shape[0]
    lists = (list_one, list_two, list_four)
    lay = Layout(here, 2 * rows // TILE, frames, tuple(a.shape[2] for a in lists))
    core = lax.axis_index("seq")
    place = jnp.stack([lax.axis_index("frame") * here, core]).astype(jnp.int32)

    k_own, v_own = (a.reshape(here, lay.half, 2, HALF, width) for a in (key_rows, value_rows))
    k_sent, v_sent = (
        swapped(lax.dynamic_index_in_dim(a, 1 - core, 2, keepdims=False)) for a in (k_own, v_own)
    )
    by_frame = [jnp.transpose(a, (1, 2, 0)) for a in lists] + [jnp.transpose(tile_counts, (2, 1, 0))]
    table = make_table(lay, place, by_frame)
    k_kept, v_kept = (
        swapped(lax.dynamic_index_in_dim(a, core, 2, keepdims=False)) for a in (k_own, v_own)
    )

    sources = (k_own, k_sent, v_own, v_sent)
    early = pack_call(lay, 0, lay.early, place, table, sources)
    early, then = lax.optimization_barrier((early, table))
    early = (shifted(early[0], "frame", 1), shifted(early[1], "frame", -1))
    late = pack_call(lay, lay.early, lay.late, place, then, sources)
    late, k_kept = lax.optimization_barrier((late, k_kept))
    late = (shifted(late[0], "frame", 1), shifted(late[1], "frame", -1))

    local = (k_own, k_sent, k_kept, v_own, v_sent, v_kept)
    acc, stats = near_call(lay, heads, False, place, table, queries, local)
    early, stats = lax.optimization_barrier((early, stats))
    early = (*early, *map(swapped, early))
    (out,) = near_call(lay, heads, True, place, table, queries, local, early)
    late, out = lax.optimization_barrier((late, out))
    late = (*late, *map(swapped, late))
    return far_call(lay, heads, place, table, queries, acc, stats, local, early, late, out)


def solution(mesh):
    placed = (
        P(("clips", "frame"), "seq", "head"),
        P(("clips", "frame"), "seq", "head"),
        P(("clips", "frame"), "seq", "head"),
        P("clips", None, None),
        P("clips", None, None),
        P("clips", None, None),
        P("clips", None, None),
    )
    return jax.shard_map(
        per_device,
        mesh=mesh,
        in_specs=placed,
        out_specs=P(("clips", "frame"), "seq", "head"),
        check_vma=False,
    )
```

time: 479 us -> 105 us (0.22); the launches traced: 470 us -> 103 us
  matrix products: 193 us -> 0 us
  local copies, waits for them, and re-layouts: 130 us -> 9.14 us
  Pallas kernels: 0 us -> 70.5 us
  waiting for transfers between devices: 68.9 us -> 8.74 us
  other arithmetic: 46.9 us -> 0.59 us
  between operations: 13.7 us -> 0.38 us
    dot_general x48 -> x0, matrix products: 193 us -> none  [the longest x24 108 us: attend_frame(): lax.dot_general(query_head, key_head, (((1,), (1,)), ((), ())), preferred...]
    pallas_call x0 -> x6, Pallas kernels: none -> 70.5 us  [the longest x2 43.9 us: near_call(): pl.pallas_call(functools.partial(near_kernel, lay, heads, whole), grid_sp...]
    gather x15 -> x0, local copies, waits for them, and re-layouts: 42.7 us -> none  [the longest x6 38.6 us: select_tiles(): return tile_array[sources[:, None], chosen]]
    ppermute x6 -> x12, waiting for transfers between devices: 50.3 us -> 8.74 us  [the longest x8 8.73 us: swapped(): return lax.ppermute(block, 'seq', [(0, 1), (1, 0)])]
    reduce_sum x4 -> x0, other arithmetic: 32.2 us -> none  [attend_frame(): row_total = jnp.sum(exponent, axis=1, keepdims=True)]
    squeeze x8 -> x2, local copies, waits for them, and re-layouts: 34.3 us -> 5.93 us  [per_device(): lax.dynamic_index_in_dim(a, core, 2, keepdims=False)]
    unnamed x24 -> x22, local copies, waits for them, and re-layouts: 26.8 us -> 3.21 us
    all_gather x1 -> x0, waiting for transfers between devices: 18.7 us -> none  [per_device(): whole_frames = lax.all_gather(paired, 'seq', axis=1, tiled=True)]
  transfers between devices with their start and end apart: 7 -> 12, of which waited for: 5 -> 5; matrix products, arithmetic and copies ran while one was open for 14% -> 2% of each run, Pallas kernels for 0% -> 52%
where the time goes in v2:
time: 105 us; the launch traced here: 103 us
  Pallas kernels  70.5 us (67%)
  starting transfers between devices  14.1 us (13%)
  local copies, waits for them, and re-layouts  9.14 us (9%)
  waiting for transfers between devices  8.74 us (8%)
    pallas_call x2, Pallas kernels, near_call(): pl.pallas_call(functools.partial(near_kernel, lay, heads, whole), grid_sp...  43.9 us
    pallas_call x1, Pallas kernels, far_call(): pl.pallas_call(functools.partial(far_kernel, lay, heads), grid_spec=pltpu...  16.3 us
    ppermute x4, starting transfers between devices, shifted(): lax.ppermute(block, axis, [(i, i + step) for i in devices if i + step in...  10.6 us
    ppermute x8, waiting for transfers between devices, swapped(): return lax.ppermute(block, 'seq', [(0, 1), (1, 0)])  8.73 us
    pallas_call x2, Pallas kernels, pack_call(): pl.pallas_call(functools.partial(pack_kernel, lay, begin, length), in_spe...  8.39 us
    squeeze x2, local copies, waits for them, and re-layouts, per_device(): lax.dynamic_index_in_dim(a, core, 2, keepdims=False)  5.93 us
    ppermute x8, starting transfers between devices, swapped(): return lax.ppermute(block, 'seq', [(0, 1), (1, 0)])  3.52 us
    unnamed x22, local copies, waits for them, and re-layouts  3.21 us
  transfers between devices with their start and end apart: 12, of which 5 were waited for; matrix products, arithmetic and copies ran while one was open for 2% of the time, Pallas kernels for 52%

profile of v2, /device:TPU:19, one launch (start us, length us, event | category | flops | bytes accessed | tf_op | source)
XLA Modules:
  0.0 103.4 jit_solution(2884833537485119671)
XLA Ops:
  0.0 4.0 %dynamic-slice_bitcast_fusion.1 = (bf16[4,4,64,768]{3,2,1,0:T(8,128)(2,1)}, bf16[4,4,64,768]{3,2,1,0:T(8,128)(2,1)}) fusion(bf16[4,4,2,64,768]{4,3,2,1,0:T(8,128)(2,1)} %bitcast.16, s32[]{:T(128)S(6)} %select_n.10, s32[]{:T(128)S(6)} %select_n.9), kind=kLoop, calls=%fused_computation.1 | loop fusion | bytes 6291464 | tf_op jit(solution)/shard_map/jit(dynamic_index_in_dim)/squeeze | solution.py:568
  4.0 0.7 collective-permute-start
  4.7 1.9 %dynamic-slice_bitcast_fusion = (bf16[4,4,64,768]{3,2,1,0:T(8,128)(2,1)}, bf16[4,4,64,768]{3,2,1,0:T(8,128)(2,1)}) fusion(bf16[4,4,2,64,768]{4,3,2,1,0:T(8,128)(2,1)S(1)} %bitcast.27, s32[]{:T(128)S(6)} %select_n.10, s32[]{:T(128)S(6)} %select_n.9), kind=kLoop, calls=%fused_computation | loop fusion | bytes 6291464 | tf_op jit(solution)/shard_map/jit(dynamic_index_in_dim)/squeeze | solution.py:568
  6.6 0.0 collective-permute-start.1
  6.6 0.5 collective-permute-start.2
  7.1 0.0 collective-permute-start.3
  7.1 0.6 pad_add_fusion.place_ref
  7.7 1.9 %tile_tables.1.table_ref = s32[216]{0:T(256)} custom-call(s32[2]{0:T(128)} %pad_add_fusion.place_ref, s32[2,4,16]{2,1,0:T(4,128)} %bitcast.28, s32[2,2,16]{2,1,0:T(2,128)} %bitcast.30, s32[2,1,16]{2,1,0:T(1,128)} %bitcast.31, s32[3,2,16]{2,1,0:T(2,128)} %bitcast.29), custom_call_target="tpu_custom_call" | custom-call | tf_op jit(solution)/shard_map/tile_tables/pallas_call | solution.py:125
  9.6 0.0 collective-permute-done.k_sent.refs_1_
  9.6 0.6 collective-permute-done.1.v_sent.refs_4_
  10.2 1.1 %copy-done.1 = bf16[4,4,64,768]{3,2,1,0:T(8,128)(2,1)} copy-done((bf16[4,4,64,768]{3,2,1,0:T(8,128)(2,1)}, bf16[4,4,64,768]{3,2,1,0:T(8,128)(2,1)S(1)}, u32[]{:S(2)}) %copy-start.1) | copy-done | bytes 1572888
  11.4 3.6 %pack_tiles.2 = (bf16[2,4,64,768]{3,2,1,0:T(8,128)(2,1)}, bf16[2,4,64,768]{3,2,1,0:T(8,128)(2,1)}) custom-call(s32[2]{0:T(128)} %pad_add_fusion.place_ref, s32[216]{0:T(256)} %tile_tables.1.table_ref, bf16[4,4,2,64,768]{4,3,2,1,0:T(8,128)(2,1)} %bitcast.17, bf16[4,4,64,768]{3,2,1,0:T(8,128)(2,1)} %collective-permute-done.k_sent.refs_1_, ...), custom_call_target="tpu_custom_call" | custom-call | tf_op jit(solution)/shard_map/pack_tiles/pallas_call | solution.py:161
  14.9 3.2 %collective-permute-start.4 = (bf16[2,4,64,768]{3,2,1,0:T(8,128)(2,1)}, bf16[2,4,64,768]{3,2,1,0:T(8,128)(2,1)S(1)}, u32[]{:S(2)}, u32[]{:S(2)}) collective-permute-start(bf16[2,4,64,768]{3,2,1,0:T(8,128)(2,1)} %get-tuple-element.30), channel_id=1, source_target_pairs={{0,4},{4,8},{8,12},{1,5},{5,9},{9,13},{2,6},{6,10},{10,14},{3,7},{... | collective-permute-start | bytes 2359304 | tf_op jit(solution)/shard_map/ppermute | solution.py:545
  18.2 2.1 %collective-permute-start.5 = (bf16[2,4,64,768]{3,2,1,0:T(8,128)(2,1)}, bf16[2,4,64,768]{3,2,1,0:T(8,128)(2,1)S(1)}, u32[]{:S(2)}, u32[]{:S(2)}) collective-permute-start(bf16[2,4,64,768]{3,2,1,0:T(8,128)(2,1)} %get-tuple-element.31), channel_id=1, source_target_pairs={{4,0},{8,4},{12,8},{5,1},{9,5},{13,9},{6,2},{10,6},{14,10},{7,3},{... | collective-permute-start | bytes 2359304 | tf_op jit(solution)/shard_map/ppermute | solution.py:545
  20.2 4.8 %pack_tiles.3 = (bf16[2,8,64,768]{3,2,1,0:T(8,128)(2,1)}, bf16[2,8,64,768]{3,2,1,0:T(8,128)(2,1)}) custom-call(s32[2]{0:T(128)} %pad_add_fusion.place_ref, s32[216]{0:T(256)} %tile_tables.1.table_ref, bf16[4,4,2,64,768]{4,3,2,1,0:T(8,128)(2,1)} %bitcast.18, bf16[4,4,64,768]{3,2,1,0:T(8,128)(2,1)} %collective-permute-done.k_sent.refs_1_, ...), custom_call_target="tpu_custom_call" | custom-call | tf_op jit(solution)/shard_map/pack_tiles/pallas_call | solution.py:161
  25.1 0.0 collective-permute-done.2.refs_2_
  25.1 3.2 %collective-permute-start.8 = (bf16[2,8,64,768]{3,2,1,0:T(8,128)(2,1)}, bf16[2,8,64,768]{3,2,1,0:T(8,128)(2,1)S(1)}, u32[]{:S(2)}, u32[]{:S(2)}) collective-permute-start(bf16[2,8,64,768]{3,2,1,0:T(8,128)(2,1)} %get-tuple-element.36), channel_id=1, source_target_pairs={{0,4},{4,8},{8,12},{1,5},{5,9},{9,13},{2,6},{6,10},{10,14},{3,7},{... | collective-permute-start | bytes 4718600 | tf_op jit(solution)/shard_map/ppermute | solution.py:545
  28.3 2.1 %collective-permute-start.9 = (bf16[2,8,64,768]{3,2,1,0:T(8,128)(2,1)}, bf16[2,8,64,768]{3,2,1,0:T(8,128)(2,1)S(1)}, u32[]{:S(2)}, u32[]{:S(2)}) collective-permute-start(bf16[2,8,64,768]{3,2,1,0:T(8,128)(2,1)} %get-tuple-element.37), channel_id=1, source_target_pairs={{4,0},{8,4},{12,8},{5,1},{9,5},{13,9},{6,2},{10,6},{14,10},{7,3},{... | collective-permute-start | bytes 4718600 | tf_op jit(solution)/shard_map/ppermute | solution.py:545
  30.4 18.9 %attend_edges.1 = (f32[2,512,768]{2,1,0:T(8,128)}, f32[2,512,128]{2,1,0:T(8,128)}) custom-call(s32[2]{0:T(128)} %pad_add_fusion.place_ref, s32[216]{0:T(256)} %tile_tables.1.table_ref, bf16[4,512,768]{2,1,0:T(8,128)(2,1)} %q_ref.5, bf16[4,4,2,64,768]{4,3,2,1,0:T(8,128)(2,1)} %bitcast.19, bf16[4,4,64,768]{3,2,1,0:T(8,128)(2,1)} %collective-permute-done.k_sent.refs_1_, ...), custom_call_target="tpu_custom_call" | custom-call | flops 6442450944 | bytes 1572864 | tf_op jit(solution)/shard_map/attend_edges/pallas_call | solution.py:459
  49.3 0.0 collective-permute-done.5.refs_7_
  49.4 1.7 %collective-permute-start.6 = (bf16[2,4,64,768]{3,2,1,0:T(8,128)(2,1)S(1)}, bf16[2,4,64,768]{3,2,1,0:T(8,128)(2,1)S(1)}, u32[]{:S(2)}, u32[]{:S(2)}) collective-permute-start(bf16[2,4,64,768]{3,2,1,0:T(8,128)(2,1)S(1)} %collective-permute-done.4.refs_6_), channel_id=1, source_target_pairs={{0,1},{1,0},{2,3},{3,2},{4,5},{5,4},{6,7},{7,6},{8,9},{9,8},{10,11... | collective-permute-start | bytes 2359304 | tf_op jit(solution)/shard_map/ppermute | solution.py:549
  51.0 0.1 collective-permute-start.7
  51.1 1.8 %collective-permute-done.6.refs_8_ = bf16[2,4,64,768]{3,2,1,0:T(8,128)(2,1)S(1)} collective-permute-done((bf16[2,4,64,768]{3,2,1,0:T(8,128)(2,1)S(1)}, bf16[2,4,64,768]{3,2,1,0:T(8,128)(2,1)S(1)}, u32[]{:S(2)}, u32[]{:S(2)}) %collective-permute-start.6) | collective-permute-done | bytes 786464 | tf_op jit(solution)/shard_map/ppermute | solution.py:549
  53.0 1.1 %collective-permute-done.7.refs_9_ = bf16[2,4,64,768]{3,2,1,0:T(8,128)(2,1)S(1)} collective-permute-done((bf16[2,4,64,768]{3,2,1,0:T(8,128)(2,1)S(1)}, bf16[2,4,64,768]{3,2,1,0:T(8,128)(2,1)S(1)}, u32[]{:S(2)}, u32[]{:S(2)}) %collective-permute-start.7) | collective-permute-done | bytes 786464 | tf_op jit(solution)/shard_map/ppermute | solution.py:549
  54.1 0.9 copy-done.10
  55.0 25.0 %attend_middle.1.refs_14_ = bf16[4,512,768]{2,1,0:T(8,128)(2,1)} custom-call(s32[2]{0:T(128)} %pad_add_fusion.place_ref, s32[216]{0:T(256)} %tile_tables.1.table_ref, bf16[4,512,768]{2,1,0:T(8,128)(2,1)} %q_ref.5, bf16[4,4,2,64,768]{4,3,2,1,0:T(8,128)(2,1)} %bitcast.20, bf16[4,4,64,768]{3,2,1,0:T(8,128)(2,1)} %collective-permute-done.k_sent.refs_1_, ...), custom_call_target="tpu_custom_call" | custom-call | flops 6442450944 | bytes 1572864 | tf_op jit(solution)/shard_map/attend_middle/pallas_call | solution.py:459
  80.0 0.4 collective-permute-start.10
  80.5 0.1 collective-permute-start.11
  80.6 2.9 %collective-permute-done.10.refs_12_ = bf16[2,8,64,768]{3,2,1,0:T(8,128)(2,1)S(1)} collective-permute-done((bf16[2,8,64,768]{3,2,1,0:T(8,128)(2,1)S(1)}, bf16[2,8,64,768]{3,2,1,0:T(8,128)(2,1)S(1)}, u32[]{:S(2)}, u32[]{:S(2)}) %collective-permute-start.10) | collective-permute-done | bytes 1572896 | tf_op jit(solution)/shard_map/ppermute | solution.py:549
  83.5 2.2 %collective-permute-done.11.refs_13_ = bf16[2,8,64,768]{3,2,1,0:T(8,128)(2,1)S(1)} collective-permute-done((bf16[2,8,64,768]{3,2,1,0:T(8,128)(2,1)S(1)}, bf16[2,8,64,768]{3,2,1,0:T(8,128)(2,1)S(1)}, u32[]{:S(2)}, u32[]{:S(2)}) %collective-permute-start.11) | collective-permute-done | bytes 1572896 | tf_op jit(solution)/shard_map/ppermute | solution.py:549
  85.8 1.2 %copy-done.6 = bf16[2,8,64,768]{3,2,1,0:T(8,128)(2,1)} copy-done((bf16[2,8,64,768]{3,2,1,0:T(8,128)(2,1)}, bf16[2,8,64,768]{3,2,1,0:T(8,128)(2,1)S(1)}, u32[]{:S(2)}) %copy-start.6) | copy-done | bytes 1572888
  86.9 16.3 %attend_late.1 = bf16[4,512,768]{2,1,0:T(8,128)(2,1)} custom-call(s32[2]{0:T(128)} %pad_add_fusion.place_ref, s32[216]{0:T(256)} %tile_tables.1.table_ref, bf16[4,512,768]{2,1,0:T(8,128)(2,1)} %q_ref.5, f32[2,512,768]{2,1,0:T(8,128)} %get-tuple-element.29.acc_ref, f32[2,512,128]{2,1,0:T(8,128)} %get-tuple-element.33.stat_ref, ...), custom_call_target="tpu_custom_call", output_to_operand_aliasing={{}: (19, {})} | custom-call | flops 2818572288 | bytes 688128 | tf_op jit(solution)/shard_map/attend_late/pallas_call | solution.py:512
  (23 shorter events, 0.0 us)
Async XLA Ops:
  0.0 4.7 %copy-start = (bf16[4,512,768]{2,1,0:T(8,128)(2,1)S(1)}, bf16[4,512,768]{2,1,0:T(8,128)(2,1)}, u32[]{:S(2)}) copy-start(bf16[4,512,768]{2,1,0:T(8,128)(2,1)} %param.9) | copy-start | bytes 9437188
  4.0 5.6 %collective-permute-start = (bf16[4,4,64,768]{3,2,1,0:T(8,128)(2,1)}, bf16[4,4,64,768]{3,2,1,0:T(8,128)(2,1)}, u32[]{:S(2)}, u32[]{:S(2)}) collective-permute-start(bf16[4,4,64,768]{3,2,1,0:T(8,128)(2,1)} %get-tuple-element.44), channel_id=1, source_target_pairs={{0,1},{1,0},{2,3},{3,2},{4,5},{5,4},{6,7},{7,6},{8,9},{9,8},{10,11... | collective-permute-start | bytes 4718600 | tf_op jit(solution)/shard_map/ppermute | solution.py:549
  6.6 3.6 %collective-permute-start.1 = (bf16[4,4,64,768]{3,2,1,0:T(8,128)(2,1)}, bf16[4,4,64,768]{3,2,1,0:T(8,128)(2,1)S(1)}, u32[]{:S(2)}, u32[]{:S(2)}) collective-permute-start(bf16[4,4,64,768]{3,2,1,0:T(8,128)(2,1)} %get-tuple-element.42), channel_id=1, source_target_pairs={{0,1},{1,0},{2,3},{3,2},{4,5},{5,4},{6,7},{7,6},{8,9},{9,8},{10,11... | collective-permute-start | bytes 4718600 | tf_op jit(solution)/shard_map/ppermute | solution.py:549
  6.6 18.5 %collective-permute-start.2 = (bf16[4,4,64,768]{3,2,1,0:T(8,128)(2,1)}, bf16[4,4,64,768]{3,2,1,0:T(8,128)(2,1)S(1)}, u32[]{:S(2)}, u32[]{:S(2)}) collective-permute-start(bf16[4,4,64,768]{3,2,1,0:T(8,128)(2,1)} %get-tuple-element.43), channel_id=1, source_target_pairs={{0,1},{1,0},{2,3},{3,2},{4,5},{5,4},{6,7},{7,6},{8,9},{9,8},{10,11... | collective-permute-start | bytes 4718600 | tf_op jit(solution)/shard_map/ppermute | solution.py:549
  7.1 23.3 %collective-permute-start.3 = (bf16[4,4,64,768]{3,2,1,0:T(8,128)(2,1)}, bf16[4,4,64,768]{3,2,1,0:T(8,128)(2,1)}, u32[]{:S(2)}, u32[]{:S(2)}) collective-permute-start(bf16[4,4,64,768]{3,2,1,0:T(8,128)(2,1)} %get-tuple-element.41), channel_id=1, source_target_pairs={{0,1},{1,0},{2,3},{3,2},{4,5},{5,4},{6,7},{7,6},{8,9},{9,8},{10,11... | collective-permute-start | bytes 4718600 | tf_op jit(solution)/shard_map/ppermute | solution.py:549
  10.2 1.1 %copy-start.1 = (bf16[4,4,64,768]{3,2,1,0:T(8,128)(2,1)}, bf16[4,4,64,768]{3,2,1,0:T(8,128)(2,1)S(1)}, u32[]{:S(2)}) copy-start(bf16[4,4,64,768]{3,2,1,0:T(8,128)(2,1)S(1)} %collective-permute-done.1.v_sent.refs_4_) | copy-start | bytes 4718596
  14.9 34.4 %collective-permute-start.4 = (bf16[2,4,64,768]{3,2,1,0:T(8,128)(2,1)}, bf16[2,4,64,768]{3,2,1,0:T(8,128)(2,1)S(1)}, u32[]{:S(2)}, u32[]{:S(2)}) collective-permute-start(bf16[2,4,64,768]{3,2,1,0:T(8,128)(2,1)} %get-tuple-element.30), channel_id=1, source_target_pairs={{0,4},{4,8},{8,12},{1,5},{5,9},{9,13},{2,6},{6,10},{10,14},{3,7},{... | collective-permute-start | bytes 2359304 | tf_op jit(solution)/shard_map/ppermute | solution.py:545
  18.2 31.2 %collective-permute-start.5 = (bf16[2,4,64,768]{3,2,1,0:T(8,128)(2,1)}, bf16[2,4,64,768]{3,2,1,0:T(8,128)(2,1)S(1)}, u32[]{:S(2)}, u32[]{:S(2)}) collective-permute-start(bf16[2,4,64,768]{3,2,1,0:T(8,128)(2,1)} %get-tuple-element.31), channel_id=1, source_target_pairs={{4,0},{8,4},{12,8},{5,1},{9,5},{13,9},{6,2},{10,6},{14,10},{7,3},{... | collective-permute-start | bytes 2359304 | tf_op jit(solution)/shard_map/ppermute | solution.py:545
  25.1 5.3 %copy-start.2 = (bf16[4,4,64,768]{3,2,1,0:T(8,128)(2,1)}, bf16[4,4,64,768]{3,2,1,0:T(8,128)(2,1)S(1)}, u32[]{:S(2)}) copy-start(bf16[4,4,64,768]{3,2,1,0:T(8,128)(2,1)S(1)} %collective-permute-done.2.refs_2_) | copy-start | bytes 4718596
  25.1 54.9 %collective-permute-start.8 = (bf16[2,8,64,768]{3,2,1,0:T(8,128)(2,1)}, bf16[2,8,64,768]{3,2,1,0:T(8,128)(2,1)S(1)}, u32[]{:S(2)}, u32[]{:S(2)}) collective-permute-start(bf16[2,8,64,768]{3,2,1,0:T(8,128)(2,1)} %get-tuple-element.36), channel_id=1, source_target_pairs={{0,4},{4,8},{8,12},{1,5},{5,9},{9,13},{2,6},{6,10},{10,14},{3,7},{... | collective-permute-start | bytes 4718600 | tf_op jit(solution)/shard_map/ppermute | solution.py:545
  28.3 51.7 %collective-permute-start.9 = (bf16[2,8,64,768]{3,2,1,0:T(8,128)(2,1)}, bf16[2,8,64,768]{3,2,1,0:T(8,128)(2,1)S(1)}, u32[]{:S(2)}, u32[]{:S(2)}) collective-permute-start(bf16[2,8,64,768]{3,2,1,0:T(8,128)(2,1)} %get-tuple-element.37), channel_id=1, source_target_pairs={{4,0},{8,4},{12,8},{5,1},{9,5},{13,9},{6,2},{10,6},{14,10},{7,3},{... | collective-permute-start | bytes 4718600 | tf_op jit(solution)/shard_map/ppermute | solution.py:545
  49.3 4.8 %copy-start.7 = (bf16[2,4,64,768]{3,2,1,0:T(8,128)(2,1)}, bf16[2,4,64,768]{3,2,1,0:T(8,128)(2,1)S(1)}, u32[]{:S(2)}) copy-start(bf16[2,4,64,768]{3,2,1,0:T(8,128)(2,1)S(1)} %collective-permute-done.4.refs_6_) | copy-start | bytes 2359300
  49.3 4.7 %copy-start.8 = (bf16[2,4,64,768]{3,2,1,0:T(8,128)(2,1)}, bf16[2,4,64,768]{3,2,1,0:T(8,128)(2,1)S(1)}, u32[]{:S(2)}) copy-start(bf16[2,4,64,768]{3,2,1,0:T(8,128)(2,1)S(1)} %collective-permute-done.5.refs_7_) | copy-start | bytes 2359300
  49.4 3.6 %collective-permute-start.6 = (bf16[2,4,64,768]{3,2,1,0:T(8,128)(2,1)S(1)}, bf16[2,4,64,768]{3,2,1,0:T(8,128)(2,1)S(1)}, u32[]{:S(2)}, u32[]{:S(2)}) collective-permute-start(bf16[2,4,64,768]{3,2,1,0:T(8,128)(2,1)S(1)} %collective-permute-done.4.refs_6_), channel_id=1, source_target_pairs={{0,1},{1,0},{2,3},{3,2},{4,5},{5,4},{6,7},{7,6},{8,9},{9,8},{10,11... | collective-permute-start | bytes 2359304 | tf_op jit(solution)/shard_map/ppermute | solution.py:549
  51.0 3.0 %collective-permute-start.7 = (bf16[2,4,64,768]{3,2,1,0:T(8,128)(2,1)S(1)}, bf16[2,4,64,768]{3,2,1,0:T(8,128)(2,1)S(1)}, u32[]{:S(2)}, u32[]{:S(2)}) collective-permute-start(bf16[2,4,64,768]{3,2,1,0:T(8,128)(2,1)S(1)} %collective-permute-done.5.refs_7_), channel_id=1, source_target_pairs={{0,1},{1,0},{2,3},{3,2},{4,5},{5,4},{6,7},{7,6},{8,9},{9,8},{10,11... | collective-permute-start | bytes 2359304 | tf_op jit(solution)/shard_map/ppermute | solution.py:549
  52.9 1.1 %copy-start.9 = (bf16[2,4,64,768]{3,2,1,0:T(8,128)(2,1)}, bf16[2,4,64,768]{3,2,1,0:T(8,128)(2,1)S(1)}, u32[]{:S(2)}) copy-start(bf16[2,4,64,768]{3,2,1,0:T(8,128)(2,1)S(1)} %collective-permute-done.6.refs_8_) | copy-start | bytes 2359300
  54.1 0.9 copy-start.10
  80.0 5.8 %copy-start.3 = (bf16[2,8,64,768]{3,2,1,0:T(8,128)(2,1)}, bf16[2,8,64,768]{3,2,1,0:T(8,128)(2,1)S(1)}, u32[]{:S(2)}) copy-start(bf16[2,8,64,768]{3,2,1,0:T(8,128)(2,1)S(1)} %collective-permute-done.8.refs_10_) | copy-start | bytes 4718596
  80.0 5.7 %copy-start.4 = (bf16[2,8,64,768]{3,2,1,0:T(8,128)(2,1)}, bf16[2,8,64,768]{3,2,1,0:T(8,128)(2,1)S(1)}, u32[]{:S(2)}) copy-start(bf16[2,8,64,768]{3,2,1,0:T(8,128)(2,1)S(1)} %collective-permute-done.9.refs_11_) | copy-start | bytes 4718596
  80.0 3.5 %collective-permute-start.10 = (bf16[2,8,64,768]{3,2,1,0:T(8,128)(2,1)S(1)}, bf16[2,8,64,768]{3,2,1,0:T(8,128)(2,1)S(1)}, u32[]{:S(2)}, u32[]{:S(2)}) collective-permute-start(bf16[2,8,64,768]{3,2,1,0:T(8,128)(2,1)S(1)} %collective-permute-done.8.refs_10_), channel_id=1, source_target_pairs={{0,1},{1,0},{2,3},{3,2},{4,5},{5,4},{6,7},{7,6},{8,9},{9,8},{10,11... | collective-permute-start | bytes 4718600 | tf_op jit(solution)/shard_map/ppermute | solution.py:549
  80.5 5.3 %collective-permute-start.11 = (bf16[2,8,64,768]{3,2,1,0:T(8,128)(2,1)S(1)}, bf16[2,8,64,768]{3,2,1,0:T(8,128)(2,1)S(1)}, u32[]{:S(2)}, u32[]{:S(2)}) collective-permute-start(bf16[2,8,64,768]{3,2,1,0:T(8,128)(2,1)S(1)} %collective-permute-done.9.refs_11_), channel_id=1, source_target_pairs={{0,1},{1,0},{2,3},{3,2},{4,5},{5,4},{6,7},{7,6},{8,9},{9,8},{10,11... | collective-permute-start | bytes 4718600 | tf_op jit(solution)/shard_map/ppermute | solution.py:549
  83.5 2.3 %copy-start.5 = (bf16[2,8,64,768]{3,2,1,0:T(8,128)(2,1)}, bf16[2,8,64,768]{3,2,1,0:T(8,128)(2,1)S(1)}, u32[]{:S(2)}) copy-start(bf16[2,8,64,768]{3,2,1,0:T(8,128)(2,1)S(1)} %collective-permute-done.10.refs_12_) | copy-start | bytes 4718596
  85.8 1.2 %copy-start.6 = (bf16[2,8,64,768]{3,2,1,0:T(8,128)(2,1)}, bf16[2,8,64,768]{3,2,1,0:T(8,128)(2,1)S(1)}, u32[]{:S(2)}) copy-start(bf16[2,8,64,768]{3,2,1,0:T(8,128)(2,1)S(1)} %collective-permute-done.11.refs_13_) | copy-start | bytes 4718596

commit v3 on v2

--- a/solution.py
+++ b/solution.py
@@ -20,7 +20,8 @@
 F32 = jnp.float32
 ANY = pl.BlockSpec(memory_space=pl.ANY)
 SMEM = pl.BlockSpec(memory_space=pltpu.SMEM)
-VMEM_LIMIT = 56 * 2**20
+VMEM_LIMIT = 40 * 2**20
+PACK_LIMIT = 16 * 2**20
 
 
 class Layout:
@@ -133,40 +134,45 @@
     )(place, *lists)
 
 
-def pack_kernel(lay, begin, length, place_ref, table_ref, k_own, k_sent, v_own, v_sent, up, down, sems):
+def pack_kernel(lay, jobs, place_ref, table_ref, *refs):
+    sources, outs, sems = refs[: -1 - len(jobs)], refs[-1 - len(jobs) : -1], refs[-1]
     core = place_ref[1]
     waits = []
-    for direction, out in ((0, up), (1, down)):
-        for item in range(length):
-            name = table_ref[direction * lay.places + begin + item]
-            frame = name // lay.tiles
-            tile = name % lay.tiles
-            mine = tile // lay.half == core
-            tile = tile % lay.half
-            for kv, (own, sent) in enumerate(((k_own, k_sent), (v_own, v_sent))):
-                target = out.at[kv, item]
+    for (direction, segments), out in zip(jobs, outs):
+        filled = 0
+        for kv, begin, length in segments:
+            own, other = sources[2 * kv : 2 * kv + 2]
+            for item in range(begin, begin + length):
+                name = table_ref[direction * lay.places + item]
+                frame = name // lay.tiles
+                tile = name % lay.tiles
+                mine = tile // lay.half == core
+                tile = tile % lay.half
                 sem = sems.at[len(waits)]
-                here = pltpu.make_async_copy(own.at[frame, tile, core], target, sem)
-                there = pltpu.make_async_copy(sent.at[frame, tile], target, sem)
+                here = pltpu.make_async_copy(own.at[frame, tile, core], out.at[filled], sem)
+                there = pltpu.make_async_copy(other.at[frame, tile, core], out.at[filled], sem)
                 pl.when(mine)(here.start)
                 pl.when(jnp.logical_not(mine))(there.start)
                 waits.append(here)
+                filled += 1
     for copy in waits:
         copy.wait()
 
 
-def pack_call(lay, begin, length, place, table, sources):
+def pack_call(lay, segment_lists, place, table, sources):
     width = sources[0].shape[-1]
-    shape = jax.ShapeDtypeStruct((2, length, HALF, width), BF)
-    return pl.pallas_call(
-        functools.partial(pack_kernel, lay, begin, length),
-        in_specs=[SMEM] * 2 + [ANY] * 4,
-        out_specs=[pl.BlockSpec(memory_space=pltpu.VMEM)] * 2,
-        out_shape=[shape] * 2,
-        scratch_shapes=[pltpu.SemaphoreType.DMA((4 * length,))],
-        compiler_params=pltpu.CompilerParams(vmem_limit_bytes=VMEM_LIMIT),
+    jobs = [(direction, segments) for segments in segment_lists for direction in (0, 1)]
+    sizes = [sum(n for _, _, n in segments) for _, segments in jobs]
+    outs = pl.pallas_call(
+        functools.partial(pack_kernel, lay, jobs),
+        in_specs=[SMEM] * 2 + [ANY] * len(sources),
+        out_specs=[pl.BlockSpec(memory_space=pltpu.VMEM)] * len(jobs),
+        out_shape=[jax.ShapeDtypeStruct((n, HALF, width), BF) for n in sizes],
+        scratch_shapes=[pltpu.SemaphoreType.DMA((sum(sizes),))],
+        compiler_params=pltpu.CompilerParams(vmem_limit_bytes=PACK_LIMIT),
         name="pack_tiles",
     )(place, table, *sources)
+    return [tuple(outs[i : i + 2]) for i in range(0, len(outs), 2)]
 
 
 def rows_of(buf, index, cols):
@@ -194,11 +200,11 @@
         l_s[head] += mixed[:, HEAD_DIM:]
 
 
-def attend_list(q_ref, kbuf, vbuf, table_ref, base, m_s, l_s, acc_s, heads):
+def attend_list(q_ref, kbuf, vbuf, table_ref, base, m_s, l_s, acc_s, heads, packed=False):
     count = table_ref[base]
 
     def add(start, n):
-        ids = [table_ref[base + 1 + start + j] for j in range(n)]
+        ids = [start + j if packed else table_ref[base + 1 + start + j] for j in range(n)]
         attend_tiles(q_ref, kbuf, vbuf, ids, m_s, l_s, acc_s, heads)
 
     def four(i, _):
@@ -255,42 +261,61 @@
 
 def local_copies(lay, index, core, local, bufs, sems):
     found = []
-    for kv, (buf, (own, sent, kept)) in enumerate(zip(bufs, (local[:3], local[3:]))):
-        mine = pl.ds(index * lay.tiles + core * lay.half, lay.half)
-        others = pl.ds(index * lay.tiles + (1 - core) * lay.half, lay.half)
-        for piece, (source, target) in enumerate(
-            ((own, buf.at[mine]), (sent, buf.at[others, core]), (kept, buf.at[others, 1 - core]))
-        ):
-            found.append(pltpu.make_async_copy(source.at[index], target, sems.at[index, 3 * kv + piece]))
+    for kv, buf in enumerate(bufs):
+        for side, owner in enumerate((core, 1 - core)):
+            target = buf.at[pl.ds(index * lay.tiles + owner * lay.half, lay.half)]
+            source = local[2 * kv + side].at[index]
+            found.append(pltpu.make_async_copy(source, target, sems.at[index, 2 * kv + side]))
     return found
 
 
-def far_copies(core, parts, bufs, begins, sems):
-    found = []
-    for part, begin in zip(parts, begins):
-        length = part[0].shape[1]
-        for side in (0, 1):
-            for direction in (0, 1):
-                for kv in (0, 1):
-                    target = bufs[kv].at[
-                        pl.ds(begin[direction], length), core if side == 0 else 1 - core
-                    ]
-                    source = part[2 * side + direction].at[kv]
+class Received:
+    def __init__(self, lay, core, refs):
+        self.lay = lay
+        self.core = core
+        self.early = (refs[:4], refs[4:8])
+        self.late = refs[8:12]
+
+    def early_copies(self, bufs, sems):
+        found = []
+        for kv, buf in enumerate(bufs):
+            for side, half in enumerate((self.core, 1 - self.core)):
+                for direction in (0, 1):
+                    begin = self.lay.own + direction * self.lay.early
+                    target = buf.at[pl.ds(begin, self.lay.early), half]
+                    source = self.early[kv][2 * side + direction]
                     found.append(pltpu.make_async_copy(source, target, sems.at[len(found)]))
-    return found
-
-
-def exact_frame(lay, heads, frame, core, table_ref, q_ref, local, parts, acc_s, m_s, l_s, tk, tv, sems):
+        return found
+
+    def start(self, item, length, targets, sems):
+        direction = item // length
+        place = item % length
+        for way in (0, 1):
+            for late in (False, True)[: 2 if length > self.lay.early else 1]:
+                here = direction == way
+                if length > self.lay.early:
+                    here = jnp.logical_and(here, (place >= self.lay.early) == late)
+
+                @pl.when(here)
+                def _(way=way, late=late):
+                    for kv, target in enumerate(targets):
+                        for side, half in enumerate((self.core, 1 - self.core)):
+                            ref = self.late if late else self.early[kv]
+                            at = place + (kv * self.lay.late - self.lay.early if late else 0)
+                            source = ref[2 * side + way].at[at]
+                            pltpu.make_async_copy(source, target.at[half], sems.at[2 * kv + side]).start()
+
+    def wait(self, targets, sems):
+        for kv, target in enumerate(targets):
+            for side in (0, 1):
+                source = self.early[0][0].at[0]
+                pltpu.make_async_copy(source, target.at[side], sems.at[2 * kv + side]).wait()
+
+
+def exact_frame(lay, heads, frame, core, table_ref, q_ref, local, received, acc_s, m_s, l_s, tk, tv, sems):
     m_s[...] = jnp.full(m_s.shape, -jnp.inf, F32)
     l_s[...] = jnp.zeros(l_s.shape, F32)
     acc_s[...] = jnp.zeros(acc_s.shape, F32)
-
-    def fetch(*pairs):
-        found = [pltpu.make_async_copy(a, b, sems.at[i]) for i, (a, b) in enumerate(pairs)]
-        for copy in found:
-            copy.start()
-        for copy in found:
-            copy.wait()
 
     def add_tile():
         for head in range(heads):
@@ -309,42 +334,22 @@
         source, tile = name // lay.tiles, name % lay.tiles
         mine = tile // lay.half == core
         tile = tile % lay.half
-        k_own, k_sent, k_kept, v_own, v_sent, v_kept = (ref.at[source, tile] for ref in local)
-
-        @pl.when(mine)
-        def _():
-            fetch((k_own, tk), (v_own, tv))
-
-        @pl.when(jnp.logical_not(mine))
-        def _():
-            fetch(
-                (k_sent, tk.at[core]),
-                (k_kept, tk.at[1 - core]),
-                (v_sent, tv.at[core]),
-                (v_kept, tv.at[1 - core]),
-            )
-
-    def far_tile(direction, part, item):
-        up, other = part[direction], part[2 + direction]
-        fetch(
-            (up.at[0, item], tk.at[core]),
-            (other.at[0, item], tk.at[1 - core]),
-            (up.at[1, item], tv.at[core]),
-            (other.at[1, item], tv.at[1 - core]),
-        )
-
-    def far_places(item, length):
-        begin = 0
-        for part in parts:
-            size = part[0].shape[1]
-            for direction in (0, 1):
-                at = item - direction * length - begin
-
-                @pl.when(jnp.logical_and(at >= 0, at < size))
-                def _(direction=direction, part=part, at=at):
-                    far_tile(direction, part, at)
-
-            begin += size
+        for side in (0, 1):
+
+            @pl.when(mine if side == 0 else jnp.logical_not(mine))
+            def _(side=side):
+                found = [
+                    pltpu.make_async_copy(local[2 * kv + side].at[source, tile], buf, sems.at[kv])
+                    for kv, buf in enumerate((tk, tv))
+                ]
+                for copy in found:
+                    copy.start()
+                for copy in found:
+                    copy.wait()
+
+    def far_tile(item, length):
+        received.start(item, length, (tk, tv), sems)
+        received.wait((tk, tv), sems)
 
     def own_step(i, _):
         near_tile(frame * lay.tiles + i)
@@ -360,71 +365,67 @@
 
         @pl.when(name >= lay.own)
         def _():
-            far_places(name - lay.own, lay.early)
+            far_tile(name - lay.own, lay.early)
 
         add_tile()
         return 0
 
     def far_step(i, _):
-        far_places(table_ref[lay.far + frame * STRIDE + 1 + i], lay.places)
+        far_tile(table_ref[lay.far + frame * STRIDE + 1 + i], lay.places)
         add_tile()
         return 0
 
     lax.fori_loop(0, lay.tiles, own_step, 0)
     lax.fori_loop(0, table_ref[lay.near + frame * STRIDE], near_step, 0)
-    lax.fori_loop(0, table_ref[lay.far + frame * STRIDE], far_step, 0)
+    if received.late:
+        lax.fori_loop(0, table_ref[lay.far + frame * STRIDE], far_step, 0)
 
 
 def near_kernel(lay, heads, whole, place_ref, table_ref, q_ref, *refs):
-    local, refs = refs[:6], refs[6:]
-    parts = ()
+    core = place_ref[1]
+    local, refs = refs[:4], refs[4:]
     if whole:
-        parts, refs = (refs[:4],), refs[4:]
+        received, refs = Received(lay, core, refs[:8]), refs[8:]
         out_ref, acc_s, kbuf, vbuf, m_s, l_s, sems, tk, tv, far_sems = refs
     else:
         acc_out, stat_ref, kbuf, vbuf, m_s, l_s, sems = refs
         acc_s = acc_out.at[0]
-    core = place_ref[1]
     step = pl.program_id(0)
     frame = step + 1 if whole else step * (lay.here - 1)
     begin = 1 if whole else 0
 
-    def copies(index):
-        return local_copies(lay, index, core, local, (kbuf, vbuf), sems)
-
-    def far():
-        return far_copies(core, parts, (kbuf, vbuf), [(lay.own, lay.own + lay.early)] * len(parts), far_sems)
-
-    order = [begin] + [i for i in range(lay.here) if i != begin]
+    def first():
+        return local_copies(lay, begin, core, local, (kbuf, vbuf), sems)
+
+    def others():
+        found = []
+        for index in range(lay.here):
+            if index != begin:
+                found += local_copies(lay, index, core, local, (kbuf, vbuf), sems)
+        return found + (received.early_copies((kbuf, vbuf), far_sems) if whole else [])
 
     @pl.when(step == 0)
     def _():
-        for index in order:
-            for copy in copies(index):
-                copy.start()
-        if whole:
-            for copy in far():
-                copy.start()
-        for copy in copies(begin):
+        for copy in first():
+            copy.start()
+        for copy in first():
             copy.wait()
+        for copy in others():
+            copy.start()
 
     attend_own(lay, q_ref, kbuf, vbuf, frame, m_s, l_s, acc_s, heads)
 
     @pl.when(step == 0)
     def _():
-        for index in order[1:]:
-            for copy in copies(index):
-                copy.wait()
-        if whole:
-            for copy in far():
-                copy.wait()
+        for copy in others():
+            copy.wait()
 
     attend_list(q_ref, kbuf, vbuf, table_ref, lay.near + frame * STRIDE, m_s, l_s, acc_s, heads)
     if whole:
 
         @pl.when(jnp.max(l_s[...]) > LARGE)
         def _():
-            exact_frame(lay, heads, frame, core, table_ref, q_ref, local, parts, acc_s, m_s, l_s, tk, tv, far_sems)
+            exact_frame(lay, heads, frame, core, table_ref, q_ref, local, received, acc_s, m_s, l_s, tk, tv, far_sems)
 
         finish(out_ref, acc_s, l_s, heads)
     else:
@@ -443,7 +444,7 @@
     count = lay.own + (2 * lay.early if whole else 0)
     bufs = [pltpu.VMEM((count, 2, HALF, width), BF)] * 2
     sums = [pltpu.VMEM((heads, rows, 128), F32)] * 2
-    sems = [pltpu.SemaphoreType.DMA((here, 6))]
+    sems = [pltpu.SemaphoreType.DMA((here, 4))]
     if whole:
         out_specs = [block]
         out_shape = [jax.ShapeDtypeStruct((here, rows, width), BF)]
@@ -461,7 +462,7 @@
         grid_spec=pltpu.PrefetchScalarGridSpec(
             num_scalar_prefetch=2,
             grid=(steps,),
-            in_specs=[block] + [ANY] * (6 + len(early)),
+            in_specs=[block] + [ANY] * (4 + len(early)),
             out_specs=out_specs,
             scratch_shapes=scratch,
         ),
@@ -473,34 +474,44 @@
 
 
 def far_kernel(lay, heads, place_ref, table_ref, q_ref, acc_ref, stat_ref, *refs):
-    local, parts = refs[:6], (refs[6:10], refs[10:14])
-    out_ref, kbuf, vbuf, acc_s, m_s, l_s, tk, tv, sems = refs[15:]
+    core = place_ref[1]
+    local, received = refs[:4], Received(lay, core, refs[4:16])
+    out_ref, kbuf, vbuf, acc_s, m_s, l_s, tk, tv, sems, exact_sems = refs[17:]
     step = pl.program_id(0)
     frame = step * (lay.here - 1)
-    core = place_ref[1]
-
-    def copies():
-        begins = [(0, lay.places), (lay.early, lay.places + lay.early)]
-        return far_copies(core, parts, (kbuf, vbuf), begins, sems)
+    room = kbuf.shape[1]
+
+    def bufs(at, i):
+        return kbuf.at[at, i], vbuf.at[at, i]
+
+    def start(at):
+        base = lay.far + at * (lay.here - 1) * STRIDE
+
+        def one(i, _):
+            received.start(table_ref[base + 1 + i], lay.places, bufs(at, i), sems.at[at * room + i])
+            return 0
+
+        lax.fori_loop(0, table_ref[base], one, 0)
 
     @pl.when(step == 0)
     def _():
-        for copy in copies():
-            copy.start()
+        start(0)
+        start(1)
 
     load_stats(stat_ref, m_s, l_s, heads)
     acc_s[...] = acc_ref[0]
-
-    @pl.when(step == 0)
-    def _():
-        for copy in copies():
-            copy.wait()
-
-    attend_list(q_ref, kbuf, vbuf, table_ref, lay.far + frame * STRIDE, m_s, l_s, acc_s, heads)
+    base = lay.far + frame * STRIDE
+
+    def wait(i, _):
+        received.wait(bufs(step, i), sems.at[step * room + i])
+        return 0
+
+    lax.fori_loop(0, table_ref[base], wait, 0)
+    attend_list(q_ref, kbuf.at[step], vbuf.at[step], table_ref, base, m_s, l_s, acc_s, heads, packed=True)
 
     @pl.when(jnp.max(l_s[...]) > LARGE)
     def _():
-        exact_frame(lay, heads, frame, core, table_ref, q_ref, local, parts, acc_s, m_s, l_s, tk, tv, sems)
+        exact_frame(lay, heads, frame, core, table_ref, q_ref, local, received, acc_s, m_s, l_s, tk, tv, exact_sems)
 
     finish(out_ref, acc_s, l_s, heads)
 
@@ -509,6 +520,8 @@
     here, rows, width = queries.shape
     block = pl.BlockSpec((1, rows, width), lambda s, *_: (s * (here - 1), 0, 0))
     anys = [*local, *early, *late, out]
+    room = sum(n for frame, column, _ in lay.remote(0) if frame == 0 for n in [lay.lengths[column]])
+    room += sum(n for frame, column, _ in lay.remote(1) if frame == 0 for n in [lay.lengths[column]])
     return pl.pallas_call(
         functools.partial(far_kernel, lay, heads),
         grid_spec=pltpu.PrefetchScalarGridSpec(
@@ -522,14 +535,15 @@
             + [ANY] * len(anys),
             out_specs=block,
             scratch_shapes=[
-                pltpu.VMEM((2 * lay.places, 2, HALF, width), BF),
-                pltpu.VMEM((2 * lay.places, 2, HALF, width), BF),
+                pltpu.VMEM((2, room, 2, HALF, width), BF),
+                pltpu.VMEM((2, room, 2, HALF, width), BF),
                 pltpu.VMEM((rows, width), F32),
                 pltpu.VMEM((heads, rows, 128), F32),
                 pltpu.VMEM((heads, rows, 128), F32),
                 pltpu.VMEM((2, HALF, width), BF),
                 pltpu.VMEM((2, HALF, width), BF),
-                pltpu.SemaphoreType.DMA((16,)),
+                pltpu.SemaphoreType.DMA((2 * room, 4)),
+                pltpu.SemaphoreType.DMA((4,)),
             ],
         ),
         out_shape=jax.ShapeDtypeStruct((here, rows, width), BF),
@@ -559,31 +573,31 @@
     place = jnp.stack([lax.axis_index("frame") * here, core]).astype(jnp.int32)
 
     k_own, v_own = (a.reshape(here, lay.half, 2, HALF, width) for a in (key_rows, value_rows))
-    k_sent, v_sent = (
-        swapped(lax.dynamic_index_in_dim(a, 1 - core, 2, keepdims=False)) for a in (k_own, v_own)
-    )
+    k_other, v_other = swapped(k_own), swapped(v_own)
     by_frame = [jnp.transpose(a, (1, 2, 0)) for a in lists] + [jnp.transpose(tile_counts, (2, 1, 0))]
     table = make_table(lay, place, by_frame)
-    k_kept, v_kept = (
-        swapped(lax.dynamic_index_in_dim(a, core, 2, keepdims=False)) for a in (k_own, v_own)
-    )
-
-    sources = (k_own, k_sent, v_own, v_sent)
-    early = pack_call(lay, 0, lay.early, place, table, sources)
-    early, then = lax.optimization_barrier((early, table))
-    early = (shifted(early[0], "frame", 1), shifted(early[1], "frame", -1))
-    late = pack_call(lay, lay.early, lay.late, place, then, sources)
-    late, k_kept = lax.optimization_barrier((late, k_kept))
-    late = (shifted(late[0], "frame", 1), shifted(late[1], "frame", -1))
-
-    local = (k_own, k_sent, k_kept, v_own, v_sent, v_kept)
+
+    def both_ways(pair):
+        return shifted(pair[0], "frame", 1), shifted(pair[1], "frame", -1)
+
+    def both_cores(pair):
+        return (*pair, *map(swapped, pair))
+
+    k_other, table = lax.optimization_barrier((k_other, table))
+    (k_early,) = pack_call(lay, [[(0, 0, lay.early)]], place, table, (k_own, k_other))
+    k_early, table = lax.optimization_barrier((k_early, table))
+    k_early = both_ways(k_early)
+    rest = [[(1, 0, lay.early)], [(0, lay.early, lay.late), (1, lay.early, lay.late)]]
+    v_early, late = pack_call(lay, rest, place, table, (k_own, k_other, v_own, v_other))
+    v_early, late = both_ways(v_early), both_ways(late)
+
+    local = (k_own, k_other, v_own, v_other)
     acc, stats = near_call(lay, heads, False, place, table, queries, local)
-    early, stats = lax.optimization_barrier((early, stats))
-    early = (*early, *map(swapped, early))
+    k_early, v_early, stats = lax.optimization_barrier((k_early, v_early, stats))
+    early = (*both_cores(k_early), *both_cores(v_early))
     (out,) = near_call(lay, heads, True, place, table, queries, local, early)
     late, out = lax.optimization_barrier((late, out))
-    late = (*late, *map(swapped, late))
-    return far_call(lay, heads, place, table, queries, acc, stats, local, early, late, out)
+    return far_call(lay, heads, place, table, queries, acc, stats, local, early, both_cores(late), out)
 
 
 def solution(mesh):

time: 105 us -> 110 us (1.048); the launches traced: 103 us -> 110 us
  starting transfers between devices: 14.1 us -> 20.4 us
  waiting for transfers between devices: 8.74 us -> 12.4 us
  local copies, waits for them, and re-layouts: 9.14 us -> 6.31 us
    pallas_call x1, Pallas kernels: 16.3 us -> 23.3 us  [far_call(): pl.pallas_call(functools.partial(far_kernel, lay, heads), grid_spec=pltpu...]
    pallas_call x2, Pallas kernels: 43.9 us -> 37.7 us  [near_call(): pl.pallas_call(functools.partial(near_kernel, lay, heads, whole), grid_sp...]
    squeeze x2 -> x0, local copies, waits for them, and re-layouts: 5.93 us -> none  [per_device(): lax.dynamic_index_in_dim(a, core, 2, keepdims=False)]
    ppermute x4 -> x6, starting transfers between devices: 10.6 us -> 16.1 us  [shifted(): lax.ppermute(block, axis, [(i, i + step) for i in devices if i + step in...]
    ppermute x8, waiting for transfers between devices: 8.73 us -> 12.4 us  [swapped(): return lax.ppermute(block, 'seq', [(0, 1), (1, 0)])]
    unnamed x22, local copies, waits for them, and re-layouts: 3.21 us -> 6.31 us
  transfers between devices with their start and end apart: 12 -> 14, of which waited for: 5 -> 7; matrix products, arithmetic and copies ran while one was open for 2% -> 0% of each run, Pallas kernels for 52% -> 43%
where the time goes in v3:
time: 110 us
  Pallas kernels  70.5 us (64%)
  starting transfers between devices  20.4 us (19%)
  waiting for transfers between devices  12.4 us (11%)
  local copies, waits for them, and re-layouts  6.31 us (6%)
    pallas_call x2, Pallas kernels, near_call(): pl.pallas_call(functools.partial(near_kernel, lay, heads, whole), grid_sp...  37.7 us
    pallas_call x1, Pallas kernels, far_call(): pl.pallas_call(functools.partial(far_kernel, lay, heads), grid_spec=pltpu...  23.3 us
    ppermute x6, starting transfers between devices, shifted(): lax.ppermute(block, axis, [(i, i + step) for i in devices if i + step in...  16.1 us
    ppermute x8, waiting for transfers between devices, swapped(): return lax.ppermute(block, 'seq', [(0, 1), (1, 0)])  12.4 us
    pallas_call x2, Pallas kernels, pack_call(): pl.pallas_call(functools.partial(pack_kernel, lay, jobs), in_specs=[SMEM]...  7.74 us
    unnamed x22, local copies, waits for them, and re-layouts  6.31 us
    ppermute x8, starting transfers between devices, swapped(): return lax.ppermute(block, 'seq', [(0, 1), (1, 0)])  4.21 us
  transfers between devices with their start and end apart: 14, of which 7 were waited for; matrix products, arithmetic and copies ran while one was open for 0% of the time, Pallas kernels for 43%

profile of v3, /device:TPU:19, one launch (start us, length us, event | category | flops | bytes accessed | tf_op | source)
XLA Modules:
  0.0 110.0 jit_solution(12361354293374057118)
XLA Ops:
  0.0 0.7 collective-permute-start
  0.8 0.7 copy-done.7
  1.4 0.7 copy-done.8
  2.1 0.7 copy-done.9
  2.8 0.7 copy-done.10
  3.5 1.8 %tile_tables.1.table_ref = s32[216]{0:T(256)S(1)} custom-call(s32[2]{0:T(128)S(1)} %pad_add_fusion.place_ref, s32[2,4,16]{2,1,0:T(4,128)S(1)} %bitcast.19, s32[2,2,16]{2,1,0:T(2,128)S(1)} %bitcast.21, s32[2,1,16]{2,1,0:T(1,128)S(1)} %bitcast.22, s32[3,2,16]{2,1,0:T(2,128)S(1)} %bitcast.20), custom_call_target="tpu_custom_call" | custom-call | tf_op jit(solution)/shard_map/tile_tables/pallas_call | solution.py:126
  5.3 5.0 %collective-permute-done.refs_1_ = bf16[4,4,2,64,768]{4,3,2,1,0:T(8,128)(2,1)S(1)} collective-permute-done((bf16[4,4,2,64,768]{4,3,2,1,0:T(8,128)(2,1)}, bf16[4,4,2,64,768]{4,3,2,1,0:T(8,128)(2,1)S(1)}, u32[]{:S(2)}, u32[]{:S(2)}) %collective-permute-start) | collective-permute-done | bytes 3145760 | tf_op jit(solution)/shard_map/ppermute | solution.py:563
  10.3 1.9 %copy-done = bf16[4,512,768]{2,1,0:T(8,128)(2,1)S(1)} copy-done((bf16[4,512,768]{2,1,0:T(8,128)(2,1)S(1)}, bf16[4,512,768]{2,1,0:T(8,128)(2,1)}, u32[]{:S(2)}) %copy-start) | copy-done | bytes 3145752
  12.2 1.8 %pack_tiles.2 = (bf16[4,64,768]{2,1,0:T(8,128)(2,1)S(1)}, bf16[4,64,768]{2,1,0:T(8,128)(2,1)S(1)}) custom-call(s32[2]{0:T(128)S(1)} %pad_add_fusion.place_ref, s32[216]{0:T(256)S(1)} %tile_tables.1.table_ref, bf16[4,4,2,64,768]{4,3,2,1,0:T(8,128)(2,1)S(1)} %bitcast.10, bf16[4,4,2,64,768]{4,3,2,1,0:T(8,128)(2,1)S(1)} %collective-permute-done.refs_1_), custom_call_target="tpu_custom_call" | custom-call | tf_op jit(solution)/shard_map/pack_tiles/pallas_call | solution.py:166
  14.1 3.5 %collective-permute-start.2 = (bf16[4,64,768]{2,1,0:T(8,128)(2,1)S(1)}, bf16[4,64,768]{2,1,0:T(8,128)(2,1)S(1)}, u32[]{:S(2)}, u32[]{:S(2)}) collective-permute-start(bf16[4,64,768]{2,1,0:T(8,128)(2,1)S(1)} %get-tuple-element.32), channel_id=1, source_target_pairs={{0,4},{4,8},{8,12},{1,5},{5,9},{9,13},{2,6},{6,10},{10,14},{3,7},{... | collective-permute-start | bytes 1179656 | tf_op jit(solution)/shard_map/ppermute | solution.py:559
  17.5 2.1 %collective-permute-start.3 = (bf16[4,64,768]{2,1,0:T(8,128)(2,1)S(1)}, bf16[4,64,768]{2,1,0:T(8,128)(2,1)S(1)}, u32[]{:S(2)}, u32[]{:S(2)}) collective-permute-start(bf16[4,64,768]{2,1,0:T(8,128)(2,1)S(1)} %get-tuple-element.33), channel_id=1, source_target_pairs={{4,0},{8,4},{12,8},{5,1},{9,5},{13,9},{6,2},{10,6},{14,10},{7,3},{... | collective-permute-start | bytes 1179656 | tf_op jit(solution)/shard_map/ppermute | solution.py:559
  19.6 5.9 %pack_tiles.3 = (bf16[4,64,768]{2,1,0:T(8,128)(2,1)S(1)}, bf16[4,64,768]{2,1,0:T(8,128)(2,1)S(1)}, bf16[16,64,768]{2,1,0:T(8,128)(2,1)S(1)}, bf16[16,64,768]{2,1,0:T(8,128)(2,1)S(1)}) custom-call(s32[2]{0:T(128)S(1)} %pad_add_fusion.place_ref, s32[216]{0:T(256)S(1)} %tile_tables.1.table_ref, bf16[4,4,2,64,768]{4,3,2,1,0:T(8,128)(2,1)S(1)} %bitcast.11, ...), custom_call_target="tpu_custom_call" | custom-call | tf_op jit(solution)/shard_map/pack_tiles/pallas_call | solution.py:166
  25.6 3.4 %collective-permute-start.4 = (bf16[4,64,768]{2,1,0:T(8,128)(2,1)S(1)}, bf16[4,64,768]{2,1,0:T(8,128)(2,1)S(1)}, u32[]{:S(2)}, u32[]{:S(2)}) collective-permute-start(bf16[4,64,768]{2,1,0:T(8,128)(2,1)S(1)} %get-tuple-element.34), channel_id=1, source_target_pairs={{0,4},{4,8},{8,12},{1,5},{5,9},{9,13},{2,6},{6,10},{10,14},{3,7},{... | collective-permute-start | bytes 1179656 | tf_op jit(solution)/shard_map/ppermute | solution.py:559
  28.9 1.9 %collective-permute-start.5 = (bf16[4,64,768]{2,1,0:T(8,128)(2,1)S(1)}, bf16[4,64,768]{2,1,0:T(8,128)(2,1)S(1)}, u32[]{:S(2)}, u32[]{:S(2)}) collective-permute-start(bf16[4,64,768]{2,1,0:T(8,128)(2,1)S(1)} %get-tuple-element.35), channel_id=1, source_target_pairs={{4,0},{8,4},{12,8},{5,1},{9,5},{13,9},{6,2},{10,6},{14,10},{7,3},{... | collective-permute-start | bytes 1179656 | tf_op jit(solution)/shard_map/ppermute | solution.py:559
  30.9 3.4 %collective-permute-start.10 = (bf16[16,64,768]{2,1,0:T(8,128)(2,1)S(1)}, bf16[16,64,768]{2,1,0:T(8,128)(2,1)S(1)}, u32[]{:S(2)}, u32[]{:S(2)}) collective-permute-start(bf16[16,64,768]{2,1,0:T(8,128)(2,1)S(1)} %get-tuple-element.42), channel_id=1, source_target_pairs={{0,4},{4,8},{8,12},{1,5},{5,9},{9,13},{2,6},{6,10},{10,14},{3,7},{... | collective-permute-start | bytes 4718600 | tf_op jit(solution)/shard_map/ppermute | solution.py:559
  34.3 1.9 %collective-permute-start.11 = (bf16[16,64,768]{2,1,0:T(8,128)(2,1)S(1)}, bf16[16,64,768]{2,1,0:T(8,128)(2,1)S(1)}, u32[]{:S(2)}, u32[]{:S(2)}) collective-permute-start(bf16[16,64,768]{2,1,0:T(8,128)(2,1)S(1)} %get-tuple-element.43), channel_id=1, source_target_pairs={{4,0},{8,4},{12,8},{5,1},{9,5},{13,9},{6,2},{10,6},{14,10},{7,3},{... | collective-permute-start | bytes 4718600 | tf_op jit(solution)/shard_map/ppermute | solution.py:559
  36.2 14.5 %attend_edges.1 = (f32[2,512,768]{2,1,0:T(8,128)S(1)}, f32[2,512,128]{2,1,0:T(8,128)S(1)}) custom-call(s32[2]{0:T(128)S(1)} %pad_add_fusion.place_ref, s32[216]{0:T(256)S(1)} %tile_tables.1.table_ref, bf16[4,512,768]{2,1,0:T(8,128)(2,1)S(1)} %copy-done.4, bf16[4,4,2,64,768]{4,3,2,1,0:T(8,128)(2,1)S(1)} %bitcast.12, ...), custom_call_target="tpu_custom_call" | custom-call | flops 6442450944 | bytes 1572864 | tf_op jit(solution)/shard_map/attend_edges/pallas_call | solution.py:460
  50.7 1.7 %copy-done.6 = f32[2,512,768]{2,1,0:T(8,128)} copy-done((f32[2,512,768]{2,1,0:T(8,128)}, f32[2,512,768]{2,1,0:T(8,128)S(1)}, u32[]{:S(2)}) %copy-start.6) | copy-done | bytes 3145752
  52.4 2.1 %collective-permute-start.6 = (bf16[4,64,768]{2,1,0:T(8,128)(2,1)S(1)}, bf16[4,64,768]{2,1,0:T(8,128)(2,1)S(1)}, u32[]{:S(2)}, u32[]{:S(2)}) collective-permute-start(bf16[4,64,768]{2,1,0:T(8,128)(2,1)S(1)} %collective-permute-done.2.refs_4_), channel_id=1, source_target_pairs={{0,1},{1,0},{2,3},{3,2},{4,5},{5,4},{6,7},{7,6},{8,9},{9,8},{10,11... | collective-permute-start | bytes 1179656 | tf_op jit(solution)/shard_map/ppermute | solution.py:563
  54.5 0.1 collective-permute-start.7
  54.6 0.4 collective-permute-start.8
  55.0 0.8 collective-permute-done.6.refs_6_
  55.8 0.4 collective-permute-start.9
  56.2 0.2 collective-permute-done.7.refs_7_
  56.4 0.6 collective-permute-done.8.refs_10_
  57.0 0.6 collective-permute-done.9.refs_11_
  57.6 23.2 %attend_middle.1.refs_16_ = bf16[4,512,768]{2,1,0:T(8,128)(2,1)} custom-call(s32[2]{0:T(128)S(1)} %pad_add_fusion.place_ref, s32[216]{0:T(256)S(1)} %tile_tables.1.table_ref, bf16[4,512,768]{2,1,0:T(8,128)(2,1)S(1)} %copy-done.4, bf16[4,4,2,64,768]{4,3,2,1,0:T(8,128)(2,1)S(1)} %bitcast.13, bf16[4,4,2,64,768]{4,3,2,1,0:T(8,128)(2,1)S(1)} %collective-permute-done.refs_1_, ...), custom_call_target="tpu_custom_call" | custom-call | flops 6442450944 | bytes 1572864 | tf_op jit(solution)/shard_map/attend_middle/pallas_call | solution.py:460
  80.8 0.4 collective-permute-start.12
  81.2 0.1 collective-permute-start.13
  81.4 2.9 %collective-permute-done.12.refs_14_ = bf16[16,64,768]{2,1,0:T(8,128)(2,1)S(1)} collective-permute-done((bf16[16,64,768]{2,1,0:T(8,128)(2,1)S(1)}, bf16[16,64,768]{2,1,0:T(8,128)(2,1)S(1)}, u32[]{:S(2)}, u32[]{:S(2)}) %collective-permute-start.12) | collective-permute-done | bytes 1572896 | tf_op jit(solution)/shard_map/ppermute | solution.py:563
  84.3 2.2 %collective-permute-done.13.refs_15_ = bf16[16,64,768]{2,1,0:T(8,128)(2,1)S(1)} collective-permute-done((bf16[16,64,768]{2,1,0:T(8,128)(2,1)S(1)}, bf16[16,64,768]{2,1,0:T(8,128)(2,1)S(1)}, u32[]{:S(2)}, u32[]{:S(2)}) %collective-permute-start.13) | collective-permute-done | bytes 1572896 | tf_op jit(solution)/shard_map/ppermute | solution.py:563
  86.5 23.3 %attend_late.1 = bf16[4,512,768]{2,1,0:T(8,128)(2,1)} custom-call(s32[2]{0:T(128)S(1)} %pad_add_fusion.place_ref, s32[216]{0:T(256)S(1)} %tile_tables.1.table_ref, bf16[4,512,768]{2,1,0:T(8,128)(2,1)S(1)} %copy-done.5, f32[2,512,768]{2,1,0:T(8,128)} %copy-done.6, f32[2,512,128]{2,1,0:T(8,128)S(1)} %get-tuple-element.37.stat_ref, ...), custom_call_target="tpu_custom_call", output_to_operand_aliasing={{}: (21, {})} | custom-call | flops 2818572288 | bytes 688128 | tf_op jit(solution)/shard_map/attend_late/pallas_call | solution.py:525
  (25 shorter events, 0.1 us)
Async XLA Ops:
  0.0 10.3 %collective-permute-start = (bf16[4,4,2,64,768]{4,3,2,1,0:T(8,128)(2,1)}, bf16[4,4,2,64,768]{4,3,2,1,0:T(8,128)(2,1)S(1)}, u32[]{:S(2)}, u32[]{:S(2)}) collective-permute-start(bf16[4,4,2,64,768]{4,3,2,1,0:T(8,128)(2,1)} %bitcast.8), channel_id=1, source_target_pairs={{0,1},{1,0},{2,3},{3,2},{4,5},{5,4},{6,7},{7,6},{8,9},{9,8},{10,11... | collective-permute-start | bytes 9437192 | tf_op jit(solution)/shard_map/ppermute | solution.py:563
  0.7 19.0 %collective-permute-start.1 = (bf16[4,4,2,64,768]{4,3,2,1,0:T(8,128)(2,1)}, bf16[4,4,2,64,768]{4,3,2,1,0:T(8,128)(2,1)}, u32[]{:S(2)}, u32[]{:S(2)}) collective-permute-start(bf16[4,4,2,64,768]{4,3,2,1,0:T(8,128)(2,1)} %bitcast.14), channel_id=1, source_target_pairs={{0,1},{1,0},{2,3},{3,2},{4,5},{5,4},{6,7},{7,6},{8,9},{9,8},{10,11... | collective-permute-start | bytes 9437192 | tf_op jit(solution)/shard_map/ppermute | solution.py:563
  0.8 0.7 copy-start.7
  1.4 0.7 copy-start.8
  2.1 0.7 copy-start.9
  2.8 0.7 copy-start.10
  10.3 1.9 %copy-start = (bf16[4,512,768]{2,1,0:T(8,128)(2,1)S(1)}, bf16[4,512,768]{2,1,0:T(8,128)(2,1)}, u32[]{:S(2)}) copy-start(bf16[4,512,768]{2,1,0:T(8,128)(2,1)} %param.8) | copy-start | bytes 9437188
  12.2 45.4 %copy-start.2 = (bf16[4,4,2,64,768]{4,3,2,1,0:T(8,128)(2,1)}, bf16[4,4,2,64,768]{4,3,2,1,0:T(8,128)(2,1)S(1)}, u32[]{:S(2)}) copy-start(bf16[4,4,2,64,768]{4,3,2,1,0:T(8,128)(2,1)S(1)} %collective-permute-done.refs_1_) | copy-start | bytes 9437188
  12.2 7.4 %copy-start.3 = (bf16[4,512,768]{2,1,0:T(8,128)(2,1)S(1)}, bf16[4,512,768]{2,1,0:T(8,128)(2,1)}, u32[]{:S(2)}) copy-start(bf16[4,512,768]{2,1,0:T(8,128)(2,1)} %param.9) | copy-start | bytes 9437188
  14.0 22.2 %copy-start.1 = (bf16[4,512,768]{2,1,0:T(8,128)(2,1)S(1)}, bf16[4,512,768]{2,1,0:T(8,128)(2,1)}, u32[]{:S(2)}) copy-start(bf16[4,512,768]{2,1,0:T(8,128)(2,1)} %param.8) | copy-start | bytes 9437188
  14.1 22.2 %copy-start.4 = (bf16[4,512,768]{2,1,0:T(8,128)(2,1)S(1)}, bf16[4,512,768]{2,1,0:T(8,128)(2,1)}, u32[]{:S(2)}) copy-start(bf16[4,512,768]{2,1,0:T(8,128)(2,1)} %q_ref.5) | copy-start | bytes 9437188
  14.1 20.2 %collective-permute-start.2 = (bf16[4,64,768]{2,1,0:T(8,128)(2,1)S(1)}, bf16[4,64,768]{2,1,0:T(8,128)(2,1)S(1)}, u32[]{:S(2)}, u32[]{:S(2)}) collective-permute-start(bf16[4,64,768]{2,1,0:T(8,128)(2,1)S(1)} %get-tuple-element.32), channel_id=1, source_target_pairs={{0,4},{4,8},{8,12},{1,5},{5,9},{9,13},{2,6},{6,10},{10,14},{3,7},{... | collective-permute-start | bytes 1179656 | tf_op jit(solution)/shard_map/ppermute | solution.py:559
  17.5 34.9 %collective-permute-start.3 = (bf16[4,64,768]{2,1,0:T(8,128)(2,1)S(1)}, bf16[4,64,768]{2,1,0:T(8,128)(2,1)S(1)}, u32[]{:S(2)}, u32[]{:S(2)}) collective-permute-start(bf16[4,64,768]{2,1,0:T(8,128)(2,1)S(1)} %get-tuple-element.33), channel_id=1, source_target_pairs={{4,0},{8,4},{12,8},{5,1},{9,5},{13,9},{6,2},{10,6},{14,10},{7,3},{... | collective-permute-start | bytes 1179656 | tf_op jit(solution)/shard_map/ppermute | solution.py:559
  25.6 26.9 %collective-permute-start.4 = (bf16[4,64,768]{2,1,0:T(8,128)(2,1)S(1)}, bf16[4,64,768]{2,1,0:T(8,128)(2,1)S(1)}, u32[]{:S(2)}, u32[]{:S(2)}) collective-permute-start(bf16[4,64,768]{2,1,0:T(8,128)(2,1)S(1)} %get-tuple-element.34), channel_id=1, source_target_pairs={{0,4},{4,8},{8,12},{1,5},{5,9},{9,13},{2,6},{6,10},{10,14},{3,7},{... | collective-permute-start | bytes 1179656 | tf_op jit(solution)/shard_map/ppermute | solution.py:559
  28.9 23.5 %collective-permute-start.5 = (bf16[4,64,768]{2,1,0:T(8,128)(2,1)S(1)}, bf16[4,64,768]{2,1,0:T(8,128)(2,1)S(1)}, u32[]{:S(2)}, u32[]{:S(2)}) collective-permute-start(bf16[4,64,768]{2,1,0:T(8,128)(2,1)S(1)} %get-tuple-element.35), channel_id=1, source_target_pairs={{4,0},{8,4},{12,8},{5,1},{9,5},{13,9},{6,2},{10,6},{14,10},{7,3},{... | collective-permute-start | bytes 1179656 | tf_op jit(solution)/shard_map/ppermute | solution.py:559
  30.9 49.9 %collective-permute-start.10 = (bf16[16,64,768]{2,1,0:T(8,128)(2,1)S(1)}, bf16[16,64,768]{2,1,0:T(8,128)(2,1)S(1)}, u32[]{:S(2)}, u32[]{:S(2)}) collective-permute-start(bf16[16,64,768]{2,1,0:T(8,128)(2,1)S(1)} %get-tuple-element.42), channel_id=1, source_target_pairs={{0,4},{4,8},{8,12},{1,5},{5,9},{9,13},{2,6},{6,10},{10,14},{3,7},{... | collective-permute-start | bytes 4718600 | tf_op jit(solution)/shard_map/ppermute | solution.py:559
  34.3 46.5 %collective-permute-start.11 = (bf16[16,64,768]{2,1,0:T(8,128)(2,1)S(1)}, bf16[16,64,768]{2,1,0:T(8,128)(2,1)S(1)}, u32[]{:S(2)}, u32[]{:S(2)}) collective-permute-start(bf16[16,64,768]{2,1,0:T(8,128)(2,1)S(1)} %get-tuple-element.43), channel_id=1, source_target_pairs={{4,0},{8,4},{12,8},{5,1},{9,5},{13,9},{6,2},{10,6},{14,10},{7,3},{... | collective-permute-start | bytes 4718600 | tf_op jit(solution)/shard_map/ppermute | solution.py:559
  50.7 1.7 %copy-start.6 = (f32[2,512,768]{2,1,0:T(8,128)}, f32[2,512,768]{2,1,0:T(8,128)S(1)}, u32[]{:S(2)}) copy-start(f32[2,512,768]{2,1,0:T(8,128)S(1)} %get-tuple-element.31.acc_ref) | copy-start | bytes 9437188
  52.4 34.1 %copy-start.5 = (bf16[4,512,768]{2,1,0:T(8,128)(2,1)S(1)}, bf16[4,512,768]{2,1,0:T(8,128)(2,1)}, u32[]{:S(2)}) copy-start(bf16[4,512,768]{2,1,0:T(8,128)(2,1)} %q_ref.5) | copy-start | bytes 9437188
  52.4 3.4 %collective-permute-start.6 = (bf16[4,64,768]{2,1,0:T(8,128)(2,1)S(1)}, bf16[4,64,768]{2,1,0:T(8,128)(2,1)S(1)}, u32[]{:S(2)}, u32[]{:S(2)}) collective-permute-start(bf16[4,64,768]{2,1,0:T(8,128)(2,1)S(1)} %collective-permute-done.2.refs_4_), channel_id=1, source_target_pairs={{0,1},{1,0},{2,3},{3,2},{4,5},{5,4},{6,7},{7,6},{8,9},{9,8},{10,11... | collective-permute-start | bytes 1179656 | tf_op jit(solution)/shard_map/ppermute | solution.py:563
  54.5 1.9 %collective-permute-start.7 = (bf16[4,64,768]{2,1,0:T(8,128)(2,1)S(1)}, bf16[4,64,768]{2,1,0:T(8,128)(2,1)S(1)}, u32[]{:S(2)}, u32[]{:S(2)}) collective-permute-start(bf16[4,64,768]{2,1,0:T(8,128)(2,1)S(1)} %collective-permute-done.3.refs_5_), channel_id=1, source_target_pairs={{0,1},{1,0},{2,3},{3,2},{4,5},{5,4},{6,7},{7,6},{8,9},{9,8},{10,11... | collective-permute-start | bytes 1179656 | tf_op jit(solution)/shard_map/ppermute | solution.py:563
  54.6 2.4 %collective-permute-start.8 = (bf16[4,64,768]{2,1,0:T(8,128)(2,1)S(1)}, bf16[4,64,768]{2,1,0:T(8,128)(2,1)S(1)}, u32[]{:S(2)}, u32[]{:S(2)}) collective-permute-start(bf16[4,64,768]{2,1,0:T(8,128)(2,1)S(1)} %collective-permute-done.4.refs_8_), channel_id=1, source_target_pairs={{0,1},{1,0},{2,3},{3,2},{4,5},{5,4},{6,7},{7,6},{8,9},{9,8},{10,11... | collective-permute-start | bytes 1179656 | tf_op jit(solution)/shard_map/ppermute | solution.py:563
  55.8 1.7 %collective-permute-start.9 = (bf16[4,64,768]{2,1,0:T(8,128)(2,1)S(1)}, bf16[4,64,768]{2,1,0:T(8,128)(2,1)S(1)}, u32[]{:S(2)}, u32[]{:S(2)}) collective-permute-start(bf16[4,64,768]{2,1,0:T(8,128)(2,1)S(1)} %collective-permute-done.5.refs_9_), channel_id=1, source_target_pairs={{0,1},{1,0},{2,3},{3,2},{4,5},{5,4},{6,7},{7,6},{8,9},{9,8},{10,11... | collective-permute-start | bytes 1179656 | tf_op jit(solution)/shard_map/ppermute | solution.py:563
  80.8 3.5 %collective-permute-start.12 = (bf16[16,64,768]{2,1,0:T(8,128)(2,1)S(1)}, bf16[16,64,768]{2,1,0:T(8,128)(2,1)S(1)}, u32[]{:S(2)}, u32[]{:S(2)}) collective-permute-start(bf16[16,64,768]{2,1,0:T(8,128)(2,1)S(1)} %collective-permute-done.10.refs_12_), channel_id=1, source_target_pairs={{0,1},{1,0},{2,3},{3,2},{4,5},{5,4},{6,7},{7,6},{8,9},{9,8},{10,11... | collective-permute-start | bytes 4718600 | tf_op jit(solution)/shard_map/ppermute | solution.py:563
  81.2 5.3 %collective-permute-start.13 = (bf16[16,64,768]{2,1,0:T(8,128)(2,1)S(1)}, bf16[16,64,768]{2,1,0:T(8,128)(2,1)S(1)}, u32[]{:S(2)}, u32[]{:S(2)}) collective-permute-start(bf16[16,64,768]{2,1,0:T(8,128)(2,1)S(1)} %collective-permute-done.11.refs_13_), channel_id=1, source_target_pairs={{0,1},{1,0},{2,3},{3,2},{4,5},{5,4},{6,7},{7,6},{8,9},{9,8},{10,11... | collective-permute-start | bytes 4718600 | tf_op jit(solution)/shard_map/ppermute | solution.py:563

commit v4 on v3

--- a/solution.py
+++ b/solution.py
@@ -20,7 +20,7 @@
 F32 = jnp.float32
 ANY = pl.BlockSpec(memory_space=pl.ANY)
 SMEM = pl.BlockSpec(memory_space=pltpu.SMEM)
-VMEM_LIMIT = 40 * 2**20
+VMEM_LIMIT = 48 * 2**20
 PACK_LIMIT = 16 * 2**20
 
 
@@ -39,6 +39,8 @@
             else:
                 self.early += lengths[column]
         self.places = self.early + self.late
+        self.second = max(self.late // 2 - 1, 1)
+        self.third = self.late - self.second
         self.near = 2 * self.places
         self.far = self.near + frames_here * STRIDE
         self.size = self.far + frames_here * STRIDE
@@ -61,6 +63,7 @@
 def table_kernel(lay, place_ref, one_ref, two_ref, four_ref, count_ref, table_ref, seen_ref):
     lists = (one_ref, two_ref, four_ref)
     first = place_ref[0]
+    odd = first // lay.here % 2
 
     def distinct(target, direction, on_slot, on_new):
         for i in range(lay.own):
@@ -91,21 +94,23 @@
     for direction in (0, 1):
         target = first + (lay.here if direction == 0 else -lay.here)
         target = jnp.clip(target, 0, lay.frames - lay.here)
+        begin = (odd + direction) % 2 * lay.places
         for place in range(lay.places):
-            table_ref[direction * lay.places + place] = 0
-
-        def note(used, name, direction=direction):
-            table_ref[direction * lay.places + jnp.minimum(used, lay.places - 1)] = name
+            table_ref[begin + place] = 0
+
+        def note(used, name, begin=begin):
+            table_ref[begin + jnp.minimum(used, lay.places - 1)] = name
 
         distinct(target, direction, lambda *_: None, note)
 
     for direction in (0, 1):
-
-        def on_slot(frame, place, alive, direction=direction):
+        way = (odd + 1 - direction) % 2
+
+        def on_slot(frame, place, alive, way=way):
             if lay.edge(frame):
-                append(lay.far, frame, direction * lay.places + place, alive)
+                append(lay.far, frame, way * lay.places + place, alive)
             else:
-                append(lay.near, frame, lay.own + direction * lay.early + place, alive)
+                append(lay.near, frame, lay.own + way * lay.early + place, alive)
 
         distinct(first, direction, on_slot, lambda *_: None)
         for frame in range(lay.here):
@@ -138,12 +143,12 @@
     sources, outs, sems = refs[: -1 - len(jobs)], refs[-1 - len(jobs) : -1], refs[-1]
     core = place_ref[1]
     waits = []
-    for (direction, segments), out in zip(jobs, outs):
+    for (way, segments), out in zip(jobs, outs):
         filled = 0
         for kv, begin, length in segments:
             own, other = sources[2 * kv : 2 * kv + 2]
             for item in range(begin, begin + length):
-                name = table_ref[direction * lay.places + item]
+                name = table_ref[way * lay.places + item]
                 frame = name // lay.tiles
                 tile = name % lay.tiles
                 mine = tile // lay.half == core
@@ -161,7 +166,7 @@
 
 def pack_call(lay, segment_lists, place, table, sources):
     width = sources[0].shape[-1]
-    jobs = [(direction, segments) for segments in segment_lists for direction in (0, 1)]
+    jobs = [(way, segments) for segments in segment_lists for way in (0, 1)]
     sizes = [sum(n for _, _, n in segments) for _, segments in jobs]
     outs = pl.pallas_call(
         functools.partial(pack_kernel, lay, jobs),
@@ -171,7 +176,7 @@
         scratch_shapes=[pltpu.SemaphoreType.DMA((sum(sizes),))],
         compiler_params=pltpu.CompilerParams(vmem_limit_bytes=PACK_LIMIT),
         name="pack_tiles",
-    )(place, table, *sources)
+    )(place, table, *in_hbm(sources))
     return [tuple(outs[i : i + 2]) for i in range(0, len(outs), 2)]
 
 
@@ -273,42 +278,41 @@
     def __init__(self, lay, core, refs):
         self.lay = lay
         self.core = core
-        self.early = (refs[:4], refs[4:8])
-        self.late = refs[8:12]
+        self.parts = [refs[i : i + 4] for i in range(0, len(refs), 4)]
+        first, second = lay.early, lay.second
+        self.ranges = [(0, first, (0, 0), (1, 0))]
+        if len(self.parts) > 2:
+            self.ranges.append((first, second, (1, first), (1, first + second)))
+            self.ranges.append((first + second, lay.third, (2, 0), (2, lay.third)))
 
     def early_copies(self, bufs, sems):
         found = []
-        for kv, buf in enumerate(bufs):
+        for buf, part in zip(bufs, self.parts):
             for side, half in enumerate((self.core, 1 - self.core)):
-                for direction in (0, 1):
-                    begin = self.lay.own + direction * self.lay.early
+                for way in (0, 1):
+                    begin = self.lay.own + way * self.lay.early
                     target = buf.at[pl.ds(begin, self.lay.early), half]
-                    source = self.early[kv][2 * side + direction]
+                    source = part[2 * side + way].at[pl.ds(0, self.lay.early)]
                     found.append(pltpu.make_async_copy(source, target, sems.at[len(found)]))
         return found
 
     def start(self, item, length, targets, sems):
-        direction = item // length
         place = item % length
         for way in (0, 1):
-            for late in (False, True)[: 2 if length > self.lay.early else 1]:
-                here = direction == way
-                if length > self.lay.early:
-                    here = jnp.logical_and(here, (place >= self.lay.early) == late)
-
-                @pl.when(here)
-                def _(way=way, late=late):
-                    for kv, target in enumerate(targets):
+            for begin, size, *rows in self.ranges:
+                inside = jnp.logical_and(place >= begin, place < begin + size)
+
+                @pl.when(jnp.logical_and(item // length == way, inside))
+                def _(way=way, begin=begin, rows=rows):
+                    for kv, (target, (part, row)) in enumerate(zip(targets, rows)):
                         for side, half in enumerate((self.core, 1 - self.core)):
-                            ref = self.late if late else self.early[kv]
-                            at = place + (kv * self.lay.late - self.lay.early if late else 0)
-                            source = ref[2 * side + way].at[at]
+                            source = self.parts[part][2 * side + way].at[place - begin + row]
                             pltpu.make_async_copy(source, target.at[half], sems.at[2 * kv + side]).start()
 
     def wait(self, targets, sems):
         for kv, target in enumerate(targets):
             for side in (0, 1):
-                source = self.early[0][0].at[0]
+                source = self.parts[0][0].at[0]
                 pltpu.make_async_copy(source, target.at[side], sems.at[2 * kv + side]).wait()
 
 
@@ -377,7 +381,7 @@
 
     lax.fori_loop(0, lay.tiles, own_step, 0)
     lax.fori_loop(0, table_ref[lay.near + frame * STRIDE], near_step, 0)
-    if received.late:
+    if len(received.parts) > 2:
         lax.fori_loop(0, table_ref[lay.far + frame * STRIDE], far_step, 0)
 
 
@@ -468,9 +472,9 @@
         ),
         out_shape=out_shape,
         compiler_params=pltpu.CompilerParams(vmem_limit_bytes=VMEM_LIMIT),
-        cost_estimate=cost(steps * rows * heads * 16 * TILE),
+        cost_estimate=cost(steps * rows * heads * (TILE if whole else 16 * TILE)),
         name="attend_middle" if whole else "attend_edges",
-    )(place, table, queries, *local, *early)
+    )(place, table, queries, *in_hbm((*local, *early)))
 
 
 def far_kernel(lay, heads, place_ref, table_ref, q_ref, acc_ref, stat_ref, *refs):
@@ -551,12 +555,16 @@
         compiler_params=pltpu.CompilerParams(vmem_limit_bytes=VMEM_LIMIT),
         cost_estimate=cost(2 * rows * heads * 7 * TILE),
         name="attend_late",
-    )(place, table, queries, acc, stats, *anys)
-
-
-def shifted(block, axis, step):
-    devices = range(lax.axis_size(axis))
-    return lax.ppermute(block, axis, [(i, i + step) for i in devices if i + step in devices])
+    )(place, table, queries, acc, stats, *in_hbm(anys[:-1]), out)
+
+
+def in_hbm(arrays):
+    return [pltpu.with_memory_space_constraint(a, pltpu.HBM) for a in arrays]
+
+
+def paired(block, way):
+    pairs = range(way, lax.axis_size("frame") - 1, 2)
+    return lax.ppermute(block, "frame", [p for i in pairs for p in ((i, i + 1), (i + 1, i))])
 
 
 def swapped(block):
@@ -573,31 +581,37 @@
     place = jnp.stack([lax.axis_index("frame") * here, core]).astype(jnp.int32)
 
     k_own, v_own = (a.reshape(here, lay.half, 2, HALF, width) for a in (key_rows, value_rows))
-    k_other, v_other = swapped(k_own), swapped(v_own)
+    k_other = swapped(k_own)
     by_frame = [jnp.transpose(a, (1, 2, 0)) for a in lists] + [jnp.transpose(tile_counts, (2, 1, 0))]
     table = make_table(lay, place, by_frame)
 
     def both_ways(pair):
-        return shifted(pair[0], "frame", 1), shifted(pair[1], "frame", -1)
+        return paired(pair[0], 0), paired(pair[1], 1)
 
     def both_cores(pair):
         return (*pair, *map(swapped, pair))
 
-    k_other, table = lax.optimization_barrier((k_other, table))
-    (k_early,) = pack_call(lay, [[(0, 0, lay.early)]], place, table, (k_own, k_other))
-    k_early, table = lax.optimization_barrier((k_early, table))
-    k_early = both_ways(k_early)
-    rest = [[(1, 0, lay.early)], [(0, lay.early, lay.late), (1, lay.early, lay.late)]]
-    v_early, late = pack_call(lay, rest, place, table, (k_own, k_other, v_own, v_other))
-    v_early, late = both_ways(v_early), both_ways(late)
+    k_other, v_own, table = lax.optimization_barrier((k_other, v_own, table))
+    v_other = swapped(v_own)
+    (first,) = pack_call(lay, [[(0, 0, lay.early)]], place, table, (k_own, k_other))
+    first, table = lax.optimization_barrier((first, table))
+    first = both_ways(first)
+    at = lay.early + lay.second
+    rest = [
+        [(1, 0, lay.early), (0, lay.early, lay.second), (1, lay.early, lay.second)],
+        [(0, at, lay.third), (1, at, lay.third)],
+    ]
+    second, third = pack_call(lay, rest, place, table, (k_own, k_other, v_own, v_other))
+    second, third = both_ways(second), both_ways(third)
 
     local = (k_own, k_other, v_own, v_other)
+    first, table = lax.optimization_barrier((first, table))
     acc, stats = near_call(lay, heads, False, place, table, queries, local)
-    k_early, v_early, stats = lax.optimization_barrier((k_early, v_early, stats))
-    early = (*both_cores(k_early), *both_cores(v_early))
+    second, stats = lax.optimization_barrier((second, stats))
+    early = (*both_cores(first), *both_cores(second))
     (out,) = near_call(lay, heads, True, place, table, queries, local, early)
-    late, out = lax.optimization_barrier((late, out))
-    return far_call(lay, heads, place, table, queries, acc, stats, local, early, both_cores(late), out)
+    third, out = lax.optimization_barrier((third, out))
+    return far_call(lay, heads, place, table, queries, acc, stats, local, early, both_cores(third), out)
 
 
 def solution(mesh):

time: 110 us -> 101 us (0.918)
  the two profiles are of different devices: /device:TPU:19 before, /device:TPU:11 now
where the time goes in v4:
time: 101 us
  Pallas kernels  63.6 us (63%)
  starting transfers between devices  14.9 us (15%)
  waiting for transfers between devices  13.4 us (13%)
  local copies, waits for them, and re-layouts  8.72 us (9%)
    pallas_call x2, Pallas kernels, near_call(): pl.pallas_call(functools.partial(near_kernel, lay, heads, whole), grid_sp...  40.2 us
    pallas_call x1, Pallas kernels, far_call(): pl.pallas_call(functools.partial(far_kernel, lay, heads), grid_spec=pltpu...  16.5 us
    ppermute x6, starting transfers between devices, paired(): lax.ppermute(block, 'frame', [p for i in pairs for p in ((i, i + 1), (i +...  10.2 us
    unnamed x40, local copies, waits for them, and re-layouts  8.72 us
    ppermute x8, waiting for transfers between devices, swapped(): return lax.ppermute(block, 'seq', [(0, 1), (1, 0)])  7.06 us
    ppermute x6, waiting for transfers between devices, paired(): lax.ppermute(block, 'frame', [p for i in pairs for p in ((i, i + 1), (i +...  6.33 us
    pallas_call x2, Pallas kernels, pack_call(): pl.pallas_call(functools.partial(pack_kernel, lay, jobs), in_specs=[SMEM]...  5.16 us
    ppermute x8, starting transfers between devices, swapped(): return lax.ppermute(block, 'seq', [(0, 1), (1, 0)])  4.65 us
  transfers between devices with their start and end apart: 14, of which 8 were waited for; matrix products, arithmetic and copies ran while one was open for 0% of the time, Pallas kernels for 47%

profile of v4, /device:TPU:11, one launch (start us, length us, event | category | flops | bytes accessed | tf_op | source)
XLA Modules:
  0.0 101.1 jit_solution(11787209539719130261)
XLA Ops:
  0.0 0.7 collective-permute-start
  0.8 0.7 copy-done.2
  1.4 0.7 copy-done.3
  2.1 0.7 copy-done.4
  2.8 0.7 copy-done.5
  3.5 1.8 %tile_tables.1.table_ref = s32[216]{0:T(256)S(1)} custom-call(s32[2]{0:T(128)S(1)} %pad_add_fusion.place_ref, s32[2,4,16]{2,1,0:T(4,128)S(1)} %bitcast.8, s32[2,2,16]{2,1,0:T(2,128)S(1)} %bitcast.10, s32[2,1,16]{2,1,0:T(1,128)S(1)} %bitcast.11, s32[3,2,16]{2,1,0:T(2,128)S(1)} %bitcast.9), custom_call_target="tpu_custom_call" | custom-call | tf_op jit(solution)/shard_map/tile_tables/pallas_call | solution.py:131
  5.3 0.9 collective-permute-done.refs_1_
  6.2 0.4 collective-permute-start.3
  6.5 1.3 %copy-done.6 = bf16[4,4,2,64,768]{4,3,2,1,0:T(8,128)(2,1)} copy-done((bf16[4,4,2,64,768]{4,3,2,1,0:T(8,128)(2,1)}, bf16[4,4,2,64,768]{4,3,2,1,0:T(8,128)(2,1)S(1)}, u32[]{:S(2)}) %copy-start.6) | copy-done | bytes 3145752
  7.8 1.9 %pack_tiles.2 = (bf16[4,64,768]{2,1,0:T(8,128)(2,1)S(1)}, bf16[4,64,768]{2,1,0:T(8,128)(2,1)S(1)}) custom-call(s32[2]{0:T(128)S(1)} %pad_add_fusion.place_ref, s32[216]{0:T(256)S(1)} %tile_tables.1.table_ref, bf16[4,4,2,64,768]{4,3,2,1,0:T(8,128)(2,1)} %bitcast.13, bf16[4,4,2,64,768]{4,3,2,1,0:T(8,128)(2,1)} %copy-done.6), custom_call_target="tpu_custom_call" | custom-call | tf_op jit(solution)/shard_map/pack_tiles/pallas_call | solution.py:171
  9.9 4.3 %collective-permute-start.2 = (bf16[4,64,768]{2,1,0:T(8,128)(2,1)S(1)}, bf16[4,64,768]{2,1,0:T(8,128)(2,1)S(1)}, u32[]{:S(2)}, u32[]{:S(2)}) collective-permute-start(bf16[4,64,768]{2,1,0:T(8,128)(2,1)S(1)} %get-tuple-element.33), channel_id=1, source_target_pairs={{4,8},{8,4},{5,9},{9,5},{6,10},{10,6},{7,11},{11,7},{20,24},{24,20... | collective-permute-start | bytes 1179656 | tf_op jit(solution)/shard_map/ppermute | solution.py:567
  14.3 1.7 %copy-done.7 = bf16[4,4,2,64,768]{4,3,2,1,0:T(8,128)(2,1)} copy-done((bf16[4,4,2,64,768]{4,3,2,1,0:T(8,128)(2,1)}, bf16[4,4,2,64,768]{4,3,2,1,0:T(8,128)(2,1)S(1)}, u32[]{:S(2)}) %copy-start.7) | copy-done | bytes 3145752
  16.0 3.3 %pack_tiles.3 = (bf16[10,64,768]{2,1,0:T(8,128)(2,1)S(1)}, bf16[10,64,768]{2,1,0:T(8,128)(2,1)S(1)}, bf16[10,64,768]{2,1,0:T(8,128)(2,1)S(1)}, bf16[10,64,768]{2,1,0:T(8,128)(2,1)S(1)}) custom-call(s32[2]{0:T(128)S(1)} %pad_add_fusion.place_ref, s32[216]{0:T(256)S(1)} %tile_tables.1.table_ref, bf16[4,4,2,64,768]{4,3,2,1,0:T(8,128)(2,1)} %bitcast.14, ...), custom_call_target="tpu_custom_call" | custom-call | tf_op jit(solution)/shard_map/pack_tiles/pallas_call | solution.py:171
  19.3 2.4 %collective-permute-start.5 = (bf16[10,64,768]{2,1,0:T(8,128)(2,1)S(1)}, bf16[10,64,768]{2,1,0:T(8,128)(2,1)S(1)}, u32[]{:S(2)}, u32[]{:S(2)}) collective-permute-start(bf16[10,64,768]{2,1,0:T(8,128)(2,1)S(1)} %get-tuple-element.39), channel_id=1, source_target_pairs={{4,8},{8,4},{5,9},{9,5},{6,10},{10,6},{7,11},{11,7},{20,24},{24,20... | collective-permute-start | bytes 2949128 | tf_op jit(solution)/shard_map/ppermute | solution.py:567
  21.8 1.3 %collective-permute-done.2.refs_5_ = bf16[4,64,768]{2,1,0:T(8,128)(2,1)S(1)} collective-permute-done((bf16[4,64,768]{2,1,0:T(8,128)(2,1)S(1)}, bf16[4,64,768]{2,1,0:T(8,128)(2,1)S(1)}, u32[]{:S(2)}, u32[]{:S(2)}) %collective-permute-start.2) | collective-permute-done | bytes 393248 | tf_op jit(solution)/shard_map/ppermute | solution.py:567
  23.1 15.8 %attend_edges.1 = (f32[2,512,768]{2,1,0:T(8,128)S(1)}, f32[2,512,128]{2,1,0:T(8,128)S(1)}) custom-call(s32[2]{0:T(128)S(1)} %pad_add_fusion.place_ref, s32[216]{0:T(256)S(1)} %tile_tables.1.table_ref, bf16[4,512,768]{2,1,0:T(8,128)(2,1)} %q_ref.5, bf16[4,4,2,64,768]{4,3,2,1,0:T(8,128)(2,1)} %bitcast.15, bf16[4,4,2,64,768]{4,3,2,1,0:T(8,128)(2,1)} %copy-done.6, ...), custom_call_target="tpu_custom_call" | custom-call | flops 6442450944 | bytes 1572864 | tf_op jit(solution)/shard_map/attend_edges/pallas_call | solution.py:464
  38.9 2.8 %collective-permute-done.4.refs_8_ = bf16[10,64,768]{2,1,0:T(8,128)(2,1)S(1)} collective-permute-done((bf16[10,64,768]{2,1,0:T(8,128)(2,1)S(1)}, bf16[10,64,768]{2,1,0:T(8,128)(2,1)S(1)}, u32[]{:S(2)}, u32[]{:S(2)}) %collective-permute-start.4) | collective-permute-done | bytes 983072 | tf_op jit(solution)/shard_map/ppermute | solution.py:567
  41.7 2.2 %collective-permute-done.5.refs_9_ = bf16[10,64,768]{2,1,0:T(8,128)(2,1)S(1)} collective-permute-done((bf16[10,64,768]{2,1,0:T(8,128)(2,1)S(1)}, bf16[10,64,768]{2,1,0:T(8,128)(2,1)S(1)}, u32[]{:S(2)}, u32[]{:S(2)}) %collective-permute-start.5) | collective-permute-done | bytes 983072 | tf_op jit(solution)/shard_map/ppermute | solution.py:567
  43.9 1.8 %collective-permute-start.8 = (bf16[10,64,768]{2,1,0:T(8,128)(2,1)S(1)}, bf16[10,64,768]{2,1,0:T(8,128)(2,1)S(1)}, u32[]{:S(2)}, u32[]{:S(2)}) collective-permute-start(bf16[10,64,768]{2,1,0:T(8,128)(2,1)S(1)} %collective-permute-done.4.refs_8_), channel_id=1, source_target_pairs={{0,1},{1,0},{2,3},{3,2},{4,5},{5,4},{6,7},{7,6},{8,9},{9,8},{10,11... | collective-permute-start | bytes 2949128 | tf_op jit(solution)/shard_map/ppermute | solution.py:571
  45.7 3.2 %collective-permute-start.11 = (bf16[10,64,768]{2,1,0:T(8,128)(2,1)S(1)}, bf16[10,64,768]{2,1,0:T(8,128)(2,1)S(1)}, u32[]{:S(2)}, u32[]{:S(2)}) collective-permute-start(bf16[10,64,768]{2,1,0:T(8,128)(2,1)S(1)} %get-tuple-element.47), channel_id=1, source_target_pairs={{4,8},{8,4},{5,9},{9,5},{6,10},{10,6},{7,11},{11,7},{20,24},{24,20... | collective-permute-start | bytes 2949128 | tf_op jit(solution)/shard_map/ppermute | solution.py:567
  48.9 0.9 collective-permute-start.6
  49.8 1.3 %collective-permute-done.6.refs_6_ = bf16[4,64,768]{2,1,0:T(8,128)(2,1)S(1)} collective-permute-done((bf16[4,64,768]{2,1,0:T(8,128)(2,1)S(1)}, bf16[4,64,768]{2,1,0:T(8,128)(2,1)S(1)}, u32[]{:S(2)}, u32[]{:S(2)}) %collective-permute-start.6) | collective-permute-done | bytes 393248 | tf_op jit(solution)/shard_map/ppermute | solution.py:571
  51.1 0.4 collective-permute-start.7
  51.5 1.3 %collective-permute-done.7.refs_7_ = bf16[4,64,768]{2,1,0:T(8,128)(2,1)S(1)} collective-permute-done((bf16[4,64,768]{2,1,0:T(8,128)(2,1)S(1)}, bf16[4,64,768]{2,1,0:T(8,128)(2,1)S(1)}, u32[]{:S(2)}, u32[]{:S(2)}) %collective-permute-start.7) | collective-permute-done | bytes 393248 | tf_op jit(solution)/shard_map/ppermute | solution.py:571
  52.9 0.7 copy-done.15
  54.0 1.0 copy-done.11
  55.0 24.4 %attend_middle.1.refs_16_ = bf16[4,512,768]{2,1,0:T(8,128)(2,1)} custom-call(s32[2]{0:T(128)S(1)} %pad_add_fusion.place_ref, s32[216]{0:T(256)S(1)} %tile_tables.1.table_ref, bf16[4,512,768]{2,1,0:T(8,128)(2,1)S(1)} %copy-done, bf16[4,4,2,64,768]{4,3,2,1,0:T(8,128)(2,1)} %bitcast.16, bf16[4,4,2,64,768]{4,3,2,1,0:T(8,128)(2,1)} %copy-done.6, ...), custom_call_target="tpu_custom_call" | custom-call | flops 402653184 | bytes 98304 | tf_op jit(solution)/shard_map/attend_middle/pallas_call | solution.py:464
  79.4 0.5 collective-permute-start.12
  80.0 2.1 %collective-permute-done.12.refs_14_ = bf16[10,64,768]{2,1,0:T(8,128)(2,1)S(1)} collective-permute-done((bf16[10,64,768]{2,1,0:T(8,128)(2,1)S(1)}, bf16[10,64,768]{2,1,0:T(8,128)(2,1)S(1)}, u32[]{:S(2)}, u32[]{:S(2)}) %collective-permute-start.12) | collective-permute-done | bytes 983072 | tf_op jit(solution)/shard_map/ppermute | solution.py:571
  82.1 1.4 %collective-permute-done.13.refs_15_ = bf16[10,64,768]{2,1,0:T(8,128)(2,1)S(1)} collective-permute-done((bf16[10,64,768]{2,1,0:T(8,128)(2,1)S(1)}, bf16[10,64,768]{2,1,0:T(8,128)(2,1)S(1)}, u32[]{:S(2)}, u32[]{:S(2)}) %collective-permute-start.13) | collective-permute-done | bytes 983072 | tf_op jit(solution)/shard_map/ppermute | solution.py:571
  83.5 0.9 copy-done.19
  84.4 16.5 %attend_late.1 = bf16[4,512,768]{2,1,0:T(8,128)(2,1)} custom-call(s32[2]{0:T(128)S(1)} %pad_add_fusion.place_ref, s32[216]{0:T(256)S(1)} %tile_tables.1.table_ref, bf16[4,512,768]{2,1,0:T(8,128)(2,1)S(1)} %copy-done, f32[2,512,768]{2,1,0:T(8,128)} %copy-done.1, f32[2,512,128]{2,1,0:T(8,128)S(1)} %get-tuple-element.41.stat_ref, ...), custom_call_target="tpu_custom_call", output_to_operand_aliasing={{}: (21, {})} | custom-call | flops 2818572288 | bytes 688128 | tf_op jit(solution)/shard_map/attend_late/pallas_call | solution.py:529
  (43 shorter events, 0.9 us)
Async XLA Ops:
  0.0 6.2 %collective-permute-start = (bf16[4,4,2,64,768]{4,3,2,1,0:T(8,128)(2,1)}, bf16[4,4,2,64,768]{4,3,2,1,0:T(8,128)(2,1)S(1)}, u32[]{:S(2)}, u32[]{:S(2)}) collective-permute-start(bf16[4,4,2,64,768]{4,3,2,1,0:T(8,128)(2,1)} %bitcast.12), channel_id=1, source_target_pairs={{0,1},{1,0},{2,3},{3,2},{4,5},{5,4},{6,7},{7,6},{8,9},{9,8},{10,11... | collective-permute-start | bytes 9437192 | tf_op jit(solution)/shard_map/ppermute | solution.py:571
  0.8 0.7 copy-start.2
  1.4 0.7 copy-start.3
  6.2 1.6 %copy-start.6 = (bf16[4,4,2,64,768]{4,3,2,1,0:T(8,128)(2,1)}, bf16[4,4,2,64,768]{4,3,2,1,0:T(8,128)(2,1)S(1)}, u32[]{:S(2)}) copy-start(bf16[4,4,2,64,768]{4,3,2,1,0:T(8,128)(2,1)S(1)} %collective-permute-done.refs_1_) | copy-start | bytes 9437188
  6.2 8.1 %collective-permute-start.3 = (bf16[4,4,2,64,768]{4,3,2,1,0:T(8,128)(2,1)}, bf16[4,4,2,64,768]{4,3,2,1,0:T(8,128)(2,1)S(1)}, u32[]{:S(2)}, u32[]{:S(2)}) collective-permute-start(bf16[4,4,2,64,768]{4,3,2,1,0:T(8,128)(2,1)} %bitcast.18), channel_id=1, source_target_pairs={{0,1},{1,0},{2,3},{3,2},{4,5},{5,4},{6,7},{7,6},{8,9},{9,8},{10,11... | collective-permute-start | bytes 9437192 | tf_op jit(solution)/shard_map/ppermute | solution.py:571
  9.7 12.1 %collective-permute-start.1 = (bf16[4,64,768]{2,1,0:T(8,128)(2,1)S(1)}, bf16[4,64,768]{2,1,0:T(8,128)(2,1)S(1)}, u32[]{:S(2)}, u32[]{:S(2)}) collective-permute-start(bf16[4,64,768]{2,1,0:T(8,128)(2,1)S(1)} %get-tuple-element.32), channel_id=1, source_target_pairs={{0,4},{4,0},{8,12},{12,8},{1,5},{5,1},{9,13},{13,9},{2,6},{6,2},{1... | collective-permute-start | bytes 1179656 | tf_op jit(solution)/shard_map/ppermute | solution.py:567
  9.9 13.2 %collective-permute-start.2 = (bf16[4,64,768]{2,1,0:T(8,128)(2,1)S(1)}, bf16[4,64,768]{2,1,0:T(8,128)(2,1)S(1)}, u32[]{:S(2)}, u32[]{:S(2)}) collective-permute-start(bf16[4,64,768]{2,1,0:T(8,128)(2,1)S(1)} %get-tuple-element.33), channel_id=1, source_target_pairs={{4,8},{8,4},{5,9},{9,5},{6,10},{10,6},{7,11},{11,7},{20,24},{24,20... | collective-permute-start | bytes 1179656 | tf_op jit(solution)/shard_map/ppermute | solution.py:567
  14.3 1.7 %copy-start.7 = (bf16[4,4,2,64,768]{4,3,2,1,0:T(8,128)(2,1)}, bf16[4,4,2,64,768]{4,3,2,1,0:T(8,128)(2,1)S(1)}, u32[]{:S(2)}) copy-start(bf16[4,4,2,64,768]{4,3,2,1,0:T(8,128)(2,1)S(1)} %collective-permute-done.3.refs_3_) | copy-start | bytes 9437188
  19.3 22.4 %collective-permute-start.4 = (bf16[10,64,768]{2,1,0:T(8,128)(2,1)S(1)}, bf16[10,64,768]{2,1,0:T(8,128)(2,1)S(1)}, u32[]{:S(2)}, u32[]{:S(2)}) collective-permute-start(bf16[10,64,768]{2,1,0:T(8,128)(2,1)S(1)} %get-tuple-element.38), channel_id=1, source_target_pairs={{0,4},{4,0},{8,12},{12,8},{1,5},{5,1},{9,13},{13,9},{2,6},{6,2},{1... | collective-permute-start | bytes 2949128 | tf_op jit(solution)/shard_map/ppermute | solution.py:567
  19.3 35.6 %copy-start = (bf16[4,512,768]{2,1,0:T(8,128)(2,1)S(1)}, bf16[4,512,768]{2,1,0:T(8,128)(2,1)}, u32[]{:S(2)}) copy-start(bf16[4,512,768]{2,1,0:T(8,128)(2,1)} %q_ref.5) | copy-start | bytes 9437188
  19.3 24.5 %collective-permute-start.5 = (bf16[10,64,768]{2,1,0:T(8,128)(2,1)S(1)}, bf16[10,64,768]{2,1,0:T(8,128)(2,1)S(1)}, u32[]{:S(2)}, u32[]{:S(2)}) collective-permute-start(bf16[10,64,768]{2,1,0:T(8,128)(2,1)S(1)} %get-tuple-element.39), channel_id=1, source_target_pairs={{4,8},{8,4},{5,9},{9,5},{6,10},{10,6},{7,11},{11,7},{20,24},{24,20... | collective-permute-start | bytes 2949128 | tf_op jit(solution)/shard_map/ppermute | solution.py:567
  21.7 27.2 %copy-start.12 = (bf16[4,64,768]{2,1,0:T(8,128)(2,1)}, bf16[4,64,768]{2,1,0:T(8,128)(2,1)S(1)}, u32[]{:S(2)}) copy-start(bf16[4,64,768]{2,1,0:T(8,128)(2,1)S(1)} %collective-permute-done.1.refs_4_) | copy-start | bytes 1179652
  23.1 28.0 %copy-start.13 = (bf16[4,64,768]{2,1,0:T(8,128)(2,1)}, bf16[4,64,768]{2,1,0:T(8,128)(2,1)S(1)}, u32[]{:S(2)}) copy-start(bf16[4,64,768]{2,1,0:T(8,128)(2,1)S(1)} %collective-permute-done.2.refs_5_) | copy-start | bytes 1179652
  38.9 40.5 %copy-start.1 = (f32[2,512,768]{2,1,0:T(8,128)}, f32[2,512,768]{2,1,0:T(8,128)S(1)}, u32[]{:S(2)}) copy-start(f32[2,512,768]{2,1,0:T(8,128)S(1)} %get-tuple-element.37.acc_ref) | copy-start | bytes 9437188
  41.7 11.2 %copy-start.8 = (bf16[10,64,768]{2,1,0:T(8,128)(2,1)}, bf16[10,64,768]{2,1,0:T(8,128)(2,1)S(1)}, u32[]{:S(2)}) copy-start(bf16[10,64,768]{2,1,0:T(8,128)(2,1)S(1)} %collective-permute-done.4.refs_8_) | copy-start | bytes 2949124
  43.9 9.0 %copy-start.9 = (bf16[10,64,768]{2,1,0:T(8,128)(2,1)}, bf16[10,64,768]{2,1,0:T(8,128)(2,1)S(1)}, u32[]{:S(2)}) copy-start(bf16[10,64,768]{2,1,0:T(8,128)(2,1)S(1)} %collective-permute-done.5.refs_9_) | copy-start | bytes 2949124
  43.9 9.0 %collective-permute-start.8 = (bf16[10,64,768]{2,1,0:T(8,128)(2,1)S(1)}, bf16[10,64,768]{2,1,0:T(8,128)(2,1)S(1)}, u32[]{:S(2)}, u32[]{:S(2)}) collective-permute-start(bf16[10,64,768]{2,1,0:T(8,128)(2,1)S(1)} %collective-permute-done.4.refs_8_), channel_id=1, source_target_pairs={{0,1},{1,0},{2,3},{3,2},{4,5},{5,4},{6,7},{7,6},{8,9},{9,8},{10,11... | collective-permute-start | bytes 2949128 | tf_op jit(solution)/shard_map/ppermute | solution.py:571
  45.7 7.2 %collective-permute-start.9 = (bf16[10,64,768]{2,1,0:T(8,128)(2,1)S(1)}, bf16[10,64,768]{2,1,0:T(8,128)(2,1)S(1)}, u32[]{:S(2)}, u32[]{:S(2)}) collective-permute-start(bf16[10,64,768]{2,1,0:T(8,128)(2,1)S(1)} %collective-permute-done.5.refs_9_), channel_id=1, source_target_pairs={{0,1},{1,0},{2,3},{3,2},{4,5},{5,4},{6,7},{7,6},{8,9},{9,8},{10,11... | collective-permute-start | bytes 2949128 | tf_op jit(solution)/shard_map/ppermute | solution.py:571
  45.7 33.7 %collective-permute-start.10 = (bf16[10,64,768]{2,1,0:T(8,128)(2,1)S(1)}, bf16[10,64,768]{2,1,0:T(8,128)(2,1)S(1)}, u32[]{:S(2)}, u32[]{:S(2)}) collective-permute-start(bf16[10,64,768]{2,1,0:T(8,128)(2,1)S(1)} %get-tuple-element.46), channel_id=1, source_target_pairs={{0,4},{4,0},{8,12},{12,8},{1,5},{5,1},{9,13},{13,9},{2,6},{6,2},{1... | collective-permute-start | bytes 2949128 | tf_op jit(solution)/shard_map/ppermute | solution.py:567
  45.7 33.7 %collective-permute-start.11 = (bf16[10,64,768]{2,1,0:T(8,128)(2,1)S(1)}, bf16[10,64,768]{2,1,0:T(8,128)(2,1)S(1)}, u32[]{:S(2)}, u32[]{:S(2)}) collective-permute-start(bf16[10,64,768]{2,1,0:T(8,128)(2,1)S(1)} %get-tuple-element.47), channel_id=1, source_target_pairs={{4,8},{8,4},{5,9},{9,5},{6,10},{10,6},{7,11},{11,7},{20,24},{24,20... | collective-permute-start | bytes 2949128 | tf_op jit(solution)/shard_map/ppermute | solution.py:567
  48.9 2.2 %collective-permute-start.6 = (bf16[4,64,768]{2,1,0:T(8,128)(2,1)S(1)}, bf16[4,64,768]{2,1,0:T(8,128)(2,1)S(1)}, u32[]{:S(2)}, u32[]{:S(2)}) collective-permute-start(bf16[4,64,768]{2,1,0:T(8,128)(2,1)S(1)} %collective-permute-done.1.refs_4_), channel_id=1, source_target_pairs={{0,1},{1,0},{2,3},{3,2},{4,5},{5,4},{6,7},{7,6},{8,9},{9,8},{10,11... | collective-permute-start | bytes 1179656 | tf_op jit(solution)/shard_map/ppermute | solution.py:571
  51.1 1.8 %copy-start.14 = (bf16[4,64,768]{2,1,0:T(8,128)(2,1)}, bf16[4,64,768]{2,1,0:T(8,128)(2,1)S(1)}, u32[]{:S(2)}) copy-start(bf16[4,64,768]{2,1,0:T(8,128)(2,1)S(1)} %collective-permute-done.6.refs_6_) | copy-start | bytes 1179652
  51.1 1.7 %collective-permute-start.7 = (bf16[4,64,768]{2,1,0:T(8,128)(2,1)S(1)}, bf16[4,64,768]{2,1,0:T(8,128)(2,1)S(1)}, u32[]{:S(2)}, u32[]{:S(2)}) collective-permute-start(bf16[4,64,768]{2,1,0:T(8,128)(2,1)S(1)} %collective-permute-done.2.refs_5_), channel_id=1, source_target_pairs={{0,1},{1,0},{2,3},{3,2},{4,5},{5,4},{6,7},{7,6},{8,9},{9,8},{10,11... | collective-permute-start | bytes 1179656 | tf_op jit(solution)/shard_map/ppermute | solution.py:571
  52.9 0.7 copy-start.15
  52.9 1.1 %copy-start.10 = (bf16[10,64,768]{2,1,0:T(8,128)(2,1)}, bf16[10,64,768]{2,1,0:T(8,128)(2,1)S(1)}, u32[]{:S(2)}) copy-start(bf16[10,64,768]{2,1,0:T(8,128)(2,1)S(1)} %collective-permute-done.8.refs_10_) | copy-start | bytes 2949124
  54.0 1.0 copy-start.11
  79.4 4.1 %copy-start.16 = (bf16[10,64,768]{2,1,0:T(8,128)(2,1)}, bf16[10,64,768]{2,1,0:T(8,128)(2,1)S(1)}, u32[]{:S(2)}) copy-start(bf16[10,64,768]{2,1,0:T(8,128)(2,1)S(1)} %collective-permute-done.10.refs_12_) | copy-start | bytes 2949124
  79.4 4.1 %copy-start.17 = (bf16[10,64,768]{2,1,0:T(8,128)(2,1)}, bf16[10,64,768]{2,1,0:T(8,128)(2,1)S(1)}, u32[]{:S(2)}) copy-start(bf16[10,64,768]{2,1,0:T(8,128)(2,1)S(1)} %collective-permute-done.11.refs_13_) | copy-start | bytes 2949124
  79.4 2.6 %collective-permute-start.12 = (bf16[10,64,768]{2,1,0:T(8,128)(2,1)S(1)}, bf16[10,64,768]{2,1,0:T(8,128)(2,1)S(1)}, u32[]{:S(2)}, u32[]{:S(2)}) collective-permute-start(bf16[10,64,768]{2,1,0:T(8,128)(2,1)S(1)} %collective-permute-done.10.refs_12_), channel_id=1, source_target_pairs={{0,1},{1,0},{2,3},{3,2},{4,5},{5,4},{6,7},{7,6},{8,9},{9,8},{10,11... | collective-permute-start | bytes 2949128 | tf_op jit(solution)/shard_map/ppermute | solution.py:571
  79.9 3.6 %collective-permute-start.13 = (bf16[10,64,768]{2,1,0:T(8,128)(2,1)S(1)}, bf16[10,64,768]{2,1,0:T(8,128)(2,1)S(1)}, u32[]{:S(2)}, u32[]{:S(2)}) collective-permute-start(bf16[10,64,768]{2,1,0:T(8,128)(2,1)S(1)} %collective-permute-done.11.refs_13_), channel_id=1, source_target_pairs={{0,1},{1,0},{2,3},{3,2},{4,5},{5,4},{6,7},{7,6},{8,9},{9,8},{10,11... | collective-permute-start | bytes 2949128 | tf_op jit(solution)/shard_map/ppermute | solution.py:571
  82.1 1.4 %copy-start.18 = (bf16[10,64,768]{2,1,0:T(8,128)(2,1)}, bf16[10,64,768]{2,1,0:T(8,128)(2,1)S(1)}, u32[]{:S(2)}) copy-start(bf16[10,64,768]{2,1,0:T(8,128)(2,1)S(1)} %collective-permute-done.12.refs_14_) | copy-start | bytes 2949124
  83.5 0.9 copy-start.19
  (2 other events, 1.4 us)

commit v5 on v4

v5 whole, which is shorter than its diff:
```python
import functools
import math

import jax
import jax.numpy as jnp
from jax import lax
from jax.experimental import pallas as pl
from jax.experimental.pallas import tpu as pltpu
from jax.sharding import PartitionSpec as P

HEAD_DIM = 128
TILE = 128
DISTANCES = (1, 2, 4)
STRIDE = 24
SCALE = math.log2(math.e) / math.sqrt(HEAD_DIM)
LARGE = 2.0**100
NT = (((1,), (1,)), ((), ()))
BF = jnp.bfloat16
F32 = jnp.float32
ANY = pl.BlockSpec(memory_space=pl.ANY)
SMEM = pl.BlockSpec(memory_space=pltpu.SMEM)
VMEM_LIMIT = 48 * 2**20
PACK_LIMIT = 16 * 2**20


class Layout:
    def __init__(self, frames_here, frame_tiles, frames, lengths):
        self.here = frames_here
        self.tiles = frame_tiles
        self.half = frame_tiles // 2
        self.own = frames_here * frame_tiles
        self.frames = frames
        self.lengths = lengths
        self.early = self.late = 0
        for frame, column, _ in self.remote(0):
            if self.edge(frame):
                self.late += lengths[column]
            else:
                self.early += lengths[column]
        self.places = self.early + self.late
        self.first = self.early + self.late // 4
        self.second = self.places - self.first
        self.near = 2 * self.places
        self.far = self.near + frames_here * STRIDE
        self.size = self.far + frames_here * STRIDE

    def edge(self, frame):
        return frame in (0, self.here - 1)

    def remote(self, direction):
        found = []
        for away in (*range(1, self.here - 1), self.here - 1, 0):
            for column in reversed(range(3)):
                distance = DISTANCES[column]
                if away < distance:
                    frame = away if direction == 0 else self.here - 1 - away
                    source = frame - distance if direction == 0 else frame + distance
                    found.append((frame, column, source % self.here))
        return found


def table_kernel(lay, place_ref, one_ref, two_ref, four_ref, count_ref, table_ref, seen_ref):
    lists = (one_ref, two_ref, four_ref)
    first = place_ref[0]
    odd = first // lay.here % 2

    def distinct(target, direction, on_slot, on_new):
        for i in range(lay.own):
            seen_ref[i] = -1
        used = jnp.int32(0)
        for frame, column, source in lay.remote(direction):
            live = count_ref[column, direction, target + frame]
            for slot in range(lay.lengths[column]):
                name = lists[column][direction, slot, target + frame] + source * lay.tiles
                alive = slot < live
                known = seen_ref[name]
                fresh = jnp.logical_and(alive, known < 0)
                place = jnp.where(fresh, used, known)
                seen_ref[name] = place
                on_new(used, name)
                on_slot(frame, place, alive)
                used = used + fresh.astype(jnp.int32)
        return used

    filled = {}

    def append(base, frame, item, alive):
        at = base + frame * STRIDE
        count = filled.get(at, jnp.int32(0))
        table_ref[at + 1 + count] = item
        filled[at] = count + alive.astype(jnp.int32)

    for direction in (0, 1):
        target = first + (lay.here if direction == 0 else -lay.here)
        target = jnp.clip(target, 0, lay.frames - lay.here)
        begin = (odd + direction) % 2 * lay.places
        for place in range(lay.places):
            table_ref[begin + place] = 0

        def note(used, name, begin=begin):
            table_ref[begin + jnp.minimum(used, lay.places - 1)] = name

        distinct(target, direction, lambda *_: None, note)

    for direction in (0, 1):
        way = (odd + 1 - direction) % 2

        def on_slot(frame, place, alive, way=way):
            if lay.edge(frame):
                append(lay.far, frame, way * lay.places + place, alive)
            else:
                append(lay.near, frame, lay.own + way * lay.early + place, alive)

        distinct(first, direction, on_slot, lambda *_: None)
        for frame in range(lay.here):
            for column, distance in enumerate(DISTANCES):
                source = frame + (2 * direction - 1) * distance
                if 0 <= source < lay.here:
                    live = count_ref[column, direction, first + frame]
                    for slot in range(lay.lengths[column]):
                        name = lists[column][direction, slot, first + frame]
                        append(lay.near, frame, source * lay.tiles + name, slot < live)
    for frame in range(lay.here):
        for base in (lay.near, lay.far):
            at = base + frame * STRIDE
            table_ref[at] = filled.get(at, jnp.int32(0))


def make_table(lay, place, lists):
    return pl.pallas_call(
        functools.partial(table_kernel, lay),
        in_specs=[SMEM] * 5,
        out_specs=SMEM,
        out_shape=jax.ShapeDtypeStruct((lay.size,), jnp.int32),
        scratch_shapes=[pltpu.SMEM((lay.own,), jnp.int32)],
        compiler_params=pltpu.CompilerParams(vmem_limit_bytes=VMEM_LIMIT),
        name="tile_tables",
    )(place, *lists)


def columns(core, width):
    return pl.ds(pl.multiple_of(core * width, HEAD_DIM), width)


def pack_kernel(lay, begin, length, place_ref, table_ref, k_own, k_other, v_own, v_other, *refs):
    outs, sems = refs[:2], refs[2]
    core = place_ref[1]
    cols = columns(core, outs[0].shape[-1])
    waits = []
    for way, out in enumerate(outs):
        for item in range(length):
            name = table_ref[way * lay.places + begin + item]
            frame = name // lay.tiles
            tile = name % lay.tiles
            mine = tile // lay.half == core
            tile = tile % lay.half
            for kv, (own, other) in enumerate(((k_own, k_other), (v_own, v_other))):
                target = out.at[kv * length + item]
                sem = sems.at[len(waits)]
                here = pltpu.make_async_copy(own.at[frame, tile, :, cols], target, sem)
                there = pltpu.make_async_copy(other.at[frame, tile], target, sem)
                pl.when(mine)(here.start)
                pl.when(jnp.logical_not(mine))(there.start)
                waits.append(here)
    for copy in waits:
        copy.wait()


def pack_call(lay, begin, length, place, table, local):
    shape = jax.ShapeDtypeStruct((2 * length, TILE, local[1].shape[-1]), BF)
    return pl.pallas_call(
        functools.partial(pack_kernel, lay, begin, length),
        in_specs=[SMEM] * 2 + [ANY] * 4,
        out_specs=[pl.BlockSpec(memory_space=pltpu.VMEM)] * 2,
        out_shape=[shape] * 2,
        scratch_shapes=[pltpu.SemaphoreType.DMA((4 * length,))],
        compiler_params=pltpu.CompilerParams(vmem_limit_bytes=PACK_LIMIT),
        name="pack_tiles",
    )(place, table, *in_hbm(local))


def rows_of(buf, index, cols):
    tiles = buf[index, :, cols]
    return tiles.reshape(tiles.size // HEAD_DIM, HEAD_DIM)


def units(heads):
    for part in (0, 1):
        for head in range(heads):
            yield part * heads + head, part, slice(head * HEAD_DIM, (head + 1) * HEAD_DIM)


def mix(weights, values):
    return jnp.dot(
        weights.astype(BF),
        jnp.concatenate([values, jnp.ones_like(values)], axis=1),
        preferred_element_type=F32,
    )


def attend_tiles(q_refs, kbuf, vbuf, ids, m_s, l_s, acc_s, heads):
    for unit, part, cols in units(heads):
        keys = jnp.concatenate([rows_of(kbuf, i, cols) for i in ids], axis=0)
        values = jnp.concatenate([rows_of(vbuf, i, cols) for i in ids], axis=0)
        scores = lax.dot_general(q_refs[part][0, :, cols], keys, NT, preferred_element_type=F32)
        shift = jnp.concatenate([m_s[unit]] * len(ids), axis=1)
        mixed = mix(jnp.exp2((scores - shift) * SCALE), values)
        acc_s[unit] += mixed[:, :HEAD_DIM]
        l_s[unit] += mixed[:, HEAD_DIM:]


def attend_list(q_refs, kbuf, vbuf, table_ref, base, m_s, l_s, acc_s, heads, packed=False):
    count = table_ref[base]

    def add(start, n):
        ids = [start + j if packed else table_ref[base + 1 + start + j] for j in range(n)]
        attend_tiles(q_refs, kbuf, vbuf, ids, m_s, l_s, acc_s, heads)

    def four(i, _):
        add(4 * i, 4)
        return 0

    lax.fori_loop(0, count // 4, four, 0)

    @pl.when(count % 4 >= 2)
    def _():
        add(count // 4 * 4, 2)

    @pl.when(count % 2 == 1)
    def _():
        add(count - 1, 1)


def attend_own(lay, q_refs, kbuf, vbuf, frame, m_s, l_s, acc_s, heads):
    own = pl.ds(frame * lay.tiles, lay.tiles)
    for unit, part, cols in units(heads):
        scores = lax.dot_general(
            q_refs[part][0, :, cols], rows_of(kbuf, own, cols), NT, preferred_element_type=F32
        )
        top = jnp.max(scores[:, :TILE], axis=1, keepdims=True)
        mixed = mix(jnp.exp2((scores - top) * SCALE), rows_of(vbuf, own, cols))
        acc_s[unit] = mixed[:, :HEAD_DIM]
        l_s[unit] = mixed[:, HEAD_DIM:]
        m_s[unit] = jnp.broadcast_to(top, m_s.shape[1:])


def save_stats(stat_ref, m_s, l_s, heads):
    rows = stat_ref.shape[1]
    lane = lax.broadcasted_iota(jnp.int32, (rows, 128), 1)
    stat = jnp.zeros((rows, 128), F32)
    for unit, _, _ in units(heads):
        stat = jnp.where(lane == unit, l_s[unit], stat)
        stat = jnp.where(lane == 64 + unit, m_s[unit], stat)
    stat_ref[0] = stat


def load_stats(stat_ref, m_s, l_s, heads):
    rows = stat_ref.shape[1]
    for unit, _, _ in units(heads):
        l_s[unit] = jnp.broadcast_to(stat_ref[0, :, unit : unit + 1], (rows, 128))
        m_s[unit] = jnp.broadcast_to(stat_ref[0, :, 64 + unit : 65 + unit], (rows, 128))


def finish(out_refs, acc_s, l_s, heads):
    for unit, part, cols in units(heads):
        out_refs[part][0, :, cols] = (acc_s[unit] / l_s[unit]).astype(BF)


def local_copies(lay, index, core, local, bufs, sems):
    found = []
    for kv, buf in enumerate(bufs):
        own = local[2 * kv].at[index, :, :, columns(core, buf.shape[-1])]
        for side, source in enumerate((own, local[2 * kv + 1].at[index])):
            owner = core if side == 0 else 1 - core
            target = buf.at[pl.ds(index * lay.tiles + owner * lay.half, lay.half)]
            found.append(pltpu.make_async_copy(source, target, sems.at[index, 2 * kv + side]))
    return found


class Received:
    def __init__(self, lay, refs):
        self.lay = lay
        self.parts = [(0, lay.first, refs[:2])]
        if len(refs) > 2:
            self.parts.append((lay.first, lay.second, refs[2:4]))

    def early_copies(self, bufs, sems):
        _, size, refs = self.parts[0]
        found = []
        for kv, buf in enumerate(bufs):
            for way in (0, 1):
                source = refs[way].at[pl.ds(kv * size, self.lay.early)]
                target = buf.at[pl.ds(self.lay.own + way * self.lay.early, self.lay.early)]
                found.append(pltpu.make_async_copy(source, target, sems.at[len(found)]))
        return found

    def start(self, item, length, targets, sems):
        place = item % length
        for way in (0, 1):
            for begin, size, refs in self.parts:
                inside = jnp.logical_and(place >= begin, place < begin + size)

                @pl.when(jnp.logical_and(item // length == way, inside))
                def _(way=way, begin=begin, size=size, refs=refs):
                    for kv, target in enumerate(targets):
                        source = refs[way].at[place - begin + kv * size]
                        pltpu.make_async_copy(source, target, sems.at[kv]).start()

    def wait(self, targets, sems):
        for kv, target in enumerate(targets):
            pltpu.make_async_copy(self.parts[0][2][0].at[0], target, sems.at[kv]).wait()


def exact_frame(lay, heads, frame, core, table_ref, q_refs, local, received, acc_s, m_s, l_s, tk, tv, sems):
    m_s[...] = jnp.full(m_s.shape, -jnp.inf, F32)
    l_s[...] = jnp.zeros(l_s.shape, F32)
    acc_s[...] = jnp.zeros(acc_s.shape, F32)

    def add_tile():
        for unit, part, cols in units(heads):
            scores = lax.dot_general(
                q_refs[part][0, :, cols], tk[:, cols], NT, preferred_element_type=F32
            )
            before = m_s[unit]
            top = jnp.maximum(before, jnp.max(scores, axis=1, keepdims=True))
            fade = jnp.exp2((before - top) * SCALE)
            mixed = mix(jnp.exp2((scores - top) * SCALE), tv[:, cols])
            acc_s[unit] = acc_s[unit] * fade + mixed[:, :HEAD_DIM]
            l_s[unit] = l_s[unit] * fade + mixed[:, HEAD_DIM:]
            m_s[unit] = top

    def near_tile(name):
        source, tile = name // lay.tiles, name % lay.tiles
        mine = tile // lay.half == core
        tile = tile % lay.half
        cols = columns(core, tk.shape[-1])
        for side in (0, 1):

            @pl.when(mine if side == 0 else jnp.logical_not(mine))
            def _(side=side):
                at = (source, tile, slice(None), cols) if side == 0 else (source, tile)
                found = [
                    pltpu.make_async_copy(local[2 * kv + side].at[at], buf, sems.at[kv])
                    for kv, buf in enumerate((tk, tv))
                ]
                for copy in found:
                    copy.start()
                for copy in found:
                    copy.wait()

    def far_tile(item, length):
        received.start(item, length, (tk, tv), sems)
        received.wait((tk, tv), sems)

    def own_step(i, _):
        near_tile(frame * lay.tiles + i)
        add_tile()
        return 0

    def near_step(i, _):
        name = table_ref[lay.near + frame * STRIDE + 1 + i]

        @pl.when(name < lay.own)
        def _():
            near_tile(name)

        @pl.when(name >= lay.own)
        def _():
            far_tile(name - lay.own, lay.early)

        add_tile()
        return 0

    def far_step(i, _):
        far_tile(table_ref[lay.far + frame * STRIDE + 1 + i], lay.places)
        add_tile()
        return 0

    lax.fori_loop(0, lay.tiles, own_step, 0)
    lax.fori_loop(0, table_ref[lay.near + frame * STRIDE], near_step, 0)
    if len(received.parts) > 1:
        lax.fori_loop(0, table_ref[lay.far + frame * STRIDE], far_step, 0)


def near_kernel(lay, heads, whole, place_ref, table_ref, q_own, q_other, *refs):
    core = place_ref[1]
    q_refs = (q_own, q_other)
    local, refs = refs[:4], refs[4:]
    if whole:
        received, out_refs, refs = Received(lay, refs[:2]), refs[2:4], refs[4:]
        acc_s, kbuf, vbuf, m_s, l_s, sems, tk, tv, far_sems = refs
    else:
        acc_out, stat_ref, kbuf, vbuf, m_s, l_s, sems = refs
        acc_s = acc_out.at[0]
    step = pl.program_id(0)
    frame = step + 1 if whole else step * (lay.here - 1)
    begin = 1 if whole else 0

    def first():
        return local_copies(lay, begin, core, local, (kbuf, vbuf), sems)

    def others():
        found = []
        for index in range(lay.here):
            if index != begin:
                found += local_copies(lay, index, core, local, (kbuf, vbuf), sems)
        return found + (received.early_copies((kbuf, vbuf), far_sems) if whole else [])

    @pl.when(step == 0)
    def _():
        for copy in first():
            copy.start()
        for copy in first():
            copy.wait()
        for copy in others():
            copy.start()

    attend_own(lay, q_refs, kbuf, vbuf, frame, m_s, l_s, acc_s, heads)

    @pl.when(step == 0)
    def _():
        for copy in others():
            copy.wait()

    attend_list(q_refs, kbuf, vbuf, table_ref, lay.near + frame * STRIDE, m_s, l_s, acc_s, heads)
    if whole:

        @pl.when(jnp.max(l_s[...]) > LARGE)
        def _():
            exact_frame(lay, heads, frame, core, table_ref, q_refs, local, received, acc_s, m_s, l_s, tk, tv, far_sems)

        finish(out_refs, acc_s, l_s, heads)
    else:
        save_stats(stat_ref, m_s, l_s, heads)


def cost(scores):
    return pl.CostEstimate(flops=scores * 4 * HEAD_DIM, bytes_accessed=scores // 8, transcendentals=scores)


def token_blocks(rows, width, frame_of):
    return (
        pl.BlockSpec((1, rows, width), lambda s, place, _: (frame_of(s), 0, place[1])),
        pl.BlockSpec((1, rows, width), lambda s, *_: (frame_of(s), 0, 0)),
    )


def near_call(lay, heads, whole, place, table, queries, local, early=()):
    here, rows, width = queries[1].shape
    steps = here - 2 if whole else 2
    own, other = token_blocks(rows, width, (lambda s: s + 1) if whole else (lambda s: s * (here - 1)))
    count = lay.own + (2 * lay.early if whole else 0)
    bufs = [pltpu.VMEM((count, TILE, width), BF)] * 2
    sums = [pltpu.VMEM((2 * heads, rows, 128), F32)] * 2
    sems = [pltpu.SemaphoreType.DMA((here, 4))]
    if whole:
        out_specs = [own, pl.BlockSpec((1, rows, width), lambda s, *_: (s, 0, 0))]
        out_shape = [jax.ShapeDtypeStruct(queries[0].shape, BF), jax.ShapeDtypeStruct((steps, rows, width), BF)]
        scratch = [sums[0], *bufs, *sums, *sems]
        scratch += [pltpu.VMEM((TILE, width), BF)] * 2 + [pltpu.SemaphoreType.DMA((4,))]
    else:
        out_specs = [
            pl.BlockSpec((1, 2 * heads, rows, 128), lambda s, *_: (s, 0, 0, 0)),
            pl.BlockSpec((1, rows, 128), lambda s, *_: (s, 0, 0)),
        ]
        out_shape = [jax.ShapeDtypeStruct((2, 2 * heads, rows, 128), F32), jax.ShapeDtypeStruct((2, rows, 128), F32)]
        scratch = [*bufs, *sums, *sems]
    return pl.pallas_call(
        functools.partial(near_kernel, lay, heads, whole),
        grid_spec=pltpu.PrefetchScalarGridSpec(
            num_scalar_prefetch=2,
            grid=(steps,),
            in_specs=[own, other] + [ANY] * (4 + len(early)),
            out_specs=out_specs,
            scratch_shapes=scratch,
        ),
        out_shape=out_shape,
        compiler_params=pltpu.CompilerParams(vmem_limit_bytes=VMEM_LIMIT),
        cost_estimate=cost(steps * rows * heads * 32 * TILE),
        name="attend_middle" if whole else "attend_edges",
    )(place, table, *queries, *in_hbm((*local, *early)))


def far_kernel(lay, heads, place_ref, table_ref, q_own, q_other, acc_ref, stat_ref, *refs):
    core = place_ref[1]
    q_refs = (q_own, q_other)
    local, received, out_refs = refs[:4], Received(lay, refs[4:8]), refs[9:11]
    kbuf, vbuf, acc_s, m_s, l_s, tk, tv, sems, exact_sems = refs[11:]
    step = pl.program_id(0)
    frame = step * (lay.here - 1)
    room = kbuf.shape[1]

    def bufs(at, i):
        return kbuf.at[at, i], vbuf.at[at, i]

    def start(at):
        base = lay.far + at * (lay.here - 1) * STRIDE

        def one(i, _):
            received.start(table_ref[base + 1 + i], lay.places, bufs(at, i), sems.at[at * room + i])
            return 0

        lax.fori_loop(0, table_ref[base], one, 0)

    @pl.when(step == 0)
    def _():
        start(0)
        start(1)

    load_stats(stat_ref, m_s, l_s, heads)
    acc_s[...] = acc_ref[0]
    base = lay.far + frame * STRIDE

    def wait(i, _):
        received.wait(bufs(step, i), sems.at[step * room + i])
        return 0

    lax.fori_loop(0, table_ref[base], wait, 0)
    attend_list(q_refs, kbuf.at[step], vbuf.at[step], table_ref, base, m_s, l_s, acc_s, heads, packed=True)

    @pl.when(jnp.max(l_s[...]) > LARGE)
    def _():
        exact_frame(lay, heads, frame, core, table_ref, q_refs, local, received, acc_s, m_s, l_s, tk, tv, exact_sems)

    finish(out_refs, acc_s, l_s, heads)


def far_call(lay, heads, place, table, queries, acc, stats, local, early, late, out):
    here, rows, width = queries[1].shape
    own, other = token_blocks(rows, width, lambda s: s * (here - 1))
    anys = [*local, *early, *late]
    room = sum(lay.lengths[column] for way in (0, 1) for frame, column, _ in lay.remote(way) if frame == 0)
    sums = pltpu.VMEM((2 * heads, rows, 128), F32)
    return pl.pallas_call(
        functools.partial(far_kernel, lay, heads),
        grid_spec=pltpu.PrefetchScalarGridSpec(
            num_scalar_prefetch=2,
            grid=(2,),
            in_specs=[
                own,
                other,
                pl.BlockSpec((1, 2 * heads, rows, 128), lambda s, *_: (s, 0, 0, 0)),
                pl.BlockSpec((1, rows, 128), lambda s, *_: (s, 0, 0)),
            ]
            + [ANY] * (len(anys) + 1),
            out_specs=[own, pl.BlockSpec((1, rows, width), lambda s, *_: (s, 0, 0))],
            scratch_shapes=[
                pltpu.VMEM((2, room, TILE, width), BF),
                pltpu.VMEM((2, room, TILE, width), BF),
                sums,
                sums,
                sums,
                pltpu.VMEM((TILE, width), BF),
                pltpu.VMEM((TILE, width), BF),
                pltpu.SemaphoreType.DMA((2 * room, 2)),
                pltpu.SemaphoreType.DMA((2,)),
            ],
        ),
        out_shape=[jax.ShapeDtypeStruct(out.shape, BF), jax.ShapeDtypeStruct((2, rows, width), BF)],
        input_output_aliases={6 + len(anys): 0},
        compiler_params=pltpu.CompilerParams(vmem_limit_bytes=VMEM_LIMIT),
        cost_estimate=cost(2 * rows * heads * 14 * TILE),
        name="attend_late",
    )(place, table, *queries, acc, stats, *in_hbm(anys), out)


def place_kernel(place_ref, block_ref, _, out_ref):
    out_ref[...] = block_ref[...]


def place_call(place, blocks, out, frame_of):
    steps, rows, width = blocks.shape
    return pl.pallas_call(
        place_kernel,
        grid_spec=pltpu.PrefetchScalarGridSpec(
            num_scalar_prefetch=1,
            grid=(steps,),
            in_specs=[pl.BlockSpec((1, rows, width), lambda s, place: (s, 0, 0)), ANY],
            out_specs=pl.BlockSpec((1, rows, width), lambda s, place: (frame_of(s), 0, 1 - place[1])),
        ),
        out_shape=jax.ShapeDtypeStruct(out.shape, BF),
        input_output_aliases={2: 0},
        compiler_params=pltpu.CompilerParams(vmem_limit_bytes=VMEM_LIMIT),
        name="place_columns",
    )(place, blocks, out)


def in_hbm(arrays):
    return [pltpu.with_memory_space_constraint(a, pltpu.HBM) for a in arrays]


def paired(block, way):
    pairs = range(way, lax.axis_size("frame") - 1, 2)
    return lax.ppermute(block, "frame", [p for i in pairs for p in ((i, i + 1), (i + 1, i))])


def swapped(block):
    return lax.ppermute(block, "seq", [(0, 1), (1, 0)])


def per_device(queries, key_rows, value_rows, list_one, list_two, list_four, tile_counts):
    here, rows, width = queries.shape
    heads = -(-width // HEAD_DIM // 2)
    part = heads * HEAD_DIM
    frames = list_one.shape[0]
    lists = (list_one, list_two, list_four)
    lay = Layout(here, 2 * rows // TILE, frames, tuple(a.shape[2] for a in lists))
    core = lax.axis_index("seq")
    place = jnp.stack([lax.axis_index("frame") * here, core]).astype(jnp.int32)
    if width < 2 * part:
        spare = ((0, 0), (0, 0), (0, 2 * part - width))
        queries, key_rows, value_rows = (jnp.pad(a, spare) for a in (queries, key_rows, value_rows))

    def exchanged(a):
        return swapped(lax.dynamic_slice_in_dim(a, (1 - core) * part, part, axis=2))

    def tiled(a):
        return a.reshape(here, lay.half, TILE, a.shape[2])

    k_other = tiled(exchanged(key_rows))
    v_other = tiled(exchanged(value_rows))
    queries = (queries, exchanged(queries))
    by_frame = [jnp.transpose(a, (1, 2, 0)) for a in lists] + [jnp.transpose(tile_counts, (2, 1, 0))]
    table = make_table(lay, place, by_frame)
    local = (tiled(key_rows), k_other, tiled(value_rows), v_other)

    def both_ways(pair):
        return paired(pair[0], 0), paired(pair[1], 1)

    early = pack_call(lay, 0, lay.first, place, table, local)
    early, table = lax.optimization_barrier((early, table))
    early = both_ways(early)
    late = both_ways(pack_call(lay, lay.first, lay.second, place, table, local))
    acc, stats = near_call(lay, heads, False, place, table, queries, local)
    early, stats = lax.optimization_barrier((early, stats))
    out, sent = near_call(lay, heads, True, place, table, queries, local, early)
    late, sent = lax.optimization_barrier((late, sent))
    middle = swapped(sent)
    out, sent = far_call(lay, heads, place, table, queries, acc, stats, local, early, late, out)
    out = place_call(place, middle, out, lambda s: s + 1)
    out = place_call(place, swapped(sent), out, lambda s: s * (here - 1))
    return out[:, :, :width]


def solution(mesh):
    placed = (
        P(("clips", "frame"), "seq", "head"),
        P(("clips", "frame"), "seq", "head"),
        P(("clips", "frame"), "seq", "head"),
        P("clips", None, None),
        P("clips", None, None),
        P("clips", None, None),
        P("clips", None, None),
    )
    return jax.shard_map(
        per_device,
        mesh=mesh,
        in_specs=placed,
        out_specs=P(("clips", "frame"), "seq", "head"),
        check_vma=False,
    )
```

time: 101 us -> 88.2 us (0.87)
  the two profiles are of different devices: /device:TPU:11 before, /device:TPU:19 now
where the time goes in v5:
time: 88.2 us; the launch traced here: 86.7 us
  Pallas kernels  61.6 us (70%)
  starting transfers between devices  10 us (11%)
  waiting for transfers between devices  7.65 us (9%)
  local copies, waits for them, and re-layouts  7.17 us (8%)
    pallas_call x2, Pallas kernels, near_call(): pl.pallas_call(functools.partial(near_kernel, lay, heads, whole), grid_sp...  37.5 us
    pallas_call x1, Pallas kernels, far_call(): pl.pallas_call(functools.partial(far_kernel, lay, heads), grid_spec=pltpu...  14 us
    ppermute x4, waiting for transfers between devices, paired(): lax.ppermute(block, 'frame', [p for i in pairs for p in ((i, i + 1), (i +...  6.86 us
    ppermute x4, starting transfers between devices, paired(): lax.ppermute(block, 'frame', [p for i in pairs for p in ((i, i + 1), (i +...  6.72 us
    dynamic_slice x3, local copies, waits for them, and re-layouts, exchanged(): return swapped(lax.dynamic_slice_in_dim(a, (1 - core) * part, part, axis=2))  5.48 us
    pallas_call x2, Pallas kernels, pack_call(): pl.pallas_call(functools.partial(pack_kernel, lay, begin, length), in_spe...  5.3 us
    ppermute x5, starting transfers between devices, swapped(): return lax.ppermute(block, 'seq', [(0, 1), (1, 0)])  3.32 us
    pallas_call x2, Pallas kernels, place_call(): pl.pallas_call(place_kernel, grid_spec=pltpu.PrefetchScalarGridSpec(num_s...  2.96 us
  transfers between devices with their start and end apart: 9, of which 5 were waited for; matrix products, arithmetic and copies ran while one was open for 3% of the time, Pallas kernels for 69%

profile of v5, /device:TPU:19, one launch (start us, length us, event | category | flops | bytes accessed | tf_op | source)
XLA Modules:
  0.0 86.7 jit_solution(5289514471164402566)
XLA Ops:
  0.0 2.9 %constant_dynamic-slice_fusion.1 = bf16[4,512,384]{2,1,0:T(8,128)(2,1)} fusion(bf16[4,512,768]{2,1,0:T(8,128)(2,1)} %param.9, s32[]{:T(128)S(6)} %select_n.2), kind=kLoop, calls=%fused_computation.1 | loop fusion | bytes 3145732 | tf_op jit(solution)/shard_map/dynamic_slice | solution.py:615
  2.9 0.7 collective-permute-start.1
  3.6 1.3 %constant_dynamic-slice_fusion.2 = bf16[4,512,384]{2,1,0:T(8,128)(2,1)} fusion(bf16[4,512,768]{2,1,0:T(8,128)(2,1)S(1)} %copy-done.7, s32[]{:T(128)S(6)} %select_n.2), kind=kLoop, calls=%fused_computation.2 | loop fusion | bytes 3145732 | tf_op jit(solution)/shard_map/dynamic_slice | solution.py:615
  4.9 0.1 collective-permute-start
  5.0 0.0 copy-done
  5.0 1.3 %constant_dynamic-slice_fusion = bf16[4,512,384]{2,1,0:T(8,128)(2,1)} fusion(bf16[4,512,768]{2,1,0:T(8,128)(2,1)S(1)} %copy-done, s32[]{:T(128)S(6)} %select_n.2), kind=kLoop, calls=%fused_computation | loop fusion | bytes 3145732 | tf_op jit(solution)/shard_map/dynamic_slice | solution.py:615
  6.3 1.0 %collective-permute-start.2 = (bf16[4,512,384]{2,1,0:T(8,128)(2,1)}, bf16[4,512,384]{2,1,0:T(8,128)(2,1)S(1)}, u32[]{:S(2)}, u32[]{:S(2)}) collective-permute-start(bf16[4,512,384]{2,1,0:T(8,128)(2,1)} %constant_dynamic-slice_fusion), channel_id=1, source_target_pairs={{0,1},{1,0},{2,3},{3,2},{4,5},{5,4},{6,7},{7,6},{8,9},{9,8},{10,11... | collective-permute-start | bytes 4718600 | tf_op jit(solution)/shard_map/ppermute | solution.py:598
  7.3 0.1 pad_add_fusion.place_ref
  7.4 1.8 %tile_tables.1.table_ref = s32[216]{0:T(256)S(1)} custom-call(s32[2]{0:T(128)S(1)} %pad_add_fusion.place_ref, s32[2,4,16]{2,1,0:T(4,128)S(1)} %bitcast.10, s32[2,2,16]{2,1,0:T(2,128)S(1)} %bitcast.12, s32[2,1,16]{2,1,0:T(1,128)S(1)} %bitcast.13, s32[3,2,16]{2,1,0:T(2,128)S(1)} %bitcast.11), custom_call_target="tpu_custom_call" | custom-call | tf_op jit(solution)/shard_map/tile_tables/pallas_call | solution.py:130
  9.2 0.0 collective-permute-done.1
  9.2 0.0 collective-permute-done
  9.2 2.5 %pack_tiles.2 = (bf16[12,128,384]{2,1,0:T(8,128)(2,1)S(1)}, bf16[12,128,384]{2,1,0:T(8,128)(2,1)S(1)}) custom-call(s32[2]{0:T(128)S(1)} %pad_add_fusion.place_ref, s32[216]{0:T(256)S(1)} %tile_tables.1.table_ref, bf16[4,4,128,768]{3,2,1,0:T(8,128)(2,1)} %bitcast.14, bf16[4,4,128,384]{3,2,1,0:T(8,128)(2,1)} %bitcast.7.k_other.refs_1_, ...), custom_call_target="tpu_custom_call" | custom-call | tf_op jit(solution)/shard_map/pack_tiles/pallas_call | solution.py:171
  11.8 1.4 %collective-permute-start.3 = (bf16[12,128,384]{2,1,0:T(8,128)(2,1)S(1)}, bf16[12,128,384]{2,1,0:T(8,128)(2,1)S(1)}, u32[]{:S(2)}, u32[]{:S(2)}) collective-permute-start(bf16[12,128,384]{2,1,0:T(8,128)(2,1)S(1)} %get-tuple-element.28), channel_id=1, source_target_pairs={{0,4},{4,0},{8,12},{12,8},{1,5},{5,1},{9,13},{13,9},{2,6},{6,2},{1... | collective-permute-start | bytes 3538952 | tf_op jit(solution)/shard_map/ppermute | solution.py:594
  13.1 1.9 %collective-permute-start.4 = (bf16[12,128,384]{2,1,0:T(8,128)(2,1)S(1)}, bf16[12,128,384]{2,1,0:T(8,128)(2,1)}, u32[]{:S(2)}, u32[]{:S(2)}) collective-permute-start(bf16[12,128,384]{2,1,0:T(8,128)(2,1)S(1)} %get-tuple-element.29), channel_id=1, source_target_pairs={{4,8},{8,4},{5,9},{9,5},{6,10},{10,6},{7,11},{11,7},{20,24},{24,20... | collective-permute-start | bytes 3538952 | tf_op jit(solution)/shard_map/ppermute | solution.py:594
  15.0 2.8 %pack_tiles.3 = (bf16[12,128,384]{2,1,0:T(8,128)(2,1)S(1)}, bf16[12,128,384]{2,1,0:T(8,128)(2,1)S(1)}) custom-call(s32[2]{0:T(128)S(1)} %pad_add_fusion.place_ref, s32[216]{0:T(256)S(1)} %tile_tables.1.table_ref, bf16[4,4,128,768]{3,2,1,0:T(8,128)(2,1)} %bitcast.15, bf16[4,4,128,384]{3,2,1,0:T(8,128)(2,1)} %bitcast.7.k_other.refs_1_, ...), custom_call_target="tpu_custom_call" | custom-call | tf_op jit(solution)/shard_map/pack_tiles/pallas_call | solution.py:171
  17.8 0.2 collective-permute-start.5
  18.0 3.3 %collective-permute-start.6 = (bf16[12,128,384]{2,1,0:T(8,128)(2,1)S(1)}, bf16[12,128,384]{2,1,0:T(8,128)(2,1)}, u32[]{:S(2)}, u32[]{:S(2)}) collective-permute-start(bf16[12,128,384]{2,1,0:T(8,128)(2,1)S(1)} %get-tuple-element.35), channel_id=1, source_target_pairs={{4,8},{8,4},{5,9},{9,5},{6,10},{10,6},{7,11},{11,7},{20,24},{24,20... | collective-permute-start | bytes 3538952 | tf_op jit(solution)/shard_map/ppermute | solution.py:594
  21.3 0.0 collective-permute-done.2.q_other
  21.3 15.9 %attend_edges.1 = (f32[2,6,512,128]{3,2,1,0:T(8,128)S(1)}, f32[2,512,128]{2,1,0:T(8,128)S(1)}) custom-call(s32[2]{0:T(128)S(1)} %pad_add_fusion.place_ref, s32[216]{0:T(256)S(1)} %tile_tables.1.table_ref, bf16[4,512,768]{2,1,0:T(8,128)(2,1)} %q_own.5, bf16[4,512,384]{2,1,0:T(8,128)(2,1)S(1)} %collective-permute-done.2.q_other, ...), custom_call_target="tpu_custom_call" | custom-call | flops 6442450944 | bytes 1572864 | tf_op jit(solution)/shard_map/attend_edges/pallas_call | solution.py:468
  37.2 1.6 %copy-done.2 = f32[2,6,512,128]{3,2,1,0:T(8,128)} copy-done((f32[2,6,512,128]{3,2,1,0:T(8,128)}, f32[2,6,512,128]{3,2,1,0:T(8,128)S(1)}, u32[]{:S(2)}) %copy-start.2) | copy-done | bytes 3145752
  38.8 0.3 collective-permute-done.3.refs_4_
  39.2 2.9 %collective-permute-done.4.refs_5_ = bf16[12,128,384]{2,1,0:T(8,128)(2,1)} collective-permute-done((bf16[12,128,384]{2,1,0:T(8,128)(2,1)S(1)}, bf16[12,128,384]{2,1,0:T(8,128)(2,1)}, u32[]{:S(2)}, u32[]{:S(2)}) %collective-permute-start.4) | collective-permute-done | bytes 1179680 | tf_op jit(solution)/shard_map/ppermute | solution.py:594
  42.0 21.6 %attend_middle.1 = (bf16[4,512,768]{2,1,0:T(8,128)(2,1)}, bf16[2,512,384]{2,1,0:T(8,128)(2,1)S(1)}) custom-call(s32[2]{0:T(128)S(1)} %pad_add_fusion.place_ref, s32[216]{0:T(256)S(1)} %tile_tables.1.table_ref, bf16[4,512,768]{2,1,0:T(8,128)(2,1)S(1)} %copy-done.1, bf16[4,512,384]{2,1,0:T(8,128)(2,1)S(1)} %collective-permute-done.2.q_other, ...), custom_call_target="tpu_custom_call" | custom-call | flops 6442450944 | bytes 1572864 | tf_op jit(solution)/shard_map/attend_middle/pallas_call | solution.py:468
  63.7 0.8 collective-permute-done.5.refs_6_
  64.4 2.9 %collective-permute-done.6.refs_7_ = bf16[12,128,384]{2,1,0:T(8,128)(2,1)} collective-permute-done((bf16[12,128,384]{2,1,0:T(8,128)(2,1)S(1)}, bf16[12,128,384]{2,1,0:T(8,128)(2,1)}, u32[]{:S(2)}, u32[]{:S(2)}) %collective-permute-start.6) | collective-permute-done | bytes 1179680 | tf_op jit(solution)/shard_map/ppermute | solution.py:594
  67.3 1.5 %collective-permute-start.8 = (bf16[2,512,384]{2,1,0:T(8,128)(2,1)S(1)}, bf16[2,512,384]{2,1,0:T(8,128)(2,1)S(1)}, u32[]{:S(2)}, u32[]{:S(2)}) collective-permute-start(bf16[2,512,384]{2,1,0:T(8,128)(2,1)S(1)} %get-tuple-element.41), channel_id=1, source_target_pairs={{0,1},{1,0},{2,3},{3,2},{4,5},{5,4},{6,7},{7,6},{8,9},{9,8},{10,11... | collective-permute-start | bytes 2359304 | tf_op jit(solution)/shard_map/ppermute | solution.py:598
  68.8 14.0 %attend_late.1 = (bf16[4,512,768]{2,1,0:T(8,128)(2,1)}, bf16[2,512,384]{2,1,0:T(8,128)(2,1)S(1)}) custom-call(s32[2]{0:T(128)S(1)} %pad_add_fusion.place_ref, s32[216]{0:T(256)S(1)} %tile_tables.1.table_ref, bf16[4,512,768]{2,1,0:T(8,128)(2,1)S(1)} %copy-done.1, ...), custom_call_target="tpu_custom_call", output_to_operand_aliasing={{0}: (14, {})} | custom-call | flops 2818572288 | bytes 688128 | tf_op jit(solution)/shard_map/attend_late/pallas_call | solution.py:534
  82.8 0.1 collective-permute-start.7
  82.9 0.0 collective-permute-done.8.block_ref
  82.9 1.5 %place_columns.2._ = bf16[4,512,768]{2,1,0:T(8,128)(2,1)} custom-call(s32[2]{0:T(128)S(1)} %pad_add_fusion.place_ref, bf16[2,512,384]{2,1,0:T(8,128)(2,1)S(1)} %collective-permute-done.8.block_ref, bf16[4,512,768]{2,1,0:T(8,128)(2,1)} %get-tuple-element.42._), custom_call_target="tpu_custom_call", output_to_operand_aliasing={{}: (2, {})} | custom-call | tf_op jit(solution)/shard_map/place_columns/pallas_call | solution.py:573
  84.4 0.8 collective-permute-done.7.block_ref
  85.2 1.5 %place_columns.3 = bf16[4,512,768]{2,1,0:T(8,128)(2,1)} custom-call(s32[2]{0:T(128)S(1)} %pad_add_fusion.place_ref, bf16[2,512,384]{2,1,0:T(8,128)(2,1)S(1)} %collective-permute-done.7.block_ref, bf16[4,512,768]{2,1,0:T(8,128)(2,1)} %place_columns.2._), custom_call_target="tpu_custom_call", output_to_operand_aliasing={{}: (2, {})} | custom-call | tf_op jit(solution)/shard_map/place_columns/pallas_call | solution.py:573
  (16 shorter events, 0.0 us)
Async XLA Ops:
  0.0 3.6 %copy-start.7 = (bf16[4,512,768]{2,1,0:T(8,128)(2,1)S(1)}, bf16[4,512,768]{2,1,0:T(8,128)(2,1)}, u32[]{:S(2)}) copy-start(bf16[4,512,768]{2,1,0:T(8,128)(2,1)} %param.8) | copy-start | bytes 9437188
  2.9 2.1 %copy-start = (bf16[4,512,768]{2,1,0:T(8,128)(2,1)S(1)}, bf16[4,512,768]{2,1,0:T(8,128)(2,1)}, u32[]{:S(2)}) copy-start(bf16[4,512,768]{2,1,0:T(8,128)(2,1)} %q_own.5) | copy-start | bytes 9437188
  2.9 6.3 %collective-permute-start.1 = (bf16[4,512,384]{2,1,0:T(8,128)(2,1)}, bf16[4,512,384]{2,1,0:T(8,128)(2,1)}, u32[]{:S(2)}, u32[]{:S(2)}) collective-permute-start(bf16[4,512,384]{2,1,0:T(8,128)(2,1)} %constant_dynamic-slice_fusion.1), channel_id=1, source_target_pairs={{0,1},{1,0},{2,3},{3,2},{4,5},{5,4},{6,7},{7,6},{8,9},{9,8},{10,11... | collective-permute-start | bytes 4718600 | tf_op jit(solution)/shard_map/ppermute | solution.py:598
  4.9 2.5 %copy-start.3 = (s32[16,2,4]{0,2,1:T(4,128)S(1)}, s32[16,2,4]{0,2,1:T(4,128)}, u32[]{:S(2)}) copy-start(s32[16,2,4]{0,2,1:T(4,128)} %param.10) | copy-start | bytes 1540
  4.9 2.5 %copy-start.4 = (s32[16,2,3]{0,1,2:T(2,128)S(1)}, s32[16,2,3]{0,1,2:T(2,128)}, u32[]{:S(2)}) copy-start(s32[16,2,3]{0,1,2:T(2,128)} %param.13) | copy-start | bytes 1156
  4.9 2.5 %copy-start.5 = (s32[16,2,2]{0,2,1:T(2,128)S(1)}, s32[16,2,2]{0,2,1:T(2,128)}, u32[]{:S(2)}) copy-start(s32[16,2,2]{0,2,1:T(2,128)} %param.11) | copy-start | bytes 772
  4.9 2.5 %copy-start.6 = (s32[16,2,1]{0,2,1:T(1,128)S(1)}, s32[16,2,1]{0,2,1:T(1,128)}, u32[]{:S(2)}) copy-start(s32[16,2,1]{0,2,1:T(1,128)} %param.12) | copy-start | bytes 388
  4.9 4.4 %collective-permute-start = (bf16[4,512,384]{2,1,0:T(8,128)(2,1)}, bf16[4,512,384]{2,1,0:T(8,128)(2,1)}, u32[]{:S(2)}, u32[]{:S(2)}) collective-permute-start(bf16[4,512,384]{2,1,0:T(8,128)(2,1)} %constant_dynamic-slice_fusion.2), channel_id=1, source_target_pairs={{0,1},{1,0},{2,3},{3,2},{4,5},{5,4},{6,7},{7,6},{8,9},{9,8},{10,11... | collective-permute-start | bytes 4718600 | tf_op jit(solution)/shard_map/ppermute | solution.py:598
  6.3 15.0 %collective-permute-start.2 = (bf16[4,512,384]{2,1,0:T(8,128)(2,1)}, bf16[4,512,384]{2,1,0:T(8,128)(2,1)S(1)}, u32[]{:S(2)}, u32[]{:S(2)}) collective-permute-start(bf16[4,512,384]{2,1,0:T(8,128)(2,1)} %constant_dynamic-slice_fusion), channel_id=1, source_target_pairs={{0,1},{1,0},{2,3},{3,2},{4,5},{5,4},{6,7},{7,6},{8,9},{9,8},{10,11... | collective-permute-start | bytes 4718600 | tf_op jit(solution)/shard_map/ppermute | solution.py:598
  11.8 27.4 %collective-permute-start.3 = (bf16[12,128,384]{2,1,0:T(8,128)(2,1)S(1)}, bf16[12,128,384]{2,1,0:T(8,128)(2,1)S(1)}, u32[]{:S(2)}, u32[]{:S(2)}) collective-permute-start(bf16[12,128,384]{2,1,0:T(8,128)(2,1)S(1)} %get-tuple-element.28), channel_id=1, source_target_pairs={{0,4},{4,0},{8,12},{12,8},{1,5},{5,1},{9,13},{13,9},{2,6},{6,2},{1... | collective-permute-start | bytes 3538952 | tf_op jit(solution)/shard_map/ppermute | solution.py:594
  13.1 28.9 %collective-permute-start.4 = (bf16[12,128,384]{2,1,0:T(8,128)(2,1)S(1)}, bf16[12,128,384]{2,1,0:T(8,128)(2,1)}, u32[]{:S(2)}, u32[]{:S(2)}) collective-permute-start(bf16[12,128,384]{2,1,0:T(8,128)(2,1)S(1)} %get-tuple-element.29), channel_id=1, source_target_pairs={{4,8},{8,4},{5,9},{9,5},{6,10},{10,6},{7,11},{11,7},{20,24},{24,20... | collective-permute-start | bytes 3538952 | tf_op jit(solution)/shard_map/ppermute | solution.py:594
  17.8 46.6 %collective-permute-start.5 = (bf16[12,128,384]{2,1,0:T(8,128)(2,1)S(1)}, bf16[12,128,384]{2,1,0:T(8,128)(2,1)}, u32[]{:S(2)}, u32[]{:S(2)}) collective-permute-start(bf16[12,128,384]{2,1,0:T(8,128)(2,1)S(1)} %get-tuple-element.34), channel_id=1, source_target_pairs={{0,4},{4,0},{8,12},{12,8},{1,5},{5,1},{9,13},{13,9},{2,6},{6,2},{1... | collective-permute-start | bytes 3538952 | tf_op jit(solution)/shard_map/ppermute | solution.py:594
  18.0 24.0 %copy-start.1 = (bf16[4,512,768]{2,1,0:T(8,128)(2,1)S(1)}, bf16[4,512,768]{2,1,0:T(8,128)(2,1)}, u32[]{:S(2)}) copy-start(bf16[4,512,768]{2,1,0:T(8,128)(2,1)} %q_own.5) | copy-start | bytes 9437188
  18.0 49.3 %collective-permute-start.6 = (bf16[12,128,384]{2,1,0:T(8,128)(2,1)S(1)}, bf16[12,128,384]{2,1,0:T(8,128)(2,1)}, u32[]{:S(2)}, u32[]{:S(2)}) collective-permute-start(bf16[12,128,384]{2,1,0:T(8,128)(2,1)S(1)} %get-tuple-element.35), channel_id=1, source_target_pairs={{4,8},{8,4},{5,9},{9,5},{6,10},{10,6},{7,11},{11,7},{20,24},{24,20... | collective-permute-start | bytes 3538952 | tf_op jit(solution)/shard_map/ppermute | solution.py:594
  37.2 1.6 %copy-start.2 = (f32[2,6,512,128]{3,2,1,0:T(8,128)}, f32[2,6,512,128]{3,2,1,0:T(8,128)S(1)}, u32[]{:S(2)}) copy-start(f32[2,6,512,128]{3,2,1,0:T(8,128)S(1)} %get-tuple-element.27.acc_ref) | copy-start | bytes 9437188
  39.2 2.9 %copy-start.8 = (bf16[12,128,384]{2,1,0:T(8,128)(2,1)}, bf16[12,128,384]{2,1,0:T(8,128)(2,1)S(1)}, u32[]{:S(2)}) copy-start(bf16[12,128,384]{2,1,0:T(8,128)(2,1)S(1)} %collective-permute-done.3.refs_4_) | copy-start | bytes 3538948
  67.3 15.6 %collective-permute-start.8 = (bf16[2,512,384]{2,1,0:T(8,128)(2,1)S(1)}, bf16[2,512,384]{2,1,0:T(8,128)(2,1)S(1)}, u32[]{:S(2)}, u32[]{:S(2)}) collective-permute-start(bf16[2,512,384]{2,1,0:T(8,128)(2,1)S(1)} %get-tuple-element.41), channel_id=1, source_target_pairs={{0,1},{1,0},{2,3},{3,2},{4,5},{5,4},{6,7},{7,6},{8,9},{9,8},{10,11... | collective-permute-start | bytes 2359304 | tf_op jit(solution)/shard_map/ppermute | solution.py:598
  82.8 2.4 %collective-permute-start.7 = (bf16[2,512,384]{2,1,0:T(8,128)(2,1)S(1)}, bf16[2,512,384]{2,1,0:T(8,128)(2,1)S(1)}, u32[]{:S(2)}, u32[]{:S(2)}) collective-permute-start(bf16[2,512,384]{2,1,0:T(8,128)(2,1)S(1)} %get-tuple-element.40), channel_id=1, source_target_pairs={{0,1},{1,0},{2,3},{3,2},{4,5},{5,4},{6,7},{7,6},{8,9},{9,8},{10,11... | collective-permute-start | bytes 2359304 | tf_op jit(solution)/shard_map/ppermute | solution.py:598

commit v6 on v5

--- a/solution.py
+++ b/solution.py
@@ -93,7 +93,7 @@
     for direction in (0, 1):
         target = first + (lay.here if direction == 0 else -lay.here)
         target = jnp.clip(target, 0, lay.frames - lay.here)
-        begin = (odd + direction) % 2 * lay.places
+        begin = (odd + direction + 1) % 2 * lay.places
         for place in range(lay.places):
             table_ref[begin + place] = 0
 
@@ -103,7 +103,7 @@
         distinct(target, direction, lambda *_: None, note)
 
     for direction in (0, 1):
-        way = (odd + 1 - direction) % 2
+        way = (odd + direction) % 2
 
         def on_slot(frame, place, alive, way=way):
             if lay.edge(frame):
@@ -455,7 +455,7 @@
     sems = [pltpu.SemaphoreType.DMA((here, 4))]
     if whole:
         out_specs = [own, pl.BlockSpec((1, rows, width), lambda s, *_: (s, 0, 0))]
-        out_shape = [jax.ShapeDtypeStruct(queries[0].shape, BF), jax.ShapeDtypeStruct((steps, rows, width), BF)]
+        out_shape = [pltpu.HBM(queries[0].shape, BF), jax.ShapeDtypeStruct((steps, rows, width), BF)]
         scratch = [sums[0], *bufs, *sums, *sems]
         scratch += [pltpu.VMEM((TILE, width), BF)] * 2 + [pltpu.SemaphoreType.DMA((4,))]
     else:
@@ -463,7 +463,7 @@
             pl.BlockSpec((1, 2 * heads, rows, 128), lambda s, *_: (s, 0, 0, 0)),
             pl.BlockSpec((1, rows, 128), lambda s, *_: (s, 0, 0)),
         ]
-        out_shape = [jax.ShapeDtypeStruct((2, 2 * heads, rows, 128), F32), jax.ShapeDtypeStruct((2, rows, 128), F32)]
+        out_shape = [pltpu.HBM((2, 2 * heads, rows, 128), F32), pltpu.HBM((2, rows, 128), F32)]
         scratch = [*bufs, *sums, *sems]
     return pl.pallas_call(
         functools.partial(near_kernel, lay, heads, whole),
@@ -590,7 +590,7 @@
 
 
 def paired(block, way):
-    pairs = range(way, lax.axis_size("frame") - 1, 2)
+    pairs = range(1 - way, lax.axis_size("frame") - 1, 2)
     return lax.ppermute(block, "frame", [p for i in pairs for p in ((i, i + 1), (i + 1, i))])
 
 
@@ -634,10 +634,9 @@
     acc, stats = near_call(lay, heads, False, place, table, queries, local)
     early, stats = lax.optimization_barrier((early, stats))
     out, sent = near_call(lay, heads, True, place, table, queries, local, early)
-    late, sent = lax.optimization_barrier((late, sent))
-    middle = swapped(sent)
+    out = place_call(place, swapped(sent), out, lambda s: s + 1)
+    late, out = lax.optimization_barrier((late, out))
     out, sent = far_call(lay, heads, place, table, queries, acc, stats, local, early, late, out)
-    out = place_call(place, middle, out, lambda s: s + 1)
     out = place_call(place, swapped(sent), out, lambda s: s * (here - 1))
     return out[:, :, :width]
 

time: 88.2 us -> 93.8 us (1.063)
  the two profiles are of different devices: /device:TPU:19 before, /device:TPU:15 now
where the time goes in v6:
time: 93.8 us; the launch traced here: 93.5 us
  Pallas kernels  65.2 us (70%)
  starting transfers between devices  10.3 us (11%)
  waiting for transfers between devices  9.83 us (10%)
  local copies, waits for them, and re-layouts  7.94 us (8%)
    pallas_call x2, Pallas kernels, near_call(): pl.pallas_call(functools.partial(near_kernel, lay, heads, whole), grid_sp...  40.1 us
    pallas_call x1, Pallas kernels, far_call(): pl.pallas_call(functools.partial(far_kernel, lay, heads), grid_spec=pltpu...  15.3 us
    ppermute x4, waiting for transfers between devices, paired(): lax.ppermute(block, 'frame', [p for i in pairs for p in ((i, i + 1), (i +...  6 us
    dynamic_slice x3, local copies, waits for them, and re-layouts, exchanged(): return swapped(lax.dynamic_slice_in_dim(a, (1 - core) * part, part, axis=2))  5.48 us
    ppermute x4, starting transfers between devices, paired(): lax.ppermute(block, 'frame', [p for i in pairs for p in ((i, i + 1), (i +...  5.45 us
    pallas_call x2, Pallas kernels, pack_call(): pl.pallas_call(functools.partial(pack_kernel, lay, begin, length), in_spe...  5.11 us
    ppermute x5, starting transfers between devices, swapped(): return lax.ppermute(block, 'seq', [(0, 1), (1, 0)])  4.85 us
    ppermute x5, waiting for transfers between devices, swapped(): return lax.ppermute(block, 'seq', [(0, 1), (1, 0)])  3.83 us
  transfers between devices with their start and end apart: 9, of which 4 were waited for; matrix products, arithmetic and copies ran while one was open for 3% of the time, Pallas kernels for 52%

profile of v6, /device:TPU:15, one launch (start us, length us, event | category | flops | bytes accessed | tf_op | source)
XLA Modules:
  0.0 93.5 jit_solution(15570619312505105317)
XLA Ops:
  0.0 2.9 %constant_dynamic-slice_fusion.1 = bf16[4,512,384]{2,1,0:T(8,128)(2,1)} fusion(bf16[4,512,768]{2,1,0:T(8,128)(2,1)} %param.9, s32[]{:T(128)S(6)} %select_n.2), kind=kLoop, calls=%fused_computation.1 | loop fusion | bytes 3145732 | tf_op jit(solution)/shard_map/dynamic_slice | solution.py:615
  2.9 0.7 collective-permute-start.1
  3.6 1.3 %constant_dynamic-slice_fusion.2 = bf16[4,512,384]{2,1,0:T(8,128)(2,1)} fusion(bf16[4,512,768]{2,1,0:T(8,128)(2,1)S(1)} %copy-done.6, s32[]{:T(128)S(6)} %select_n.2), kind=kLoop, calls=%fused_computation.2 | loop fusion | bytes 3145732 | tf_op jit(solution)/shard_map/dynamic_slice | solution.py:615
  4.9 0.1 collective-permute-start
  5.0 0.0 copy-done
  5.0 1.3 %constant_dynamic-slice_fusion = bf16[4,512,384]{2,1,0:T(8,128)(2,1)} fusion(bf16[4,512,768]{2,1,0:T(8,128)(2,1)S(1)} %copy-done, s32[]{:T(128)S(6)} %select_n.2), kind=kLoop, calls=%fused_computation | loop fusion | bytes 3145732 | tf_op jit(solution)/shard_map/dynamic_slice | solution.py:615
  6.3 1.0 %collective-permute-start.2 = (bf16[4,512,384]{2,1,0:T(8,128)(2,1)}, bf16[4,512,384]{2,1,0:T(8,128)(2,1)}, u32[]{:S(2)}, u32[]{:S(2)}) collective-permute-start(bf16[4,512,384]{2,1,0:T(8,128)(2,1)} %constant_dynamic-slice_fusion), channel_id=1, source_target_pairs={{0,1},{1,0},{2,3},{3,2},{4,5},{5,4},{6,7},{7,6},{8,9},{9,8},{10,11... | collective-permute-start | bytes 4718600 | tf_op jit(solution)/shard_map/ppermute | solution.py:598
  7.3 0.1 pad_add_fusion.place_ref
  7.4 1.8 %tile_tables.1.table_ref = s32[216]{0:T(256)S(1)} custom-call(s32[2]{0:T(128)S(1)} %pad_add_fusion.place_ref, s32[2,4,16]{2,1,0:T(4,128)S(1)} %bitcast.10, s32[2,2,16]{2,1,0:T(2,128)S(1)} %bitcast.12, s32[2,1,16]{2,1,0:T(1,128)S(1)} %bitcast.13, s32[3,2,16]{2,1,0:T(2,128)S(1)} %bitcast.11), custom_call_target="tpu_custom_call" | custom-call | tf_op jit(solution)/shard_map/tile_tables/pallas_call | solution.py:130
  9.2 0.0 collective-permute-done.1
  9.2 0.0 collective-permute-done
  9.2 2.5 %pack_tiles.2 = (bf16[12,128,384]{2,1,0:T(8,128)(2,1)S(1)}, bf16[12,128,384]{2,1,0:T(8,128)(2,1)S(1)}) custom-call(s32[2]{0:T(128)S(1)} %pad_add_fusion.place_ref, s32[216]{0:T(256)S(1)} %tile_tables.1.table_ref, bf16[4,4,128,768]{3,2,1,0:T(8,128)(2,1)} %bitcast.14, bf16[4,4,128,384]{3,2,1,0:T(8,128)(2,1)} %bitcast.7.k_other.refs_1_, ...), custom_call_target="tpu_custom_call" | custom-call | tf_op jit(solution)/shard_map/pack_tiles/pallas_call | solution.py:171
  11.7 3.2 %collective-permute-start.3 = (bf16[12,128,384]{2,1,0:T(8,128)(2,1)S(1)}, bf16[12,128,384]{2,1,0:T(8,128)(2,1)S(1)}, u32[]{:S(2)}, u32[]{:S(2)}) collective-permute-start(bf16[12,128,384]{2,1,0:T(8,128)(2,1)S(1)} %get-tuple-element.28), channel_id=1, source_target_pairs={{4,8},{8,4},{5,9},{9,5},{6,10},{10,6},{7,11},{11,7},{20,24},{24,20... | collective-permute-start | bytes 3538952 | tf_op jit(solution)/shard_map/ppermute | solution.py:594
  15.0 0.1 collective-permute-start.4
  15.0 2.6 %pack_tiles.3 = (bf16[12,128,384]{2,1,0:T(8,128)(2,1)S(1)}, bf16[12,128,384]{2,1,0:T(8,128)(2,1)S(1)}) custom-call(s32[2]{0:T(128)S(1)} %pad_add_fusion.place_ref, s32[216]{0:T(256)S(1)} %tile_tables.1.table_ref, bf16[4,4,128,768]{3,2,1,0:T(8,128)(2,1)} %bitcast.15, bf16[4,4,128,384]{3,2,1,0:T(8,128)(2,1)} %bitcast.7.k_other.refs_1_, ...), custom_call_target="tpu_custom_call" | custom-call | tf_op jit(solution)/shard_map/pack_tiles/pallas_call | solution.py:171
  17.6 2.0 %collective-permute-start.5 = (bf16[12,128,384]{2,1,0:T(8,128)(2,1)S(1)}, bf16[12,128,384]{2,1,0:T(8,128)(2,1)S(1)}, u32[]{:S(2)}, u32[]{:S(2)}) collective-permute-start(bf16[12,128,384]{2,1,0:T(8,128)(2,1)S(1)} %get-tuple-element.34), channel_id=1, source_target_pairs={{4,8},{8,4},{5,9},{9,5},{6,10},{10,6},{7,11},{11,7},{20,24},{24,20... | collective-permute-start | bytes 3538952 | tf_op jit(solution)/shard_map/ppermute | solution.py:594
  19.6 0.2 collective-permute-start.6
  19.8 16.1 %attend_edges.1 = (f32[2,6,512,128]{3,2,1,0:T(8,128)}, f32[2,512,128]{2,1,0:T(8,128)}) custom-call(s32[2]{0:T(128)S(1)} %pad_add_fusion.place_ref, s32[216]{0:T(256)S(1)} %tile_tables.1.table_ref, bf16[4,512,768]{2,1,0:T(8,128)(2,1)S(1)} %copy-done, bf16[4,512,384]{2,1,0:T(8,128)(2,1)} %collective-permute-done.2.q_other, bf16[4,4,128,768]{3,2,1,0:T(8,128)(2,1)} %bitcast.16, ...), custom_call_target="tpu_custom_call" | custom-call | flops 6442450944 | bytes 1572864 | tf_op jit(solution)/shard_map/attend_edges/pallas_call | solution.py:468
  35.9 4.9 %collective-permute-done.3.refs_4_ = bf16[12,128,384]{2,1,0:T(8,128)(2,1)S(1)} collective-permute-done((bf16[12,128,384]{2,1,0:T(8,128)(2,1)S(1)}, bf16[12,128,384]{2,1,0:T(8,128)(2,1)S(1)}, u32[]{:S(2)}, u32[]{:S(2)}) %collective-permute-start.3) | collective-permute-done | bytes 1179680 | tf_op jit(solution)/shard_map/ppermute | solution.py:594
  40.9 1.1 %collective-permute-done.4.refs_5_ = bf16[12,128,384]{2,1,0:T(8,128)(2,1)S(1)} collective-permute-done((bf16[12,128,384]{2,1,0:T(8,128)(2,1)S(1)}, bf16[12,128,384]{2,1,0:T(8,128)(2,1)S(1)}, u32[]{:S(2)}, u32[]{:S(2)}) %collective-permute-start.4) | collective-permute-done | bytes 1179680 | tf_op jit(solution)/shard_map/ppermute | solution.py:594
  41.9 0.0 copy-done.7
  42.0 1.0 %copy-done.8 = bf16[12,128,384]{2,1,0:T(8,128)(2,1)} copy-done((bf16[12,128,384]{2,1,0:T(8,128)(2,1)}, bf16[12,128,384]{2,1,0:T(8,128)(2,1)S(1)}, u32[]{:S(2)}) %copy-start.8) | copy-done | bytes 1179672
  42.9 24.0 %attend_middle.1 = (bf16[4,512,768]{2,1,0:T(8,128)(2,1)}, bf16[2,512,384]{2,1,0:T(8,128)(2,1)S(1)}) custom-call(s32[2]{0:T(128)S(1)} %pad_add_fusion.place_ref, s32[216]{0:T(256)S(1)} %tile_tables.1.table_ref, bf16[4,512,768]{2,1,0:T(8,128)(2,1)S(1)} %copy-done, bf16[4,512,384]{2,1,0:T(8,128)(2,1)} %collective-permute-done.2.q_other, ...), custom_call_target="tpu_custom_call" | custom-call | flops 6442450944 | bytes 1572864 | tf_op jit(solution)/shard_map/attend_middle/pallas_call | solution.py:468
  66.9 2.6 %collective-permute-start.7 = (bf16[2,512,384]{2,1,0:T(8,128)(2,1)S(1)}, bf16[2,512,384]{2,1,0:T(8,128)(2,1)S(1)}, u32[]{:S(2)}, u32[]{:S(2)}) collective-permute-start(bf16[2,512,384]{2,1,0:T(8,128)(2,1)S(1)} %get-tuple-element.36), channel_id=1, source_target_pairs={{0,1},{1,0},{2,3},{3,2},{4,5},{5,4},{6,7},{7,6},{8,9},{9,8},{10,11... | collective-permute-start | bytes 2359304 | tf_op jit(solution)/shard_map/ppermute | solution.py:598
  69.5 1.9 %collective-permute-done.7.block_ref = bf16[2,512,384]{2,1,0:T(8,128)(2,1)S(1)} collective-permute-done((bf16[2,512,384]{2,1,0:T(8,128)(2,1)S(1)}, bf16[2,512,384]{2,1,0:T(8,128)(2,1)S(1)}, u32[]{:S(2)}, u32[]{:S(2)}) %collective-permute-start.7) | collective-permute-done | bytes 786464 | tf_op jit(solution)/shard_map/ppermute | solution.py:598
  71.4 1.5 %place_columns.2.refs_8_ = bf16[4,512,768]{2,1,0:T(8,128)(2,1)} custom-call(s32[2]{0:T(128)S(1)} %pad_add_fusion.place_ref, bf16[2,512,384]{2,1,0:T(8,128)(2,1)S(1)} %collective-permute-done.7.block_ref, bf16[4,512,768]{2,1,0:T(8,128)(2,1)} %get-tuple-element.37._), custom_call_target="tpu_custom_call", output_to_operand_aliasing={{}: (2, {})} | custom-call | tf_op jit(solution)/shard_map/place_columns/pallas_call | solution.py:573
  72.9 1.0 %copy-done.9 = bf16[12,128,384]{2,1,0:T(8,128)(2,1)} copy-done((bf16[12,128,384]{2,1,0:T(8,128)(2,1)}, bf16[12,128,384]{2,1,0:T(8,128)(2,1)S(1)}, u32[]{:S(2)}) %copy-start.9) | copy-done | bytes 1179672
  74.0 0.4 copy-done.10
  74.4 15.3 %attend_late.1 = (bf16[4,512,768]{2,1,0:T(8,128)(2,1)}, bf16[2,512,384]{2,1,0:T(8,128)(2,1)S(1)}) custom-call(s32[2]{0:T(128)S(1)} %pad_add_fusion.place_ref, s32[216]{0:T(256)S(1)} %tile_tables.1.table_ref, bf16[4,512,768]{2,1,0:T(8,128)(2,1)S(1)} %copy-done, bf16[4,512,384]{2,1,0:T(8,128)(2,1)} %collective-permute-done.2.q_other, ...), custom_call_target="tpu_custom_call", output_to_operand_aliasing={{0}: (14, {})} | custom-call | flops 2818572288 | bytes 688128 | tf_op jit(solution)/shard_map/attend_late/pallas_call | solution.py:534
  89.7 0.4 collective-permute-start.8
  90.1 1.9 %collective-permute-done.8.block_ref = bf16[2,512,384]{2,1,0:T(8,128)(2,1)S(1)} collective-permute-done((bf16[2,512,384]{2,1,0:T(8,128)(2,1)S(1)}, bf16[2,512,384]{2,1,0:T(8,128)(2,1)S(1)}, u32[]{:S(2)}, u32[]{:S(2)}) %collective-permute-start.8) | collective-permute-done | bytes 786464 | tf_op jit(solution)/shard_map/ppermute | solution.py:598
  92.0 1.5 %place_columns.3 = bf16[4,512,768]{2,1,0:T(8,128)(2,1)} custom-call(s32[2]{0:T(128)S(1)} %pad_add_fusion.place_ref, bf16[2,512,384]{2,1,0:T(8,128)(2,1)S(1)} %collective-permute-done.8.block_ref, bf16[4,512,768]{2,1,0:T(8,128)(2,1)} %get-tuple-element.42._), custom_call_target="tpu_custom_call", output_to_operand_aliasing={{}: (2, {})} | custom-call | tf_op jit(solution)/shard_map/place_columns/pallas_call | solution.py:573
  (20 shorter events, 0.0 us)
Async XLA Ops:
  0.0 3.6 %copy-start.6 = (bf16[4,512,768]{2,1,0:T(8,128)(2,1)S(1)}, bf16[4,512,768]{2,1,0:T(8,128)(2,1)}, u32[]{:S(2)}) copy-start(bf16[4,512,768]{2,1,0:T(8,128)(2,1)} %param.8) | copy-start | bytes 9437188
  2.9 2.1 %copy-start = (bf16[4,512,768]{2,1,0:T(8,128)(2,1)S(1)}, bf16[4,512,768]{2,1,0:T(8,128)(2,1)}, u32[]{:S(2)}) copy-start(bf16[4,512,768]{2,1,0:T(8,128)(2,1)} %q_own.5) | copy-start | bytes 9437188
  2.9 6.3 %collective-permute-start.1 = (bf16[4,512,384]{2,1,0:T(8,128)(2,1)}, bf16[4,512,384]{2,1,0:T(8,128)(2,1)}, u32[]{:S(2)}, u32[]{:S(2)}) collective-permute-start(bf16[4,512,384]{2,1,0:T(8,128)(2,1)} %constant_dynamic-slice_fusion.1), channel_id=1, source_target_pairs={{0,1},{1,0},{2,3},{3,2},{4,5},{5,4},{6,7},{7,6},{8,9},{9,8},{10,11... | collective-permute-start | bytes 4718600 | tf_op jit(solution)/shard_map/ppermute | solution.py:598
  4.9 2.5 %copy-start.2 = (s32[16,2,4]{0,2,1:T(4,128)S(1)}, s32[16,2,4]{0,2,1:T(4,128)}, u32[]{:S(2)}) copy-start(s32[16,2,4]{0,2,1:T(4,128)} %param.10) | copy-start | bytes 1540
  4.9 2.5 %copy-start.3 = (s32[16,2,3]{0,1,2:T(2,128)S(1)}, s32[16,2,3]{0,1,2:T(2,128)}, u32[]{:S(2)}) copy-start(s32[16,2,3]{0,1,2:T(2,128)} %param.13) | copy-start | bytes 1156
  4.9 2.5 %copy-start.4 = (s32[16,2,2]{0,2,1:T(2,128)S(1)}, s32[16,2,2]{0,2,1:T(2,128)}, u32[]{:S(2)}) copy-start(s32[16,2,2]{0,2,1:T(2,128)} %param.11) | copy-start | bytes 772
  4.9 2.5 %copy-start.5 = (s32[16,2,1]{0,2,1:T(1,128)S(1)}, s32[16,2,1]{0,2,1:T(1,128)}, u32[]{:S(2)}) copy-start(s32[16,2,1]{0,2,1:T(1,128)} %param.12) | copy-start | bytes 388
  4.9 4.3 %collective-permute-start = (bf16[4,512,384]{2,1,0:T(8,128)(2,1)}, bf16[4,512,384]{2,1,0:T(8,128)(2,1)}, u32[]{:S(2)}, u32[]{:S(2)}) collective-permute-start(bf16[4,512,384]{2,1,0:T(8,128)(2,1)} %constant_dynamic-slice_fusion.2), channel_id=1, source_target_pairs={{0,1},{1,0},{2,3},{3,2},{4,5},{5,4},{6,7},{7,6},{8,9},{9,8},{10,11... | collective-permute-start | bytes 4718600 | tf_op jit(solution)/shard_map/ppermute | solution.py:598
  6.3 13.5 %collective-permute-start.2 = (bf16[4,512,384]{2,1,0:T(8,128)(2,1)}, bf16[4,512,384]{2,1,0:T(8,128)(2,1)}, u32[]{:S(2)}, u32[]{:S(2)}) collective-permute-start(bf16[4,512,384]{2,1,0:T(8,128)(2,1)} %constant_dynamic-slice_fusion), channel_id=1, source_target_pairs={{0,1},{1,0},{2,3},{3,2},{4,5},{5,4},{6,7},{7,6},{8,9},{9,8},{10,11... | collective-permute-start | bytes 4718600 | tf_op jit(solution)/shard_map/ppermute | solution.py:598
  11.7 29.1 %collective-permute-start.3 = (bf16[12,128,384]{2,1,0:T(8,128)(2,1)S(1)}, bf16[12,128,384]{2,1,0:T(8,128)(2,1)S(1)}, u32[]{:S(2)}, u32[]{:S(2)}) collective-permute-start(bf16[12,128,384]{2,1,0:T(8,128)(2,1)S(1)} %get-tuple-element.28), channel_id=1, source_target_pairs={{4,8},{8,4},{5,9},{9,5},{6,10},{10,6},{7,11},{11,7},{20,24},{24,20... | collective-permute-start | bytes 3538952 | tf_op jit(solution)/shard_map/ppermute | solution.py:594
  15.0 27.0 %collective-permute-start.4 = (bf16[12,128,384]{2,1,0:T(8,128)(2,1)S(1)}, bf16[12,128,384]{2,1,0:T(8,128)(2,1)S(1)}, u32[]{:S(2)}, u32[]{:S(2)}) collective-permute-start(bf16[12,128,384]{2,1,0:T(8,128)(2,1)S(1)} %get-tuple-element.29), channel_id=1, source_target_pairs={{0,4},{4,0},{8,12},{12,8},{1,5},{5,1},{9,13},{13,9},{2,6},{6,2},{1... | collective-permute-start | bytes 3538952 | tf_op jit(solution)/shard_map/ppermute | solution.py:594
  17.6 55.3 %collective-permute-start.5 = (bf16[12,128,384]{2,1,0:T(8,128)(2,1)S(1)}, bf16[12,128,384]{2,1,0:T(8,128)(2,1)S(1)}, u32[]{:S(2)}, u32[]{:S(2)}) collective-permute-start(bf16[12,128,384]{2,1,0:T(8,128)(2,1)S(1)} %get-tuple-element.34), channel_id=1, source_target_pairs={{4,8},{8,4},{5,9},{9,5},{6,10},{10,6},{7,11},{11,7},{20,24},{24,20... | collective-permute-start | bytes 3538952 | tf_op jit(solution)/shard_map/ppermute | solution.py:594
  19.6 53.3 %collective-permute-start.6 = (bf16[12,128,384]{2,1,0:T(8,128)(2,1)S(1)}, bf16[12,128,384]{2,1,0:T(8,128)(2,1)S(1)}, u32[]{:S(2)}, u32[]{:S(2)}) collective-permute-start(bf16[12,128,384]{2,1,0:T(8,128)(2,1)S(1)} %get-tuple-element.35), channel_id=1, source_target_pairs={{0,4},{4,0},{8,12},{12,8},{1,5},{5,1},{9,13},{13,9},{2,6},{6,2},{1... | collective-permute-start | bytes 3538952 | tf_op jit(solution)/shard_map/ppermute | solution.py:594
  40.9 1.1 %copy-start.7 = (bf16[12,128,384]{2,1,0:T(8,128)(2,1)}, bf16[12,128,384]{2,1,0:T(8,128)(2,1)S(1)}, u32[]{:S(2)}) copy-start(bf16[12,128,384]{2,1,0:T(8,128)(2,1)S(1)} %collective-permute-done.3.refs_4_) | copy-start | bytes 3538948
  41.9 1.0 %copy-start.8 = (bf16[12,128,384]{2,1,0:T(8,128)(2,1)}, bf16[12,128,384]{2,1,0:T(8,128)(2,1)S(1)}, u32[]{:S(2)}) copy-start(bf16[12,128,384]{2,1,0:T(8,128)(2,1)S(1)} %collective-permute-done.4.refs_5_) | copy-start | bytes 3538948
  66.9 4.5 %collective-permute-start.7 = (bf16[2,512,384]{2,1,0:T(8,128)(2,1)S(1)}, bf16[2,512,384]{2,1,0:T(8,128)(2,1)S(1)}, u32[]{:S(2)}, u32[]{:S(2)}) collective-permute-start(bf16[2,512,384]{2,1,0:T(8,128)(2,1)S(1)} %get-tuple-element.36), channel_id=1, source_target_pairs={{0,1},{1,0},{2,3},{3,2},{4,5},{5,4},{6,7},{7,6},{8,9},{9,8},{10,11... | collective-permute-start | bytes 2359304 | tf_op jit(solution)/shard_map/ppermute | solution.py:598
  71.4 2.9 %copy-start.1 = (f32[2,512,128]{2,1,0:T(8,128)S(1)}, f32[2,512,128]{2,1,0:T(8,128)}, u32[]{:S(2)}) copy-start(f32[2,512,128]{2,1,0:T(8,128)} %get-tuple-element.31.stat_ref) | copy-start | bytes 1572868
  72.9 1.0 %copy-start.9 = (bf16[12,128,384]{2,1,0:T(8,128)(2,1)}, bf16[12,128,384]{2,1,0:T(8,128)(2,1)S(1)}, u32[]{:S(2)}) copy-start(bf16[12,128,384]{2,1,0:T(8,128)(2,1)S(1)} %collective-permute-done.5.refs_6_) | copy-start | bytes 3538948
  72.9 1.4 %copy-start.10 = (bf16[12,128,384]{2,1,0:T(8,128)(2,1)}, bf16[12,128,384]{2,1,0:T(8,128)(2,1)S(1)}, u32[]{:S(2)}) copy-start(bf16[12,128,384]{2,1,0:T(8,128)(2,1)S(1)} %collective-permute-done.6.refs_7_) | copy-start | bytes 3538948
  89.7 2.4 %collective-permute-start.8 = (bf16[2,512,384]{2,1,0:T(8,128)(2,1)S(1)}, bf16[2,512,384]{2,1,0:T(8,128)(2,1)S(1)}, u32[]{:S(2)}, u32[]{:S(2)}) collective-permute-start(bf16[2,512,384]{2,1,0:T(8,128)(2,1)S(1)} %get-tuple-element.41), channel_id=1, source_target_pairs={{0,1},{1,0},{2,3},{3,2},{4,5},{5,4},{6,7},{7,6},{8,9},{9,8},{10,11... | collective-permute-start | bytes 2359304 | tf_op jit(solution)/shard_map/ppermute | solution.py:598

commit v7 on v6

--- a/solution.py
+++ b/solution.py
@@ -19,7 +19,7 @@
 F32 = jnp.float32
 ANY = pl.BlockSpec(memory_space=pl.ANY)
 SMEM = pl.BlockSpec(memory_space=pltpu.SMEM)
-VMEM_LIMIT = 48 * 2**20
+VMEM_LIMIT = 62 * 2**20
 PACK_LIMIT = 16 * 2**20
 
 
@@ -38,8 +38,8 @@
             else:
                 self.early += lengths[column]
         self.places = self.early + self.late
-        self.first = self.early + self.late // 4
-        self.second = self.places - self.first
+        self.first = self.early
+        self.second = self.late
         self.near = 2 * self.places
         self.far = self.near + frames_here * STRIDE
         self.size = self.far + frames_here * STRIDE
@@ -425,11 +425,14 @@
     attend_list(q_refs, kbuf, vbuf, table_ref, lay.near + frame * STRIDE, m_s, l_s, acc_s, heads)
     if whole:
 
-        @pl.when(jnp.max(l_s[...]) > LARGE)
+        too_large = jnp.max(l_s[...]) > LARGE
+        finish(out_refs, acc_s, l_s, heads)
+
+        @pl.when(too_large)
         def _():
             exact_frame(lay, heads, frame, core, table_ref, q_refs, local, received, acc_s, m_s, l_s, tk, tv, far_sems)
-
-        finish(out_refs, acc_s, l_s, heads)
+            finish(out_refs, acc_s, l_s, heads)
+
     else:
         save_stats(stat_ref, m_s, l_s, heads)
 
@@ -476,7 +479,7 @@
         ),
         out_shape=out_shape,
         compiler_params=pltpu.CompilerParams(vmem_limit_bytes=VMEM_LIMIT),
-        cost_estimate=cost(steps * rows * heads * 32 * TILE),
+        cost_estimate=cost(steps * rows * heads * (4 if whole else 32) * TILE),
         name="attend_middle" if whole else "attend_edges",
     )(place, table, *queries, *in_hbm((*local, *early)))
 
@@ -518,11 +521,13 @@
     lax.fori_loop(0, table_ref[base], wait, 0)
     attend_list(q_refs, kbuf.at[step], vbuf.at[step], table_ref, base, m_s, l_s, acc_s, heads, packed=True)
 
-    @pl.when(jnp.max(l_s[...]) > LARGE)
+    too_large = jnp.max(l_s[...]) > LARGE
+    finish(out_refs, acc_s, l_s, heads)
+
+    @pl.when(too_large)
     def _():
         exact_frame(lay, heads, frame, core, table_ref, q_refs, local, received, acc_s, m_s, l_s, tk, tv, exact_sems)
-
-    finish(out_refs, acc_s, l_s, heads)
+        finish(out_refs, acc_s, l_s, heads)
 
 
 def far_call(lay, heads, place, table, queries, acc, stats, local, early, late, out):
@@ -580,7 +585,7 @@
         ),
         out_shape=jax.ShapeDtypeStruct(out.shape, BF),
         input_output_aliases={2: 0},
-        compiler_params=pltpu.CompilerParams(vmem_limit_bytes=VMEM_LIMIT),
+        compiler_params=pltpu.CompilerParams(vmem_limit_bytes=PACK_LIMIT),
         name="place_columns",
     )(place, blocks, out)
 

time: 93.8 us -> 92.5 us (0.986)
  the two profiles are of different devices: /device:TPU:15 before, /device:TPU:19 now
where the time goes in v7:
time: 92.5 us; the launch traced here: 91.5 us
  Pallas kernels  67.9 us (73%)
  starting transfers between devices  9.36 us (10%)
  local copies, waits for them, and re-layouts  8 us (9%)
  waiting for transfers between devices  5.51 us (6%)
    pallas_call x2, Pallas kernels, near_call(): pl.pallas_call(functools.partial(near_kernel, lay, heads, whole), grid_sp...  39.6 us
    pallas_call x1, Pallas kernels, far_call(): pl.pallas_call(functools.partial(far_kernel, lay, heads), grid_spec=pltpu...  16.1 us
    pallas_call x2, Pallas kernels, pack_call(): pl.pallas_call(functools.partial(pack_kernel, lay, begin, length), in_spe...  7.34 us
    ppermute x4, starting transfers between devices, paired(): lax.ppermute(block, 'frame', [p for i in pairs for p in ((i, i + 1), (i +...  5.53 us
    dynamic_slice x3, local copies, waits for them, and re-layouts, exchanged(): return swapped(lax.dynamic_slice_in_dim(a, (1 - core) * part, part, axis=2))  5.49 us
    ppermute x5, waiting for transfers between devices, swapped(): return lax.ppermute(block, 'seq', [(0, 1), (1, 0)])  4.25 us
    ppermute x5, starting transfers between devices, swapped(): return lax.ppermute(block, 'seq', [(0, 1), (1, 0)])  3.83 us
    pallas_call x2, Pallas kernels, place_call(): pl.pallas_call(place_kernel, grid_spec=pltpu.PrefetchScalarGridSpec(num_s...  2.95 us
  transfers between devices with their start and end apart: 9, of which 3 were waited for; matrix products, arithmetic and copies ran while one was open for 4% of the time, Pallas kernels for 55%

profile of v7, /device:TPU:19, one launch (start us, length us, event | category | flops | bytes accessed | tf_op | source)
XLA Modules:
  0.0 91.5 jit_solution(13836744194594409968)
XLA Ops:
  0.0 2.9 %constant_dynamic-slice_fusion.1 = bf16[4,512,384]{2,1,0:T(8,128)(2,1)} fusion(bf16[4,512,768]{2,1,0:T(8,128)(2,1)} %param.9, s32[]{:T(128)S(6)} %select_n.2), kind=kLoop, calls=%fused_computation.1 | loop fusion | bytes 3145732 | tf_op jit(solution)/shard_map/dynamic_slice | solution.py:620
  2.9 0.7 collective-permute-start.1
  3.5 1.3 %constant_dynamic-slice_fusion.2 = bf16[4,512,384]{2,1,0:T(8,128)(2,1)} fusion(bf16[4,512,768]{2,1,0:T(8,128)(2,1)S(1)} %copy-done.4, s32[]{:T(128)S(6)} %select_n.2), kind=kLoop, calls=%fused_computation.2 | loop fusion | bytes 3145732 | tf_op jit(solution)/shard_map/dynamic_slice | solution.py:620
  4.9 0.0 collective-permute-start
  4.9 0.1 copy-done.6
  5.0 1.3 %constant_dynamic-slice_fusion = bf16[4,512,384]{2,1,0:T(8,128)(2,1)} fusion(bf16[4,512,768]{2,1,0:T(8,128)(2,1)S(1)} %copy-done.6, s32[]{:T(128)S(6)} %select_n.2), kind=kLoop, calls=%fused_computation | loop fusion | bytes 3145732 | tf_op jit(solution)/shard_map/dynamic_slice | solution.py:620
  6.3 1.0 %collective-permute-start.2 = (bf16[4,512,384]{2,1,0:T(8,128)(2,1)}, bf16[4,512,384]{2,1,0:T(8,128)(2,1)}, u32[]{:S(2)}, u32[]{:S(2)}) collective-permute-start(bf16[4,512,384]{2,1,0:T(8,128)(2,1)} %constant_dynamic-slice_fusion), channel_id=1, source_target_pairs={{0,1},{1,0},{2,3},{3,2},{4,5},{5,4},{6,7},{7,6},{8,9},{9,8},{10,11... | collective-permute-start | bytes 4718600 | tf_op jit(solution)/shard_map/ppermute | solution.py:603
  7.3 0.7 pad_add_fusion.place_ref
  7.9 1.9 %tile_tables.1.table_ref = s32[216]{0:T(256)} custom-call(s32[2]{0:T(128)} %pad_add_fusion.place_ref, s32[2,4,16]{2,1,0:T(4,128)} %bitcast.25, s32[2,2,16]{2,1,0:T(2,128)} %bitcast.27, s32[2,1,16]{2,1,0:T(1,128)} %bitcast.28, s32[3,2,16]{2,1,0:T(2,128)} %bitcast.26), custom_call_target="tpu_custom_call" | custom-call | tf_op jit(solution)/shard_map/tile_tables/pallas_call | solution.py:130
  9.8 0.0 collective-permute-done.1
  9.9 0.0 collective-permute-done
  9.9 1.1 %copy-done.5 = bf16[4,512,384]{2,1,0:T(8,128)(2,1)} copy-done((bf16[4,512,384]{2,1,0:T(8,128)(2,1)}, bf16[4,512,384]{2,1,0:T(8,128)(2,1)S(1)}, u32[]{:S(2)}) %copy-start.5) | copy-done | bytes 1572888
  11.0 0.6 copy-done
  11.6 0.7 copy-done.1
  12.3 3.3 %pack_tiles.2 = (bf16[8,128,384]{2,1,0:T(8,128)(2,1)}, bf16[8,128,384]{2,1,0:T(8,128)(2,1)}) custom-call(s32[2]{0:T(128)S(1)} %copy-done.1, s32[216]{0:T(256)S(1)} %copy-done, bf16[4,4,128,768]{3,2,1,0:T(8,128)(2,1)} %bitcast.10, bf16[4,4,128,384]{3,2,1,0:T(8,128)(2,1)} %bitcast.7.k_other.refs_1_, bf16[4,4,128,768]{3,2,1,0:T(8,128)(2,1)} %bitcast.15, ...), custom_call_target="tpu_custom_call" | custom-call | tf_op jit(solution)/shard_map/pack_tiles/pallas_call | solution.py:171
  15.7 2.1 %collective-permute-start.3 = (bf16[8,128,384]{2,1,0:T(8,128)(2,1)}, bf16[8,128,384]{2,1,0:T(8,128)(2,1)}, u32[]{:S(2)}, u32[]{:S(2)}) collective-permute-start(bf16[8,128,384]{2,1,0:T(8,128)(2,1)} %get-tuple-element.28), channel_id=1, source_target_pairs={{4,8},{8,4},{5,9},{9,5},{6,10},{10,6},{7,11},{11,7},{20,24},{24,20... | collective-permute-start | bytes 2359304 | tf_op jit(solution)/shard_map/ppermute | solution.py:599
  17.7 0.8 collective-permute-start.4
  18.6 4.0 %pack_tiles.3 = (bf16[16,128,384]{2,1,0:T(8,128)(2,1)}, bf16[16,128,384]{2,1,0:T(8,128)(2,1)S(1)}) custom-call(s32[2]{0:T(128)S(1)} %copy-done.1, s32[216]{0:T(256)S(1)} %copy-done, bf16[4,4,128,768]{3,2,1,0:T(8,128)(2,1)} %bitcast.11, bf16[4,4,128,384]{3,2,1,0:T(8,128)(2,1)} %bitcast.7.k_other.refs_1_, bf16[4,4,128,768]{3,2,1,0:T(8,128)(2,1)} %bitcast.16, ...), custom_call_target="tpu_custom_call" | custom-call | tf_op jit(solution)/shard_map/pack_tiles/pallas_call | solution.py:171
  22.6 2.5 %collective-permute-start.5 = (bf16[16,128,384]{2,1,0:T(8,128)(2,1)}, bf16[16,128,384]{2,1,0:T(8,128)(2,1)}, u32[]{:S(2)}, u32[]{:S(2)}) collective-permute-start(bf16[16,128,384]{2,1,0:T(8,128)(2,1)} %get-tuple-element.34), channel_id=1, source_target_pairs={{4,8},{8,4},{5,9},{9,5},{6,10},{10,6},{7,11},{11,7},{20,24},{24,20... | collective-permute-start | bytes 4718600 | tf_op jit(solution)/shard_map/ppermute | solution.py:599
  25.1 0.1 collective-permute-start.6
  25.2 0.0 collective-permute-done.2.q_other
  25.2 17.5 %attend_edges.1 = (f32[2,6,512,128]{3,2,1,0:T(8,128)}, f32[2,512,128]{2,1,0:T(8,128)}) custom-call(s32[2]{0:T(128)} %pad_add_fusion.place_ref, s32[216]{0:T(256)} %tile_tables.1.table_ref, bf16[4,512,768]{2,1,0:T(8,128)(2,1)} %q_own.5, bf16[4,512,384]{2,1,0:T(8,128)(2,1)} %collective-permute-done.2.q_other, bf16[4,4,128,768]{3,2,1,0:T(8,128)(2,1)} %bitcast.12, ...), custom_call_target="tpu_custom_call" | custom-call | flops 6442450944 | bytes 1572864 | tf_op jit(solution)/shard_map/attend_edges/pallas_call | solution.py:471
  42.7 22.1 %attend_middle.1 = (bf16[4,512,768]{2,1,0:T(8,128)(2,1)}, bf16[2,512,384]{2,1,0:T(8,128)(2,1)}) custom-call(s32[2]{0:T(128)} %pad_add_fusion.place_ref, s32[216]{0:T(256)} %tile_tables.1.table_ref, bf16[4,512,768]{2,1,0:T(8,128)(2,1)} %q_own.5, bf16[4,512,384]{2,1,0:T(8,128)(2,1)} %collective-permute-done.2.q_other, bf16[4,4,128,768]{3,2,1,0:T(8,128)(2,1)} %bitcast.13, ...), custom_call_target="tpu_custom_call" | custom-call | flops 805306368 | bytes 196608 | tf_op jit(solution)/shard_map/attend_middle/pallas_call | solution.py:471
  64.9 1.0 %collective-permute-start.7 = (bf16[2,512,384]{2,1,0:T(8,128)(2,1)}, bf16[2,512,384]{2,1,0:T(8,128)(2,1)S(1)}, u32[]{:S(2)}, u32[]{:S(2)}) collective-permute-start(bf16[2,512,384]{2,1,0:T(8,128)(2,1)} %get-tuple-element.36), channel_id=1, source_target_pairs={{0,1},{1,0},{2,3},{3,2},{4,5},{5,4},{6,7},{7,6},{8,9},{9,8},{10,11... | collective-permute-start | bytes 2359304 | tf_op jit(solution)/shard_map/ppermute | solution.py:603
  65.9 2.1 %collective-permute-done.7.block_ref = bf16[2,512,384]{2,1,0:T(8,128)(2,1)S(1)} collective-permute-done((bf16[2,512,384]{2,1,0:T(8,128)(2,1)}, bf16[2,512,384]{2,1,0:T(8,128)(2,1)S(1)}, u32[]{:S(2)}, u32[]{:S(2)}) %collective-permute-start.7) | collective-permute-done | bytes 786464 | tf_op jit(solution)/shard_map/ppermute | solution.py:603
  68.0 1.5 %place_columns.2.refs_8_ = bf16[4,512,768]{2,1,0:T(8,128)(2,1)} custom-call(s32[2]{0:T(128)S(1)} %copy-done.2, bf16[2,512,384]{2,1,0:T(8,128)(2,1)S(1)} %collective-permute-done.7.block_ref, bf16[4,512,768]{2,1,0:T(8,128)(2,1)} %get-tuple-element.37._), custom_call_target="tpu_custom_call", output_to_operand_aliasing={{}: (2, {})} | custom-call | tf_op jit(solution)/shard_map/place_columns/pallas_call | solution.py:578
  69.5 1.2 %collective-permute-done.5.refs_6_ = bf16[16,128,384]{2,1,0:T(8,128)(2,1)} collective-permute-done((bf16[16,128,384]{2,1,0:T(8,128)(2,1)}, bf16[16,128,384]{2,1,0:T(8,128)(2,1)}, u32[]{:S(2)}, u32[]{:S(2)}) %collective-permute-start.5) | collective-permute-done | bytes 1572896 | tf_op jit(solution)/shard_map/ppermute | solution.py:599
  70.7 0.0 collective-permute-done.6.refs_7_
  70.8 16.1 %attend_late.1 = (bf16[4,512,768]{2,1,0:T(8,128)(2,1)}, bf16[2,512,384]{2,1,0:T(8,128)(2,1)}) custom-call(s32[2]{0:T(128)} %pad_add_fusion.place_ref, s32[216]{0:T(256)} %tile_tables.1.table_ref, bf16[4,512,768]{2,1,0:T(8,128)(2,1)} %q_own.5, bf16[4,512,384]{2,1,0:T(8,128)(2,1)} %collective-permute-done.2.q_other, ...), custom_call_target="tpu_custom_call", output_to_operand_aliasing={{0}: (14, {})} | custom-call | flops 2818572288 | bytes 688128 | tf_op jit(solution)/shard_map/attend_late/pallas_call | solution.py:539
  86.8 1.1 %collective-permute-start.8 = (bf16[2,512,384]{2,1,0:T(8,128)(2,1)}, bf16[2,512,384]{2,1,0:T(8,128)(2,1)S(1)}, u32[]{:S(2)}, u32[]{:S(2)}) collective-permute-start(bf16[2,512,384]{2,1,0:T(8,128)(2,1)} %get-tuple-element.41), channel_id=1, source_target_pairs={{0,1},{1,0},{2,3},{3,2},{4,5},{5,4},{6,7},{7,6},{8,9},{9,8},{10,11... | collective-permute-start | bytes 2359304 | tf_op jit(solution)/shard_map/ppermute | solution.py:603
  87.9 2.1 %collective-permute-done.8.block_ref = bf16[2,512,384]{2,1,0:T(8,128)(2,1)S(1)} collective-permute-done((bf16[2,512,384]{2,1,0:T(8,128)(2,1)}, bf16[2,512,384]{2,1,0:T(8,128)(2,1)S(1)}, u32[]{:S(2)}, u32[]{:S(2)}) %collective-permute-start.8) | collective-permute-done | bytes 786464 | tf_op jit(solution)/shard_map/ppermute | solution.py:603
  90.0 1.5 %place_columns.3 = bf16[4,512,768]{2,1,0:T(8,128)(2,1)} custom-call(s32[2]{0:T(128)S(1)} %copy-done.3, bf16[2,512,384]{2,1,0:T(8,128)(2,1)S(1)} %collective-permute-done.8.block_ref, bf16[4,512,768]{2,1,0:T(8,128)(2,1)} %get-tuple-element.42._), custom_call_target="tpu_custom_call", output_to_operand_aliasing={{}: (2, {})} | custom-call | tf_op jit(solution)/shard_map/place_columns/pallas_call | solution.py:578
  (12 shorter events, 0.0 us)
Async XLA Ops:
  0.0 3.5 %copy-start.4 = (bf16[4,512,768]{2,1,0:T(8,128)(2,1)S(1)}, bf16[4,512,768]{2,1,0:T(8,128)(2,1)}, u32[]{:S(2)}) copy-start(bf16[4,512,768]{2,1,0:T(8,128)(2,1)} %param.8) | copy-start | bytes 9437188
  2.9 2.1 %copy-start.6 = (bf16[4,512,768]{2,1,0:T(8,128)(2,1)S(1)}, bf16[4,512,768]{2,1,0:T(8,128)(2,1)}, u32[]{:S(2)}) copy-start(bf16[4,512,768]{2,1,0:T(8,128)(2,1)} %q_own.5) | copy-start | bytes 9437188
  2.9 7.0 %collective-permute-start.1 = (bf16[4,512,384]{2,1,0:T(8,128)(2,1)}, bf16[4,512,384]{2,1,0:T(8,128)(2,1)S(1)}, u32[]{:S(2)}, u32[]{:S(2)}) collective-permute-start(bf16[4,512,384]{2,1,0:T(8,128)(2,1)} %constant_dynamic-slice_fusion.1), channel_id=1, source_target_pairs={{0,1},{1,0},{2,3},{3,2},{4,5},{5,4},{6,7},{7,6},{8,9},{9,8},{10,11... | collective-permute-start | bytes 4718600 | tf_op jit(solution)/shard_map/ppermute | solution.py:603
  4.9 5.0 %collective-permute-start = (bf16[4,512,384]{2,1,0:T(8,128)(2,1)}, bf16[4,512,384]{2,1,0:T(8,128)(2,1)}, u32[]{:S(2)}, u32[]{:S(2)}) collective-permute-start(bf16[4,512,384]{2,1,0:T(8,128)(2,1)} %constant_dynamic-slice_fusion.2), channel_id=1, source_target_pairs={{0,1},{1,0},{2,3},{3,2},{4,5},{5,4},{6,7},{7,6},{8,9},{9,8},{10,11... | collective-permute-start | bytes 4718600 | tf_op jit(solution)/shard_map/ppermute | solution.py:603
  6.3 19.0 %collective-permute-start.2 = (bf16[4,512,384]{2,1,0:T(8,128)(2,1)}, bf16[4,512,384]{2,1,0:T(8,128)(2,1)}, u32[]{:S(2)}, u32[]{:S(2)}) collective-permute-start(bf16[4,512,384]{2,1,0:T(8,128)(2,1)} %constant_dynamic-slice_fusion), channel_id=1, source_target_pairs={{0,1},{1,0},{2,3},{3,2},{4,5},{5,4},{6,7},{7,6},{8,9},{9,8},{10,11... | collective-permute-start | bytes 4718600 | tf_op jit(solution)/shard_map/ppermute | solution.py:603
  9.9 1.1 %copy-start.5 = (bf16[4,512,384]{2,1,0:T(8,128)(2,1)}, bf16[4,512,384]{2,1,0:T(8,128)(2,1)S(1)}, u32[]{:S(2)}) copy-start(bf16[4,512,384]{2,1,0:T(8,128)(2,1)S(1)} %collective-permute-done.1) | copy-start | bytes 4718596
  11.0 0.6 copy-start
  11.6 0.7 copy-start.1
  15.7 27.1 %collective-permute-start.3 = (bf16[8,128,384]{2,1,0:T(8,128)(2,1)}, bf16[8,128,384]{2,1,0:T(8,128)(2,1)}, u32[]{:S(2)}, u32[]{:S(2)}) collective-permute-start(bf16[8,128,384]{2,1,0:T(8,128)(2,1)} %get-tuple-element.28), channel_id=1, source_target_pairs={{4,8},{8,4},{5,9},{9,5},{6,10},{10,6},{7,11},{11,7},{20,24},{24,20... | collective-permute-start | bytes 2359304 | tf_op jit(solution)/shard_map/ppermute | solution.py:599
  17.7 25.0 %collective-permute-start.4 = (bf16[8,128,384]{2,1,0:T(8,128)(2,1)}, bf16[8,128,384]{2,1,0:T(8,128)(2,1)}, u32[]{:S(2)}, u32[]{:S(2)}) collective-permute-start(bf16[8,128,384]{2,1,0:T(8,128)(2,1)} %get-tuple-element.29), channel_id=1, source_target_pairs={{0,4},{4,0},{8,12},{12,8},{1,5},{5,1},{9,13},{13,9},{2,6},{6,2},{1... | collective-permute-start | bytes 2359304 | tf_op jit(solution)/shard_map/ppermute | solution.py:599
  22.6 48.2 %collective-permute-start.5 = (bf16[16,128,384]{2,1,0:T(8,128)(2,1)}, bf16[16,128,384]{2,1,0:T(8,128)(2,1)}, u32[]{:S(2)}, u32[]{:S(2)}) collective-permute-start(bf16[16,128,384]{2,1,0:T(8,128)(2,1)} %get-tuple-element.34), channel_id=1, source_target_pairs={{4,8},{8,4},{5,9},{9,5},{6,10},{10,6},{7,11},{11,7},{20,24},{24,20... | collective-permute-start | bytes 4718600 | tf_op jit(solution)/shard_map/ppermute | solution.py:599
  25.1 45.7 %collective-permute-start.6 = (bf16[16,128,384]{2,1,0:T(8,128)(2,1)S(1)}, bf16[16,128,384]{2,1,0:T(8,128)(2,1)}, u32[]{:S(2)}, u32[]{:S(2)}) collective-permute-start(bf16[16,128,384]{2,1,0:T(8,128)(2,1)S(1)} %get-tuple-element.35), channel_id=1, source_target_pairs={{0,4},{4,0},{8,12},{12,8},{1,5},{5,1},{9,13},{13,9},{2,6},{6,2},{1... | collective-permute-start | bytes 4718600 | tf_op jit(solution)/shard_map/ppermute | solution.py:599
  42.7 25.3 %copy-start.2 = (s32[2]{0:T(128)S(1)}, s32[2]{0:T(128)}, u32[]{:S(2)}) copy-start(s32[2]{0:T(128)} %pad_add_fusion.place_ref) | copy-start | bytes 28
  64.9 3.1 %collective-permute-start.7 = (bf16[2,512,384]{2,1,0:T(8,128)(2,1)}, bf16[2,512,384]{2,1,0:T(8,128)(2,1)S(1)}, u32[]{:S(2)}, u32[]{:S(2)}) collective-permute-start(bf16[2,512,384]{2,1,0:T(8,128)(2,1)} %get-tuple-element.36), channel_id=1, source_target_pairs={{0,1},{1,0},{2,3},{3,2},{4,5},{5,4},{6,7},{7,6},{8,9},{9,8},{10,11... | collective-permute-start | bytes 2359304 | tf_op jit(solution)/shard_map/ppermute | solution.py:603
  70.7 19.3 %copy-start.3 = (s32[2]{0:T(128)S(1)}, s32[2]{0:T(128)}, u32[]{:S(2)}) copy-start(s32[2]{0:T(128)} %pad_add_fusion.place_ref) | copy-start | bytes 28
  86.8 3.2 %collective-permute-start.8 = (bf16[2,512,384]{2,1,0:T(8,128)(2,1)}, bf16[2,512,384]{2,1,0:T(8,128)(2,1)S(1)}, u32[]{:S(2)}, u32[]{:S(2)}) collective-permute-start(bf16[2,512,384]{2,1,0:T(8,128)(2,1)} %get-tuple-element.41), channel_id=1, source_target_pairs={{0,1},{1,0},{2,3},{3,2},{4,5},{5,4},{6,7},{7,6},{8,9},{9,8},{10,11... | collective-permute-start | bytes 2359304 | tf_op jit(solution)/shard_map/ppermute | solution.py:603

commit v8 on v5

--- a/solution.py
+++ b/solution.py
@@ -38,7 +38,7 @@
             else:
                 self.early += lengths[column]
         self.places = self.early + self.late
-        self.first = self.early + self.late // 4
+        self.first = self.early
         self.second = self.places - self.first
         self.near = 2 * self.places
         self.far = self.near + frames_here * STRIDE
@@ -142,8 +142,8 @@
     return pl.ds(pl.multiple_of(core * width, HEAD_DIM), width)
 
 
-def pack_kernel(lay, begin, length, place_ref, table_ref, k_own, k_other, v_own, v_other, *refs):
-    outs, sems = refs[:2], refs[2]
+def pack_kernel(lay, begin, length, place_ref, table_ref, *refs):
+    sources, outs, sems = refs[:-3], refs[-3:-1], refs[-1]
     core = place_ref[1]
     cols = columns(core, outs[0].shape[-1])
     waits = []
@@ -154,7 +154,8 @@
             tile = name % lay.tiles
             mine = tile // lay.half == core
             tile = tile % lay.half
-            for kv, (own, other) in enumerate(((k_own, k_other), (v_own, v_other))):
+            for kv in range(len(sources) // 2):
+                own, other = sources[2 * kv : 2 * kv + 2]
                 target = out.at[kv * length + item]
                 sem = sems.at[len(waits)]
                 here = pltpu.make_async_copy(own.at[frame, tile, :, cols], target, sem)
@@ -167,13 +168,14 @@
 
 
 def pack_call(lay, begin, length, place, table, local):
-    shape = jax.ShapeDtypeStruct((2 * length, TILE, local[1].shape[-1]), BF)
+    kinds = len(local) // 2
+    shape = jax.ShapeDtypeStruct((kinds * length, TILE, local[1].shape[-1]), BF)
     return pl.pallas_call(
         functools.partial(pack_kernel, lay, begin, length),
-        in_specs=[SMEM] * 2 + [ANY] * 4,
+        in_specs=[SMEM] * 2 + [ANY] * len(local),
         out_specs=[pl.BlockSpec(memory_space=pltpu.VMEM)] * 2,
         out_shape=[shape] * 2,
-        scratch_shapes=[pltpu.SemaphoreType.DMA((4 * length,))],
+        scratch_shapes=[pltpu.SemaphoreType.DMA((2 * kinds * length,))],
         compiler_params=pltpu.CompilerParams(vmem_limit_bytes=PACK_LIMIT),
         name="pack_tiles",
     )(place, table, *in_hbm(local))
@@ -280,16 +282,15 @@
 class Received:
     def __init__(self, lay, refs):
         self.lay = lay
-        self.parts = [(0, lay.first, refs[:2])]
-        if len(refs) > 2:
-            self.parts.append((lay.first, lay.second, refs[2:4]))
+        self.parts = [(0, lay.first, ((refs[:2], 0), (refs[2:4], 0)))]
+        if len(refs) > 4:
+            self.parts.append((lay.first, lay.second, ((refs[4:6], 0), (refs[4:6], lay.second))))
 
     def early_copies(self, bufs, sems):
-        _, size, refs = self.parts[0]
         found = []
-        for kv, buf in enumerate(bufs):
+        for buf, (refs, _) in zip(bufs, self.parts[0][2]):
             for way in (0, 1):
-                source = refs[way].at[pl.ds(kv * size, self.lay.early)]
+                source = refs[way].at[pl.ds(0, self.lay.early)]
                 target = buf.at[pl.ds(self.lay.own + way * self.lay.early, self.lay.early)]
                 found.append(pltpu.make_async_copy(source, target, sems.at[len(found)]))
         return found
@@ -297,18 +298,18 @@
     def start(self, item, length, targets, sems):
         place = item % length
         for way in (0, 1):
-            for begin, size, refs in self.parts:
+            for begin, size, kinds in self.parts:
                 inside = jnp.logical_and(place >= begin, place < begin + size)
 
                 @pl.when(jnp.logical_and(item // length == way, inside))
-                def _(way=way, begin=begin, size=size, refs=refs):
-                    for kv, target in enumerate(targets):
-                        source = refs[way].at[place - begin + kv * size]
+                def _(way=way, begin=begin, kinds=kinds):
+                    for kv, (target, (refs, row)) in enumerate(zip(targets, kinds)):
+                        source = refs[way].at[place - begin + row]
                         pltpu.make_async_copy(source, target, sems.at[kv]).start()
 
     def wait(self, targets, sems):
         for kv, target in enumerate(targets):
-            pltpu.make_async_copy(self.parts[0][2][0].at[0], target, sems.at[kv]).wait()
+            pltpu.make_async_copy(self.parts[0][2][0][0][0].at[0], target, sems.at[kv]).wait()
 
 
 def exact_frame(lay, heads, frame, core, table_ref, q_refs, local, received, acc_s, m_s, l_s, tk, tv, sems):
@@ -387,7 +388,7 @@
     q_refs = (q_own, q_other)
     local, refs = refs[:4], refs[4:]
     if whole:
-        received, out_refs, refs = Received(lay, refs[:2]), refs[2:4], refs[4:]
+        received, out_refs, refs = Received(lay, refs[:4]), refs[4:6], refs[6:]
         acc_s, kbuf, vbuf, m_s, l_s, sems, tk, tv, far_sems = refs
     else:
         acc_out, stat_ref, kbuf, vbuf, m_s, l_s, sems = refs
@@ -476,7 +477,7 @@
         ),
         out_shape=out_shape,
         compiler_params=pltpu.CompilerParams(vmem_limit_bytes=VMEM_LIMIT),
-        cost_estimate=cost(steps * rows * heads * 32 * TILE),
+        cost_estimate=cost(steps * rows * heads * (128 if whole else 8) * TILE),
         name="attend_middle" if whole else "attend_edges",
     )(place, table, *queries, *in_hbm((*local, *early)))
 
@@ -484,8 +485,8 @@
 def far_kernel(lay, heads, place_ref, table_ref, q_own, q_other, acc_ref, stat_ref, *refs):
     core = place_ref[1]
     q_refs = (q_own, q_other)
-    local, received, out_refs = refs[:4], Received(lay, refs[4:8]), refs[9:11]
-    kbuf, vbuf, acc_s, m_s, l_s, tk, tv, sems, exact_sems = refs[11:]
+    local, received, out_refs = refs[:4], Received(lay, refs[4:10]), refs[11:13]
+    kbuf, vbuf, acc_s, m_s, l_s, tk, tv, sems, exact_sems = refs[13:]
     step = pl.program_id(0)
     frame = step * (lay.here - 1)
     room = kbuf.shape[1]
@@ -619,7 +620,6 @@
 
     k_other = tiled(exchanged(key_rows))
     v_other = tiled(exchanged(value_rows))
-    queries = (queries, exchanged(queries))
     by_frame = [jnp.transpose(a, (1, 2, 0)) for a in lists] + [jnp.transpose(tile_counts, (2, 1, 0))]
     table = make_table(lay, place, by_frame)
     local = (tiled(key_rows), k_other, tiled(value_rows), v_other)
@@ -627,12 +627,19 @@
     def both_ways(pair):
         return paired(pair[0], 0), paired(pair[1], 1)
 
-    early = pack_call(lay, 0, lay.first, place, table, local)
-    early, table = lax.optimization_barrier((early, table))
-    early = both_ways(early)
+    keys = pack_call(lay, 0, lay.first, place, table, local[:2])
+    keys, v_other, queries, table = lax.optimization_barrier((keys, v_other, queries, table))
+    keys = both_ways(keys)
+    queries = (queries, exchanged(queries))
+    local = (*local[:3], v_other)
+    values = pack_call(lay, 0, lay.first, place, table, local[2:])
+    values, table = lax.optimization_barrier((values, table))
+    values = both_ways(values)
     late = both_ways(pack_call(lay, lay.first, lay.second, place, table, local))
+    keys, table = lax.optimization_barrier((keys, table))
     acc, stats = near_call(lay, heads, False, place, table, queries, local)
-    early, stats = lax.optimization_barrier((early, stats))
+    values, stats = lax.optimization_barrier((values, stats))
+    early = (*keys, *values)
     out, sent = near_call(lay, heads, True, place, table, queries, local, early)
     late, sent = lax.optimization_barrier((late, sent))
     middle = swapped(sent)

time: 88.2 us -> 89.3 us (1.012)
  waiting for transfers between devices: 7.65 us -> 2.1 us
  Pallas kernels: 61.6 us -> 66.1 us
  starting transfers between devices: 10 us -> 13.7 us
    ppermute x4 -> x6, waiting for transfers between devices: 6.86 us -> 1.57 us  [paired(): lax.ppermute(block, 'frame', [p for i in pairs for p in ((i, i + 1), (i +...]
    ppermute x4 -> x6, starting transfers between devices: 6.72 us -> 9.69 us  [paired(): lax.ppermute(block, 'frame', [p for i in pairs for p in ((i, i + 1), (i +...]
    pallas_call x2, Pallas kernels: 37.5 us -> 40.1 us  [near_call(): pl.pallas_call(functools.partial(near_kernel, lay, heads, whole), grid_sp...]
    pallas_call x2 -> x3, Pallas kernels: 5.3 us -> 6.84 us  [pack_call(): pl.pallas_call(functools.partial(pack_kernel, lay, begin, length), in_spe...]
    dynamic_slice x3, local copies, waits for them, and re-layouts: 5.48 us -> 4.37 us  [exchanged(): return swapped(lax.dynamic_slice_in_dim(a, (1 - core) * part, part, axis=2))]
    unnamed x18 -> x28, local copies, waits for them, and re-layouts: 1.7 us -> 1.99 us
  transfers between devices with their start and end apart: 9 -> 11, of which waited for: 5 -> 3; matrix products, arithmetic and copies ran while one was open for 3% -> 2% of each run, Pallas kernels for 69% -> 73%
where the time goes in v8:
time: 89.3 us; the launch traced here: 88.6 us
  Pallas kernels  66.1 us (74%)
  starting transfers between devices  13.7 us (15%)
  local copies, waits for them, and re-layouts  6.36 us (7%)
  waiting for transfers between devices  2.1 us (2%)
    pallas_call x2, Pallas kernels, near_call(): pl.pallas_call(functools.partial(near_kernel, lay, heads, whole), grid_sp...  40.1 us
    pallas_call x1, Pallas kernels, far_call(): pl.pallas_call(functools.partial(far_kernel, lay, heads), grid_spec=pltpu...  14.4 us
    ppermute x6, starting transfers between devices, paired(): lax.ppermute(block, 'frame', [p for i in pairs for p in ((i, i + 1), (i +...  9.69 us
    pallas_call x3, Pallas kernels, pack_call(): pl.pallas_call(functools.partial(pack_kernel, lay, begin, length), in_spe...  6.84 us
    dynamic_slice x3, local copies, waits for them, and re-layouts, exchanged(): return swapped(lax.dynamic_slice_in_dim(a, (1 - core) * part, part, axis=2))  4.37 us
    ppermute x5, starting transfers between devices, swapped(): return lax.ppermute(block, 'seq', [(0, 1), (1, 0)])  4.03 us
    pallas_call x2, Pallas kernels, place_call(): pl.pallas_call(place_kernel, grid_spec=pltpu.PrefetchScalarGridSpec(num_s...  2.95 us
    unnamed x28, local copies, waits for them, and re-layouts  1.99 us
  transfers between devices with their start and end apart: 11, of which 3 were waited for; matrix products, arithmetic and copies ran while one was open for 2% of the time, Pallas kernels for 73%

profile of v8, /device:TPU:19, one launch (start us, length us, event | category | flops | bytes accessed | tf_op | source)
XLA Modules:
  0.0 88.6 jit_solution(7170833726688014245)
XLA Ops:
  0.0 2.9 %constant_dynamic-slice_fusion.2 = bf16[4,512,384]{2,1,0:T(8,128)(2,1)} fusion(bf16[4,512,768]{2,1,0:T(8,128)(2,1)} %param.8, s32[]{:T(128)S(6)} %select_n.2), kind=kLoop, calls=%fused_computation.2 | loop fusion | bytes 3145732 | tf_op jit(solution)/shard_map/dynamic_slice | solution.py:616
  2.9 0.7 collective-permute-start
  3.6 1.4 %constant_dynamic-slice_fusion.1 = bf16[4,512,384]{2,1,0:T(8,128)(2,1)} fusion(bf16[4,512,768]{2,1,0:T(8,128)(2,1)S(1)} %copy-done.7, s32[]{:T(128)S(6)} %select_n.2), kind=kLoop, calls=%fused_computation.1 | loop fusion | bytes 3145732 | tf_op jit(solution)/shard_map/dynamic_slice | solution.py:616
  5.0 0.0 collective-permute-start.1
  5.0 0.1 pad_add_fusion.place_ref
  5.1 1.8 %tile_tables.1.table_ref = s32[216]{0:T(256)S(1)} custom-call(s32[2]{0:T(128)S(1)} %pad_add_fusion.place_ref, s32[2,4,16]{2,1,0:T(4,128)S(1)} %bitcast.10, s32[2,2,16]{2,1,0:T(2,128)S(1)} %bitcast.12, s32[2,1,16]{2,1,0:T(1,128)S(1)} %bitcast.13, s32[3,2,16]{2,1,0:T(2,128)S(1)} %bitcast.11), custom_call_target="tpu_custom_call" | custom-call | tf_op jit(solution)/shard_map/tile_tables/pallas_call | solution.py:130
  6.9 0.1 collective-permute-done
  7.0 2.1 %pack_tiles.3 = (bf16[4,128,384]{2,1,0:T(8,128)(2,1)S(1)}, bf16[4,128,384]{2,1,0:T(8,128)(2,1)S(1)}) custom-call(s32[2]{0:T(128)S(1)} %pad_add_fusion.place_ref, s32[216]{0:T(256)S(1)} %tile_tables.1.table_ref, bf16[4,4,128,768]{3,2,1,0:T(8,128)(2,1)} %bitcast.14, bf16[4,4,128,384]{3,2,1,0:T(8,128)(2,1)} %bitcast.7.refs_1_), custom_call_target="tpu_custom_call" | custom-call | tf_op jit(solution)/shard_map/pack_tiles/pallas_call | solution.py:173
  9.1 0.0 collective-permute-done.1
  9.1 0.1 copy-done
  9.2 0.2 constant_dynamic-slice_fusion
  9.4 1.0 %copy-done.8 = bf16[4,512,384]{2,1,0:T(8,128)(2,1)} copy-done((bf16[4,512,384]{2,1,0:T(8,128)(2,1)}, bf16[4,512,384]{2,1,0:T(8,128)(2,1)S(1)}, u32[]{:S(2)}) %copy-start.8) | copy-done | bytes 1572888
  10.3 0.4 collective-permute-start.4
  10.8 1.3 %collective-permute-start.2 = (bf16[4,128,384]{2,1,0:T(8,128)(2,1)S(1)}, bf16[4,128,384]{2,1,0:T(8,128)(2,1)S(1)}, u32[]{:S(2)}, u32[]{:S(2)}) collective-permute-start(bf16[4,128,384]{2,1,0:T(8,128)(2,1)S(1)} %get-tuple-element.36), channel_id=1, source_target_pairs={{0,4},{4,0},{8,12},{12,8},{1,5},{5,1},{9,13},{13,9},{2,6},{6,2},{1... | collective-permute-start | bytes 1179656 | tf_op jit(solution)/shard_map/ppermute | solution.py:595
  12.1 1.9 %collective-permute-start.3 = (bf16[4,128,384]{2,1,0:T(8,128)(2,1)S(1)}, bf16[4,128,384]{2,1,0:T(8,128)(2,1)S(1)}, u32[]{:S(2)}, u32[]{:S(2)}) collective-permute-start(bf16[4,128,384]{2,1,0:T(8,128)(2,1)S(1)} %get-tuple-element.37), channel_id=1, source_target_pairs={{4,8},{8,4},{5,9},{9,5},{6,10},{10,6},{7,11},{11,7},{20,24},{24,20... | collective-permute-start | bytes 1179656 | tf_op jit(solution)/shard_map/ppermute | solution.py:595
  14.0 1.9 %pack_tiles.4 = (bf16[4,128,384]{2,1,0:T(8,128)(2,1)S(1)}, bf16[4,128,384]{2,1,0:T(8,128)(2,1)S(1)}) custom-call(s32[2]{0:T(128)S(1)} %pad_add_fusion.place_ref, s32[216]{0:T(256)S(1)} %tile_tables.1.table_ref, bf16[4,4,128,768]{3,2,1,0:T(8,128)(2,1)} %bitcast.19, bf16[4,4,128,384]{3,2,1,0:T(8,128)(2,1)} %bitcast.24), custom_call_target="tpu_custom_call" | custom-call | tf_op jit(solution)/shard_map/pack_tiles/pallas_call | solution.py:173
  15.9 0.1 collective-permute-start.5
  15.9 3.4 %collective-permute-start.6 = (bf16[4,128,384]{2,1,0:T(8,128)(2,1)S(1)}, bf16[4,128,384]{2,1,0:T(8,128)(2,1)S(1)}, u32[]{:S(2)}, u32[]{:S(2)}) collective-permute-start(bf16[4,128,384]{2,1,0:T(8,128)(2,1)S(1)} %get-tuple-element.47), channel_id=1, source_target_pairs={{4,8},{8,4},{5,9},{9,5},{6,10},{10,6},{7,11},{11,7},{20,24},{24,20... | collective-permute-start | bytes 1179656 | tf_op jit(solution)/shard_map/ppermute | solution.py:595
  19.3 2.8 %pack_tiles.5 = (bf16[16,128,384]{2,1,0:T(8,128)(2,1)S(1)}, bf16[16,128,384]{2,1,0:T(8,128)(2,1)S(1)}) custom-call(s32[2]{0:T(128)S(1)} %pad_add_fusion.place_ref, s32[216]{0:T(256)S(1)} %tile_tables.1.table_ref, bf16[4,4,128,768]{3,2,1,0:T(8,128)(2,1)} %bitcast.15, bf16[4,4,128,384]{3,2,1,0:T(8,128)(2,1)} %bitcast.7.refs_1_, ...), custom_call_target="tpu_custom_call" | custom-call | tf_op jit(solution)/shard_map/pack_tiles/pallas_call | solution.py:173
  22.2 0.5 collective-permute-start.7
  22.7 1.6 %collective-permute-done.3.refs_5_ = bf16[4,128,384]{2,1,0:T(8,128)(2,1)S(1)} collective-permute-done((bf16[4,128,384]{2,1,0:T(8,128)(2,1)S(1)}, bf16[4,128,384]{2,1,0:T(8,128)(2,1)S(1)}, u32[]{:S(2)}, u32[]{:S(2)}) %collective-permute-start.3) | collective-permute-done | bytes 393248 | tf_op jit(solution)/shard_map/ppermute | solution.py:595
  24.3 2.5 %collective-permute-start.8 = (bf16[16,128,384]{2,1,0:T(8,128)(2,1)S(1)}, bf16[16,128,384]{2,1,0:T(8,128)(2,1)}, u32[]{:S(2)}, u32[]{:S(2)}) collective-permute-start(bf16[16,128,384]{2,1,0:T(8,128)(2,1)S(1)} %get-tuple-element.55), channel_id=1, source_target_pairs={{4,8},{8,4},{5,9},{9,5},{6,10},{10,6},{7,11},{11,7},{20,24},{24,20... | collective-permute-start | bytes 4718600 | tf_op jit(solution)/shard_map/ppermute | solution.py:595
  26.8 16.2 %attend_edges.1 = (f32[2,6,512,128]{3,2,1,0:T(8,128)S(1)}, f32[2,512,128]{2,1,0:T(8,128)S(1)}) custom-call(s32[2]{0:T(128)S(1)} %pad_add_fusion.place_ref, s32[216]{0:T(256)S(1)} %tile_tables.1.table_ref, bf16[4,512,768]{2,1,0:T(8,128)(2,1)} %q_own.2, bf16[4,512,384]{2,1,0:T(8,128)(2,1)S(1)} %collective-permute-done.4.q_other, ...), custom_call_target="tpu_custom_call" | custom-call | flops 1610612736 | bytes 393216 | tf_op jit(solution)/shard_map/attend_edges/pallas_call | solution.py:469
  43.0 0.8 copy-done.12
  43.8 0.1 copy-done.13
  44.0 23.9 %attend_middle.1 = (bf16[4,512,768]{2,1,0:T(8,128)(2,1)}, bf16[2,512,384]{2,1,0:T(8,128)(2,1)S(1)}) custom-call(s32[2]{0:T(128)S(1)} %pad_add_fusion.place_ref, s32[216]{0:T(256)S(1)} %tile_tables.1.table_ref, bf16[4,512,768]{2,1,0:T(8,128)(2,1)S(1)} %copy-done.1, bf16[4,512,384]{2,1,0:T(8,128)(2,1)S(1)} %collective-permute-done.4.q_other, ...), custom_call_target="tpu_custom_call" | custom-call | flops 25769803776 | bytes 6291456 | tf_op jit(solution)/shard_map/attend_middle/pallas_call | solution.py:469
  68.0 1.7 %collective-permute-start.10 = (bf16[2,512,384]{2,1,0:T(8,128)(2,1)S(1)}, bf16[2,512,384]{2,1,0:T(8,128)(2,1)S(1)}, u32[]{:S(2)}, u32[]{:S(2)}) collective-permute-start(bf16[2,512,384]{2,1,0:T(8,128)(2,1)S(1)} %get-tuple-element.61), channel_id=1, source_target_pairs={{0,1},{1,0},{2,3},{3,2},{4,5},{5,4},{6,7},{7,6},{8,9},{9,8},{10,11... | collective-permute-start | bytes 2359304 | tf_op jit(solution)/shard_map/ppermute | solution.py:599
  69.7 14.4 %attend_late.1 = (bf16[4,512,768]{2,1,0:T(8,128)(2,1)}, bf16[2,512,384]{2,1,0:T(8,128)(2,1)S(1)}) custom-call(s32[2]{0:T(128)S(1)} %pad_add_fusion.place_ref, s32[216]{0:T(256)S(1)} %tile_tables.1.table_ref, bf16[4,512,768]{2,1,0:T(8,128)(2,1)S(1)} %copy-done.1, ...), custom_call_target="tpu_custom_call", output_to_operand_aliasing={{0}: (16, {})} | custom-call | flops 2818572288 | bytes 688128 | tf_op jit(solution)/shard_map/attend_late/pallas_call | solution.py:535
  84.0 1.1 %collective-permute-start.9 = (bf16[2,512,384]{2,1,0:T(8,128)(2,1)S(1)}, bf16[2,512,384]{2,1,0:T(8,128)(2,1)S(1)}, u32[]{:S(2)}, u32[]{:S(2)}) collective-permute-start(bf16[2,512,384]{2,1,0:T(8,128)(2,1)S(1)} %get-tuple-element.60), channel_id=1, source_target_pairs={{0,1},{1,0},{2,3},{3,2},{4,5},{5,4},{6,7},{7,6},{8,9},{9,8},{10,11... | collective-permute-start | bytes 2359304 | tf_op jit(solution)/shard_map/ppermute | solution.py:599
  85.2 1.5 %place_columns.2._ = bf16[4,512,768]{2,1,0:T(8,128)(2,1)} custom-call(s32[2]{0:T(128)S(1)} %pad_add_fusion.place_ref, bf16[2,512,384]{2,1,0:T(8,128)(2,1)S(1)} %collective-permute-done.10.block_ref, bf16[4,512,768]{2,1,0:T(8,128)(2,1)} %get-tuple-element.62._), custom_call_target="tpu_custom_call", output_to_operand_aliasing={{}: (2, {})} | custom-call | tf_op jit(solution)/shard_map/place_columns/pallas_call | solution.py:574
  86.7 0.4 collective-permute-done.9.block_ref
  87.1 1.5 %place_columns.3 = bf16[4,512,768]{2,1,0:T(8,128)(2,1)} custom-call(s32[2]{0:T(128)S(1)} %pad_add_fusion.place_ref, bf16[2,512,384]{2,1,0:T(8,128)(2,1)S(1)} %collective-permute-done.9.block_ref, bf16[4,512,768]{2,1,0:T(8,128)(2,1)} %place_columns.2._), custom_call_target="tpu_custom_call", output_to_operand_aliasing={{}: (2, {})} | custom-call | tf_op jit(solution)/shard_map/place_columns/pallas_call | solution.py:574
  (31 shorter events, 0.1 us)
Async XLA Ops:
  0.0 3.6 %copy-start.7 = (bf16[4,512,768]{2,1,0:T(8,128)(2,1)S(1)}, bf16[4,512,768]{2,1,0:T(8,128)(2,1)}, u32[]{:S(2)}) copy-start(bf16[4,512,768]{2,1,0:T(8,128)(2,1)} %param.9) | copy-start | bytes 9437188
  2.9 2.2 %copy-start.3 = (s32[16,2,4]{0,2,1:T(4,128)S(1)}, s32[16,2,4]{0,2,1:T(4,128)}, u32[]{:S(2)}) copy-start(s32[16,2,4]{0,2,1:T(4,128)} %param.10) | copy-start | bytes 1540
  2.9 2.2 %copy-start.4 = (s32[16,2,3]{0,1,2:T(2,128)S(1)}, s32[16,2,3]{0,1,2:T(2,128)}, u32[]{:S(2)}) copy-start(s32[16,2,3]{0,1,2:T(2,128)} %param.13) | copy-start | bytes 1156
  2.9 2.2 %copy-start.5 = (s32[16,2,2]{0,2,1:T(2,128)S(1)}, s32[16,2,2]{0,2,1:T(2,128)}, u32[]{:S(2)}) copy-start(s32[16,2,2]{0,2,1:T(2,128)} %param.11) | copy-start | bytes 772
  2.9 2.2 %copy-start.6 = (s32[16,2,1]{0,2,1:T(1,128)S(1)}, s32[16,2,1]{0,2,1:T(1,128)}, u32[]{:S(2)}) copy-start(s32[16,2,1]{0,2,1:T(1,128)} %param.12) | copy-start | bytes 388
  2.9 4.1 %collective-permute-start = (bf16[4,512,384]{2,1,0:T(8,128)(2,1)}, bf16[4,512,384]{2,1,0:T(8,128)(2,1)}, u32[]{:S(2)}, u32[]{:S(2)}) collective-permute-start(bf16[4,512,384]{2,1,0:T(8,128)(2,1)} %constant_dynamic-slice_fusion.2), channel_id=1, source_target_pairs={{0,1},{1,0},{2,3},{3,2},{4,5},{5,4},{6,7},{7,6},{8,9},{9,8},{10,11... | collective-permute-start | bytes 4718600 | tf_op jit(solution)/shard_map/ppermute | solution.py:599
  5.0 4.2 %collective-permute-start.1 = (bf16[4,512,384]{2,1,0:T(8,128)(2,1)}, bf16[4,512,384]{2,1,0:T(8,128)(2,1)S(1)}, u32[]{:S(2)}, u32[]{:S(2)}) collective-permute-start(bf16[4,512,384]{2,1,0:T(8,128)(2,1)} %constant_dynamic-slice_fusion.1), channel_id=1, source_target_pairs={{0,1},{1,0},{2,3},{3,2},{4,5},{5,4},{6,7},{7,6},{8,9},{9,8},{10,11... | collective-permute-start | bytes 4718600 | tf_op jit(solution)/shard_map/ppermute | solution.py:599
  7.0 2.2 %copy-start = (bf16[4,512,768]{2,1,0:T(8,128)(2,1)S(1)}, bf16[4,512,768]{2,1,0:T(8,128)(2,1)}, u32[]{:S(2)}) copy-start(bf16[4,512,768]{2,1,0:T(8,128)(2,1)} %q_own.2) | copy-start | bytes 9437188
  9.1 1.2 %copy-start.8 = (bf16[4,512,384]{2,1,0:T(8,128)(2,1)}, bf16[4,512,384]{2,1,0:T(8,128)(2,1)S(1)}, u32[]{:S(2)}) copy-start(bf16[4,512,384]{2,1,0:T(8,128)(2,1)S(1)} %collective-permute-done.1) | copy-start | bytes 4718596
  10.3 16.5 %collective-permute-start.4 = (bf16[4,512,384]{2,1,0:T(8,128)(2,1)S(1)}, bf16[4,512,384]{2,1,0:T(8,128)(2,1)S(1)}, u32[]{:S(2)}, u32[]{:S(2)}) collective-permute-start(bf16[4,512,384]{2,1,0:T(8,128)(2,1)S(1)} %constant_dynamic-slice_fusion), channel_id=1, source_target_pairs={{0,1},{1,0},{2,3},{3,2},{4,5},{5,4},{6,7},{7,6},{8,9},{9,8},{10,11... | collective-permute-start | bytes 4718600 | tf_op jit(solution)/shard_map/ppermute | solution.py:599
  10.8 11.4 %collective-permute-start.2 = (bf16[4,128,384]{2,1,0:T(8,128)(2,1)S(1)}, bf16[4,128,384]{2,1,0:T(8,128)(2,1)S(1)}, u32[]{:S(2)}, u32[]{:S(2)}) collective-permute-start(bf16[4,128,384]{2,1,0:T(8,128)(2,1)S(1)} %get-tuple-element.36), channel_id=1, source_target_pairs={{0,4},{4,0},{8,12},{12,8},{1,5},{5,1},{9,13},{13,9},{2,6},{6,2},{1... | collective-permute-start | bytes 1179656 | tf_op jit(solution)/shard_map/ppermute | solution.py:595
  12.1 12.2 %collective-permute-start.3 = (bf16[4,128,384]{2,1,0:T(8,128)(2,1)S(1)}, bf16[4,128,384]{2,1,0:T(8,128)(2,1)S(1)}, u32[]{:S(2)}, u32[]{:S(2)}) collective-permute-start(bf16[4,128,384]{2,1,0:T(8,128)(2,1)S(1)} %get-tuple-element.37), channel_id=1, source_target_pairs={{4,8},{8,4},{5,9},{9,5},{6,10},{10,6},{7,11},{11,7},{20,24},{24,20... | collective-permute-start | bytes 1179656 | tf_op jit(solution)/shard_map/ppermute | solution.py:595
  15.9 27.1 %collective-permute-start.5 = (bf16[4,128,384]{2,1,0:T(8,128)(2,1)S(1)}, bf16[4,128,384]{2,1,0:T(8,128)(2,1)S(1)}, u32[]{:S(2)}, u32[]{:S(2)}) collective-permute-start(bf16[4,128,384]{2,1,0:T(8,128)(2,1)S(1)} %get-tuple-element.46), channel_id=1, source_target_pairs={{0,4},{4,0},{8,12},{12,8},{1,5},{5,1},{9,13},{13,9},{2,6},{6,2},{1... | collective-permute-start | bytes 1179656 | tf_op jit(solution)/shard_map/ppermute | solution.py:595
  15.9 27.1 %collective-permute-start.6 = (bf16[4,128,384]{2,1,0:T(8,128)(2,1)S(1)}, bf16[4,128,384]{2,1,0:T(8,128)(2,1)S(1)}, u32[]{:S(2)}, u32[]{:S(2)}) collective-permute-start(bf16[4,128,384]{2,1,0:T(8,128)(2,1)S(1)} %get-tuple-element.47), channel_id=1, source_target_pairs={{4,8},{8,4},{5,9},{9,5},{6,10},{10,6},{7,11},{11,7},{20,24},{24,20... | collective-permute-start | bytes 1179656 | tf_op jit(solution)/shard_map/ppermute | solution.py:595
  22.2 20.8 %copy-start.10 = (bf16[4,128,384]{2,1,0:T(8,128)(2,1)}, bf16[4,128,384]{2,1,0:T(8,128)(2,1)S(1)}, u32[]{:S(2)}) copy-start(bf16[4,128,384]{2,1,0:T(8,128)(2,1)S(1)} %collective-permute-done.2.refs_4_) | copy-start | bytes 1179652
  22.2 45.7 %collective-permute-start.7 = (bf16[16,128,384]{2,1,0:T(8,128)(2,1)S(1)}, bf16[16,128,384]{2,1,0:T(8,128)(2,1)S(1)}, u32[]{:S(2)}, u32[]{:S(2)}) collective-permute-start(bf16[16,128,384]{2,1,0:T(8,128)(2,1)S(1)} %get-tuple-element.54), channel_id=1, source_target_pairs={{0,4},{4,0},{8,12},{12,8},{1,5},{5,1},{9,13},{13,9},{2,6},{6,2},{1... | collective-permute-start | bytes 4718600 | tf_op jit(solution)/shard_map/ppermute | solution.py:595
  24.3 18.7 %copy-start.11 = (bf16[4,128,384]{2,1,0:T(8,128)(2,1)}, bf16[4,128,384]{2,1,0:T(8,128)(2,1)S(1)}, u32[]{:S(2)}) copy-start(bf16[4,128,384]{2,1,0:T(8,128)(2,1)S(1)} %collective-permute-done.3.refs_5_) | copy-start | bytes 1179652
  24.3 19.7 %copy-start.1 = (bf16[4,512,768]{2,1,0:T(8,128)(2,1)S(1)}, bf16[4,512,768]{2,1,0:T(8,128)(2,1)}, u32[]{:S(2)}) copy-start(bf16[4,512,768]{2,1,0:T(8,128)(2,1)} %q_own.2) | copy-start | bytes 9437188
  24.3 43.7 %collective-permute-start.8 = (bf16[16,128,384]{2,1,0:T(8,128)(2,1)S(1)}, bf16[16,128,384]{2,1,0:T(8,128)(2,1)}, u32[]{:S(2)}, u32[]{:S(2)}) collective-permute-start(bf16[16,128,384]{2,1,0:T(8,128)(2,1)S(1)} %get-tuple-element.55), channel_id=1, source_target_pairs={{4,8},{8,4},{5,9},{9,5},{6,10},{10,6},{7,11},{11,7},{20,24},{24,20... | collective-permute-start | bytes 4718600 | tf_op jit(solution)/shard_map/ppermute | solution.py:595
  43.0 24.9 %copy-start.2 = (f32[2,6,512,128]{3,2,1,0:T(8,128)}, f32[2,6,512,128]{3,2,1,0:T(8,128)S(1)}, u32[]{:S(2)}) copy-start(f32[2,6,512,128]{3,2,1,0:T(8,128)S(1)} %get-tuple-element.45.acc_ref) | copy-start | bytes 9437188
  43.0 0.8 copy-start.12
  43.0 0.9 %copy-start.13 = (bf16[4,128,384]{2,1,0:T(8,128)(2,1)}, bf16[4,128,384]{2,1,0:T(8,128)(2,1)S(1)}, u32[]{:S(2)}) copy-start(bf16[4,128,384]{2,1,0:T(8,128)(2,1)S(1)} %collective-permute-done.6.refs_7_) | copy-start | bytes 1179652
  67.9 1.7 %copy-start.9 = (bf16[16,128,384]{2,1,0:T(8,128)(2,1)}, bf16[16,128,384]{2,1,0:T(8,128)(2,1)S(1)}, u32[]{:S(2)}) copy-start(bf16[16,128,384]{2,1,0:T(8,128)(2,1)S(1)} %collective-permute-done.7.refs_8_) | copy-start | bytes 4718596
  68.0 17.2 %collective-permute-start.10 = (bf16[2,512,384]{2,1,0:T(8,128)(2,1)S(1)}, bf16[2,512,384]{2,1,0:T(8,128)(2,1)S(1)}, u32[]{:S(2)}, u32[]{:S(2)}) collective-permute-start(bf16[2,512,384]{2,1,0:T(8,128)(2,1)S(1)} %get-tuple-element.61), channel_id=1, source_target_pairs={{0,1},{1,0},{2,3},{3,2},{4,5},{5,4},{6,7},{7,6},{8,9},{9,8},{10,11... | collective-permute-start | bytes 2359304 | tf_op jit(solution)/shard_map/ppermute | solution.py:599
  84.0 3.0 %collective-permute-start.9 = (bf16[2,512,384]{2,1,0:T(8,128)(2,1)S(1)}, bf16[2,512,384]{2,1,0:T(8,128)(2,1)S(1)}, u32[]{:S(2)}, u32[]{:S(2)}) collective-permute-start(bf16[2,512,384]{2,1,0:T(8,128)(2,1)S(1)} %get-tuple-element.60), channel_id=1, source_target_pairs={{0,1},{1,0},{2,3},{3,2},{4,5},{5,4},{6,7},{7,6},{8,9},{9,8},{10,11... | collective-permute-start | bytes 2359304 | tf_op jit(solution)/shard_map/ppermute | solution.py:599
